TPU v7x, 256 devices: a whole 4x4x8 slice. The times are simulated.
256 devices in a mesh: seq: 64 (over x, y, z_hi), head: 4 (over z_lo, core).
Axes of the slice: x: 4, y: 4, z: 8 (z_hi: 4, z_lo: 2; z = z_hi * 2 + z_lo), core: 2. Of those that a mesh axis runs over, the one named last changes fastest.
Arguments:
- trunk_keys: bfloat16 [4, 32768, 512], P('head', 'seq'), may hold values from -6 to 6
- trunk_values: bfloat16 [4, 32768, 512], P('head', 'seq'), may hold values from -6 to 6
- trunk_rates: float32 [4, 32768], P('head', 'seq'), may hold values from 0.001 to 0.01
- segment_end: int32 [1], replicated, may hold values from 8192 to 24576
- fast_weights: bfloat16 [3, 4, 512, 512], P(None, 'head'), may hold values from -0.25 to 0.25
- step_sizes: float32 [4], P('head'), may hold values from 0.3 to 1
- branch_query: bfloat16 [4, 32768, 512], P('head', 'seq'), may hold values from -24 to 24
- branch_keys: bfloat16 [4, 32768, 512], P('head', 'seq'), may hold values from -24 to 24
- branch_values: bfloat16 [4, 32768, 512], P('head', 'seq'), may hold values from -6 to 6
- branch_lengths: int32 [16], replicated, may hold values from 1537 to 2048, as said below
- fork_points: int32 [16], replicated, may hold values from 0 to 32768
- out_gain: float32 [4, 512], P('head'), may hold values from 0.1 to 1.9
Outputs:
- branch_out: bfloat16 [4, 32768, 512], P('head', 'seq')
- fast_after: bfloat16 [3, 4, 512, 512], P(None, 'head')
Inputs may be any that keep to these rules, and one draw needn't show every extreme that they name: `branch_lengths`: only the last 512 slots of a branch can be empty; some branch has all its slots live.
All inputs are finite; a program needn't handle non-finite values.
Results may differ from a plain program's by a relative error of at most 0.02.
Values may be sent and summed in bfloat16 or wider, within the bound.
No kernel may reach another device: no remote copies, remote signals or barrier semaphores. Data moves between devices by JAX's collectives and lax.ppermute only.
A program may use at most 64 MiB of HBM per device.

v0:
```python
import jax
import jax.numpy as jnp
from jax import lax
from jax.sharding import PartitionSpec as P

NS_STEPS = 2
WIN = 512
BR_SPAN = 4


poly_one = 3.4445
poly_two = -4.775
poly_three = 2.0315


def from_behind(value, axis, steps):
    count = lax.axis_size(axis)
    first, last = (max(0, -steps), min(count, count - steps))
    return lax.ppermute(value, axis, [(source, source + steps) for source in range(first, last)])


def segment_gradient(fast_state, key_rows, value_rows, rate_row):
    proj_first = jnp.dot(key_rows, fast_state[0].T, preferred_element_type=jnp.float32)
    proj_third = jnp.dot(key_rows, fast_state[1].T, preferred_element_type=jnp.float32)
    sigmoid_first = jax.nn.sigmoid(proj_first)
    silu_first = proj_first * sigmoid_first
    hidden = (silu_first * proj_third).astype(jnp.bfloat16)
    pushed = (rate_row[:, None] * value_rows.astype(jnp.float32)).astype(jnp.bfloat16)
    returned = jnp.dot(pushed, fast_state[2].T, preferred_element_type=jnp.float32)
    delta_first = (
        returned * proj_third * sigmoid_first * (1.0 + proj_first * (1.0 - sigmoid_first))
    ).astype(jnp.bfloat16)
    delta_third = (returned * silu_first).astype(jnp.bfloat16)
    contract = (((0,), (0,)), ((), ()))
    grad_first = lax.dot_general(
        delta_first, key_rows, contract, preferred_element_type=jnp.float32
    )
    grad_third = lax.dot_general(
        delta_third, key_rows, contract, preferred_element_type=jnp.float32
    )
    grad_second = lax.dot_general(hidden, pushed, contract, preferred_element_type=jnp.float32)
    return jnp.stack([grad_first, grad_third, grad_second])


def normalize_sum(summed):
    frobenius = jnp.sqrt(jnp.sum(summed * summed, axis=(-2, -1), keepdims=True))
    return (summed / (frobenius + 1e-07)).astype(jnp.bfloat16)


def iterate_polynomial(current):
    for sweep_index in range(NS_STEPS):
        gram_matrix = jnp.einsum(
            "...ij,...kj->...ik", current, current, preferred_element_type=jnp.float32
        ).astype(jnp.bfloat16)
        square = jnp.einsum(
            "...ij,...jk->...ik", gram_matrix, gram_matrix, preferred_element_type=jnp.float32
        )
        polynomial = (poly_two * gram_matrix.astype(jnp.float32) + poly_three * square).astype(
            jnp.bfloat16
        )
        update_term = jnp.einsum(
            "...ij,...jk->...ik", polynomial, current, preferred_element_type=jnp.float32
        )
        current = (poly_one * current.astype(jnp.float32) + update_term).astype(jnp.bfloat16)
    return current


def refresh(weights, direction, step_sizes):
    old_rows = weights.astype(jnp.float32)
    moved_rows = old_rows + step_sizes[:, None, None, None] * direction.astype(jnp.float32)
    old_scale = jnp.sqrt(jnp.mean(old_rows * old_rows, axis=-1, keepdims=True) + 1e-06)
    new_scale = jnp.sqrt(jnp.mean(moved_rows * moved_rows, axis=-1, keepdims=True) + 1e-06)
    return (moved_rows * (old_scale / new_scale)).astype(jnp.bfloat16)


def per_device(
    trunk_keys,
    trunk_values,
    trunk_rates,
    segment_end,
    fast_weights,
    step_sizes,
    branch_query,
    branch_keys,
    branch_values,
    branch_lengths,
    fork_points,
    out_gain,
):
    seq_count = lax.axis_size("seq")
    seq_index = lax.axis_index("seq")
    row_count = trunk_keys.shape[1]
    split_point = segment_end[0]
    positions = seq_index * row_count + jnp.arange(row_count, dtype=jnp.int32)
    weights = jnp.moveaxis(fast_weights, 1, 0)
    states = [weights]
    for period in range(2):
        inside = positions < split_point if period == 0 else positions >= split_point
        masked = trunk_rates * inside.astype(jnp.float32)[None, :]
        partial_sums = jax.vmap(segment_gradient)(weights, trunk_keys, trunk_values, masked)
        pieces = lax.psum_scatter(partial_sums, "seq", scatter_dimension=2, tiled=True)
        gathered = lax.all_gather(pieces.astype(jnp.bfloat16), "seq", axis=2, tiled=True).astype(
            pieces.dtype
        )
        start_state = normalize_sum(gathered)
        direction = iterate_polynomial(start_state)
        weights = refresh(weights, direction, step_sizes)
        states.append(weights)
    head_count, branch_rows, feature_width = branch_query.shape
    prior_keys, prior_values = from_behind((branch_keys, branch_values), "seq", 1)
    all_keys = jnp.concatenate([prior_keys, branch_keys], axis=1)
    all_values = jnp.concatenate([prior_values, branch_values], axis=1)
    branch_id = seq_index // BR_SPAN
    span_pos = seq_index % BR_SPAN
    length_here = jnp.clip(
        jnp.take(branch_lengths, branch_id) - span_pos * branch_rows, 0, branch_rows
    )
    slot_index = jnp.arange(WIN + branch_rows, dtype=jnp.int32)
    live_slots = jnp.where(slot_index < WIN, span_pos > 0, slot_index - WIN < length_here)
    scale = feature_width ** (-0.5)

    def attend_block(block_index):
        start_row = block_index * WIN
        row_index = start_row + jnp.arange(WIN, dtype=jnp.int32)[:, None]
        slot_block = start_row + jnp.arange(2 * WIN, dtype=jnp.int32)[None, :]
        allowed = (slot_block == row_index + WIN) | live_slots[None, :] & (
            slot_block > row_index
        ) & (slot_block <= row_index + WIN)
        scores = (
            jnp.einsum("hrd,hkd->hrk", branch_query, all_keys, preferred_element_type=jnp.float32)
            * scale
        )
        scores = jnp.where(allowed[None], scores, -jnp.inf)
        row_max = jnp.max(scores, axis=-1, keepdims=True)
        exponent = jnp.exp(scores - row_max)
        attention_weights = (exponent / jnp.sum(exponent, axis=-1, keepdims=True)).astype(
            jnp.bfloat16
        )
        return jnp.einsum(
            "hrk,hkd->hrd", attention_weights, all_values, preferred_element_type=jnp.float32
        )

    block_count = branch_rows // WIN
    attended = lax.map(attend_block, jnp.arange(block_count, dtype=jnp.int32))
    attended = jnp.moveaxis(attended, 0, 1).reshape(head_count, branch_rows, feature_width)
    trunk_total = row_count * seq_count
    fork_here = jnp.take(fork_points, branch_id)
    chosen = jnp.where(fork_here < split_point, 0, jnp.where(fork_here < trunk_total, 1, 2))
    fast_set = jnp.take(jnp.stack(states), chosen, axis=0)
    proj_first = jnp.einsum(
        "hrd,hfd->hrf", branch_query, fast_set[:, 0], preferred_element_type=jnp.float32
    )
    proj_third = jnp.einsum(
        "hrd,hfd->hrf", branch_query, fast_set[:, 1], preferred_element_type=jnp.float32
    )
    hidden = (jax.nn.silu(proj_first) * proj_third).astype(jnp.bfloat16)
    applied = jnp.einsum("hrf,hfd->hrd", hidden, fast_set[:, 2], preferred_element_type=jnp.float32)
    summed = attended + applied
    energy = lax.psum(jnp.sum(summed * summed, axis=(0, 2)), "head")
    total_width = head_count * lax.axis_size("head") * feature_width
    normed = summed * lax.rsqrt(energy / total_width + 1e-06)[None, :, None] * out_gain[:, None, :]
    row_index = jnp.arange(branch_rows, dtype=jnp.int32)
    result = jnp.where((row_index < length_here)[None, :, None], normed, 0.0).astype(jnp.bfloat16)
    return (result, jnp.moveaxis(weights, 0, 1))


def solution(mesh):
    placed = (
        P("head", "seq", None),
        P("head", "seq", None),
        P("head", "seq"),
        P(),
        P(None, "head", None, None),
        P("head"),
        P("head", "seq", None),
        P("head", "seq", None),
        P("head", "seq", None),
        P(),
        P(),
        P("head", None),
    )
    return jax.shard_map(
        per_device,
        mesh=mesh,
        in_specs=placed,
        out_specs=(P("head", "seq", None), P(None, "head", None, None)),
        check_vma=False,
    )
```

profile of v0, /device:TPU:1, one launch (start us, length us, event | category | flops | bytes accessed | tf_op | source)
XLA Modules:
  0.0 1033.1 jit_solution(1651604838990128928)
XLA Ops:
  8.2 2.6 fusion.47
  10.8 1.4 fusion.48
  16.3 2.0 maximum_bitcast_fusion
  18.4 342.6 %reduce-scatter.3.cloned.1.call-done = f32[1,3,8,512]{3,2,1,0:T(8,128)} async-done(((f32[1,3,512,512]{3,2,1,0:T(8,128)}), f32[1,3,8,512]{3,2,1,0:T(8,128)}) %reduce-scatter.3.cloned.1.call-update) | async-done | bytes 49168 | tf_op jit(solution)/shard_map/reduce_scatter | solution.py:101
  360.9 1.4 convert_element_type.180
  363.3 121.6 %all-gather.3.cloned.1.call-done = bf16[1,3,512,512]{3,2,1,0:T(8,128)(2,1)} async-done(((bf16[1,3,8,512]{3,2,1,0:T(8,128)(2,1)}), bf16[1,3,512,512]{3,2,1,0:T(8,128)(2,1)}) %all-gather.3.cloned.1.call-update) | async-done | bytes 1572880 | tf_op jit(solution)/shard_map/all_gather | solution.py:102
  484.9 1.9 fusion.1
  486.8 4.2 convolution_convert_fusion.3
  490.9 6.5 fusion.9
  497.4 4.1 convolution_convert_fusion.2
  501.5 6.9 fusion
  508.4 2.5 multiply_convert_fusion.1
  514.2 2.0 maximum_bitcast_fusion.1
  516.3 336.1 %reduce-scatter.5.cloned.1.call-done = f32[1,3,8,512]{3,2,1,0:T(8,128)} async-done(((f32[1,3,512,512]{3,2,1,0:T(8,128)}), f32[1,3,8,512]{3,2,1,0:T(8,128)}) %reduce-scatter.5.cloned.1.call-update) | async-done | bytes 49168 | tf_op jit(solution)/shard_map/reduce_scatter | solution.py:101
  852.4 1.4 convert_element_type.200
  853.8 2.1 collective-permute-start
  856.0 2.1 collective-permute-start.1
  860.6 9.4 collective-permute-done
  870.0 2.2 fusion.95
  872.2 1.3 copy-done.5
  873.9 109.7 %all-gather.5.cloned.1.call-done = bf16[1,3,512,512]{3,2,1,0:T(8,128)(2,1)} async-done(((bf16[1,3,8,512]{3,2,1,0:T(8,128)(2,1)}), bf16[1,3,512,512]{3,2,1,0:T(8,128)(2,1)}) %all-gather.5.cloned.1.call-update) | async-done | bytes 1572880 | tf_op jit(solution)/shard_map/all_gather | solution.py:102
  983.5 1.9 fusion.4
  985.5 4.2 convolution_convert_fusion.1
  989.6 6.5 fusion.7
  996.1 4.1 convolution_convert_fusion
  1000.2 7.0 fusion.3
  1007.3 3.2 fusion.63
  1011.5 1.1 copy-done.3
  1013.1 3.2 fusion.28
  1016.3 2.8 multiply_reduce_fusion.2
  1019.1 6.3 psum.7
  1025.6 1.0 copy.25
  (62 shorter events, 11.3 us)
Async XLA Ops:
  7.2 1.0 copy-start
  7.2 3.6 copy-start.1
  7.2 353.8 %reduce-scatter.3.cloned.1.call-start = ((), (), s32[]{:S(2)}) async-start(), calls=%async_computation.2 | async-start | bytes 3194880 | tf_op jit(solution)/shard_map/reduce_scatter | solution.py:101
  8.2 4.7 copy-start.10
  8.2 4.7 copy-start.4
  12.9 1.2 copy-start.6
  12.9 1.5 copy-start.7
  18.3 466.6 %all-gather.3.cloned.1.call-start = ((), (), s32[]{:S(2)}) async-start(), calls=%async_computation.3 | async-start | bytes 1597440 | tf_op jit(solution)/shard_map/all_gather | solution.py:102
  362.4 490.0 %reduce-scatter.5.cloned.1.call-start = ((), (), s32[]{:S(2)}) async-start(), calls=%async_computation.4 | async-start | bytes 3194880 | tf_op jit(solution)/shard_map/reduce_scatter | solution.py:101
  516.2 337.6 %copy-start.11 = (bf16[1,512,512]{2,1,0:T(8,128)(2,1)S(1)}, bf16[1,512,512]{2,1,0:T(8,128)(2,1)}, u32[]{:S(2)}) copy-start(bf16[1,512,512]{2,1,0:T(8,128)(2,1)} %param.19) | copy-start | bytes 1572868
  516.2 341.9 %copy-start.13 = (s32[16]{0:T(128)S(1)}, s32[16]{0:T(128)}, u32[]{:S(2)}) copy-start(s32[16]{0:T(128)} %param.22) | copy-start | bytes 196
  516.2 343.1 %copy-start.14 = (s32[16]{0:T(128)S(1)}, s32[16]{0:T(128)}, u32[]{:S(2)}) copy-start(s32[16]{0:T(128)} %param.21) | copy-start | bytes 196
  516.2 353.8 %copy-start.8 = (bf16[1,512,512]{2,1,0:T(8,128)(2,1)S(1)}, bf16[1,512,512]{2,1,0:T(8,128)(2,1)}, u32[]{:S(2)}) copy-start(bf16[1,512,512]{2,1,0:T(8,128)(2,1)} %param.18) | copy-start | bytes 1572868
  516.2 467.3 %all-gather.5.cloned.1.call-start = ((), (), s32[]{:S(2)}) async-start(), calls=%async_computation.5 | async-start | bytes 1597440 | tf_op jit(solution)/shard_map/all_gather | solution.py:102
  853.8 16.1 %collective-permute-start = (bf16[1,512,512]{2,1,0:T(8,128)(2,1)S(1)}, bf16[1,512,512]{2,1,0:T(8,128)(2,1)}, u32[]{:S(2)}, u32[]{:S(2)}) collective-permute-start(bf16[1,512,512]{2,1,0:T(8,128)(2,1)S(1)} %copy-done.11), channel_id=1, source_target_pairs={{0,4},{4,8},{8,12},{12,16},{16,20},{20,24},{24,28},{28,32},{32,36}... | collective-permute-start | bytes 1572872 | tf_op jit(solution)/shard_map/ppermute | solution.py:19
  856.0 160.3 %collective-permute-start.1 = (bf16[1,512,512]{2,1,0:T(8,128)(2,1)}, bf16[1,512,512]{2,1,0:T(8,128)(2,1)}, u32[]{:S(2)}, u32[]{:S(2)}) collective-permute-start(bf16[1,512,512]{2,1,0:T(8,128)(2,1)} %param.20), channel_id=1, source_target_pairs={{0,4},{4,8},{8,12},{12,16},{16,20},{20,24},{24,28},{28,32},{32,36}... | collective-permute-start | bytes 1572872 | tf_op jit(solution)/shard_map/ppermute | solution.py:19
  872.2 1.4 copy-start.5
  1007.3 3.3 copy-start.2
  1011.5 1.2 copy-start.3
  1013.1 3.2 copy-start.12
  1016.3 9.2 copy-start.9
Sparse Core Ops, SparseCore 0:
  18.4 342.4 reduce-scatter.2
  365.1 119.6 all-gather.2
  516.3 336.0 reduce-scatter.4
  856.0 127.5 all-gather.4
where the time goes:
time: 1030 us
  waiting for transfers between devices  919 us (89%)
  matrix products  61.7 us (6%)
  other arithmetic  17.8 us (2%)
  between operations  16.5 us (2%)
    reduce_scatter x2, waiting for transfers between devices, per_device(): lax.psum_scatter(partial_sums, 'seq', scatter_dimension=2, tiled=True)  679 us
    all_gather x2, waiting for transfers between devices, per_device(): lax.all_gather(pieces.astype(jnp.bfloat16), 'seq', axis=2, tiled=True)  231 us
    dot_general x4, matrix products, iterate_polynomial(): jnp.einsum('...ij,...jk->...ik', polynomial, current, preferred_element_t...  26.9 us
  transfers between devices with their start and end apart: 6, of which 5 were waited for; matrix products, arithmetic and copies ran while one was open for 3% of the time, Pallas kernels for 0%

commit v1 on v0

--- a/solution.py
+++ b/solution.py
@@ -1,6 +1,7 @@
 import jax
 import jax.numpy as jnp
 from jax import lax
+from jax.sharding import Mesh
 from jax.sharding import PartitionSpec as P
 
 NS_STEPS = 2
@@ -13,10 +14,31 @@
 poly_three = 2.0315
 
 
-def from_behind(value, axis, steps):
-    count = lax.axis_size(axis)
-    first, last = (max(0, -steps), min(count, count - steps))
-    return lax.ppermute(value, axis, [(source, source + steps) for source in range(first, last)])
+PLANE = ("x", "y")
+SEQ = ("x", "y", "z")
+HEAD = ("w", "c")
+
+
+def from_behind(value):
+    count = lax.axis_size("z")
+    return lax.ppermute(value, "z", [(source, source + 1) for source in range(count - 1)])
+
+
+def sum_everywhere(partial_sums):
+    kinds, rows, columns = partial_sums.shape
+    planes = lax.axis_size(PLANE)
+    depth = lax.axis_size("z")
+    parts = partial_sums.astype(jnp.bfloat16).reshape(kinds, planes, rows // planes, columns)
+    received = lax.all_to_all(parts.swapaxes(0, 1), PLANE, 0, 0, tiled=False)
+    mine = jnp.sum(received.astype(jnp.float32), axis=0).astype(jnp.bfloat16)
+    total = mine.astype(jnp.float32)
+    for step in range(1, depth):
+        other = lax.ppermute(mine, "z", [(i, (i + step) % depth) for i in range(depth)])
+        total = total + other.astype(jnp.float32)
+    total = total.astype(jnp.bfloat16)
+    return lax.all_to_all(
+        jnp.broadcast_to(total[None], (planes, *total.shape)), PLANE, 0, 0, tiled=False
+    )
 
 
 def segment_gradient(fast_state, key_rows, value_rows, rate_row):
@@ -87,8 +109,9 @@
     fork_points,
     out_gain,
 ):
-    seq_count = lax.axis_size("seq")
-    seq_index = lax.axis_index("seq")
+    prior_keys, prior_values = from_behind((branch_keys, branch_values))
+    seq_count = lax.axis_size(SEQ)
+    seq_index = lax.axis_index(SEQ)
     row_count = trunk_keys.shape[1]
     split_point = segment_end[0]
     positions = seq_index * row_count + jnp.arange(row_count, dtype=jnp.int32)
@@ -98,16 +121,13 @@
         inside = positions < split_point if period == 0 else positions >= split_point
         masked = trunk_rates * inside.astype(jnp.float32)[None, :]
         partial_sums = jax.vmap(segment_gradient)(weights, trunk_keys, trunk_values, masked)
-        pieces = lax.psum_scatter(partial_sums, "seq", scatter_dimension=2, tiled=True)
-        gathered = lax.all_gather(pieces.astype(jnp.bfloat16), "seq", axis=2, tiled=True).astype(
-            pieces.dtype
-        )
+        gathered = sum_everywhere(partial_sums[0])
+        gathered = gathered.swapaxes(0, 1).reshape(partial_sums.shape).astype(jnp.float32)
         start_state = normalize_sum(gathered)
         direction = iterate_polynomial(start_state)
         weights = refresh(weights, direction, step_sizes)
         states.append(weights)
     head_count, branch_rows, feature_width = branch_query.shape
-    prior_keys, prior_values = from_behind((branch_keys, branch_values), "seq", 1)
     all_keys = jnp.concatenate([prior_keys, branch_keys], axis=1)
     all_values = jnp.concatenate([prior_values, branch_values], axis=1)
     branch_id = seq_index // BR_SPAN
@@ -156,8 +176,8 @@
     hidden = (jax.nn.silu(proj_first) * proj_third).astype(jnp.bfloat16)
     applied = jnp.einsum("hrf,hfd->hrd", hidden, fast_set[:, 2], preferred_element_type=jnp.float32)
     summed = attended + applied
-    energy = lax.psum(jnp.sum(summed * summed, axis=(0, 2)), "head")
-    total_width = head_count * lax.axis_size("head") * feature_width
+    energy = lax.psum(jnp.sum(summed * summed, axis=(0, 2)), HEAD)
+    total_width = head_count * lax.axis_size(HEAD) * feature_width
     normed = summed * lax.rsqrt(energy / total_width + 1e-06)[None, :, None] * out_gain[:, None, :]
     row_index = jnp.arange(branch_rows, dtype=jnp.int32)
     result = jnp.where((row_index < length_here)[None, :, None], normed, 0.0).astype(jnp.bfloat16)
@@ -165,24 +185,26 @@
 
 
 def solution(mesh):
+    fine = Mesh(mesh.devices.reshape(4, 4, 4, 2, 2), (*SEQ, *HEAD))
+    rows = P(HEAD, SEQ, None)
     placed = (
-        P("head", "seq", None),
-        P("head", "seq", None),
-        P("head", "seq"),
+        rows,
+        rows,
+        P(HEAD, SEQ),
         P(),
-        P(None, "head", None, None),
-        P("head"),
-        P("head", "seq", None),
-        P("head", "seq", None),
-        P("head", "seq", None),
+        P(None, HEAD, None, None),
+        P(HEAD),
+        rows,
+        rows,
+        rows,
         P(),
         P(),
-        P("head", None),
+        P(HEAD, None),
     )
     return jax.shard_map(
         per_device,
-        mesh=mesh,
+        mesh=fine,
         in_specs=placed,
-        out_specs=(P("head", "seq", None), P(None, "head", None, None)),
+        out_specs=(rows, P(None, HEAD, None, None)),
         check_vma=False,
     )

time: 1030 us -> 251 us (0.24)
  waiting for transfers between devices: 919 us -> 22.1 us
  blocking collectives: 6.33 us -> 86 us
  starting transfers between devices: 4.55 us -> 36.6 us
  local copies, waits for them, and re-layouts: 6.73 us -> 20.3 us
  between operations: 16.5 us -> 3.59 us
    reduce_scatter x2 -> x0, waiting for transfers between devices: 679 us -> none  [per_device(): lax.psum_scatter(partial_sums, 'seq', scatter_dimension=2, tiled=True)]
    all_gather x2 -> x0, waiting for transfers between devices: 231 us -> none  [per_device(): lax.all_gather(pieces.astype(jnp.bfloat16), 'seq', axis=2, tiled=True)]
    all_to_all x0 -> x2, blocking collectives: none -> 53.4 us  [sum_everywhere(): received = lax.all_to_all(parts.swapaxes(0, 1), PLANE, 0, 0, tiled=False)]
    psum x1, blocking collectives: 6.33 us -> 32.6 us  [per_device(): energy = lax.psum(jnp.sum(summed * summed, axis=(0, 2)), HEAD)]
    ppermute x2 -> x8, starting transfers between devices: 4.21 us -> 26.9 us  [the longest x6 18.4 us: sum_everywhere(): lax.ppermute(mine, 'z', [(i, (i + step) % depth) for i in range(depth)])]
    all_to_all x0 -> x2, waiting for transfers between devices: none -> 14.9 us  [sum_everywhere(): lax.all_to_all(jnp.broadcast_to(total[None], (planes, *total.shape)), PLA...]
  transfers between devices with their start and end apart: 6 -> 10, of which waited for: 5 -> 6; matrix products, arithmetic and copies ran while one was open for 3% -> 19% of each run, Pallas kernels for 0% -> 0%
where the time goes in v1:
time: 251 us; the launch traced here: 250 us
  blocking collectives  86 us (34%)
  matrix products  56.4 us (22%)
  starting transfers between devices  36.6 us (15%)
  other arithmetic  25.4 us (10%)
  waiting for transfers between devices  22.1 us (9%)
  local copies, waits for them, and re-layouts  20.3 us (8%)
  between operations  3.59 us (1%)
    all_to_all x2, blocking collectives, sum_everywhere(): received = lax.all_to_all(parts.swapaxes(0, 1), PLANE, 0, 0, tiled=False)  53.4 us
    psum x1, blocking collectives, per_device(): energy = lax.psum(jnp.sum(summed * summed, axis=(0, 2)), HEAD)  32.6 us
    dot_general x4, matrix products, iterate_polynomial(): jnp.einsum('...ij,...jk->...ik', polynomial, current, preferred_element_t...  25.7 us
    ppermute x6, starting transfers between devices, sum_everywhere(): lax.ppermute(mine, 'z', [(i, (i + step) % depth) for i in range(depth)])  18.4 us
    all_to_all x2, waiting for transfers between devices, sum_everywhere(): lax.all_to_all(jnp.broadcast_to(total[None], (planes, *total.shape)), PLA...  14.9 us
    dot_general x4, matrix products, iterate_polynomial(): jnp.einsum('...ij,...kj->...ik', current, current, preferred_element_type...  12.7 us
    all_to_all x2, starting transfers between devices, sum_everywhere(): lax.all_to_all(jnp.broadcast_to(total[None], (planes, *total.shape)), PLA...  9.75 us
    unnamed x39, local copies, waits for them, and re-layouts  9.05 us
  transfers between devices with their start and end apart: 10, of which 6 were waited for; matrix products, arithmetic and copies ran while one was open for 19% of the time, Pallas kernels for 0%

profile of v1, /device:TPU:1, one launch (start us, length us, event | category | flops | bytes accessed | tf_op | source)
XLA Modules:
  0.0 250.4 jit_solution(16739285176354264000)
XLA Ops:
  6.5 28.9 %all_to_all.20 = bf16[16,3,32,512]{3,2,1,0:T(8,128)(2,1)S(1)} all-to-all(bf16[16,3,32,512]{3,2,1,0:T(8,128)(2,1)S(1)} %copy.44), channel_id=1, replica_groups=mesh['x'=4,'y'=4,'z'=4,'w'=2,'c'=2] {'x','y'}, dimensions={0} | all-to-all | bytes 3145728 | tf_op jit(solution)/shard_map/all_to_all | solution.py:32
  35.6 3.1 %collective-permute-start.2 = (bf16[3,32,512]{2,1,0:T(8,128)(2,1)S(1)}, bf16[3,32,512]{2,1,0:T(8,128)(2,1)S(1)}, u32[]{:S(2)}, u32[]{:S(2)}) collective-permute-start(bf16[3,32,512]{2,1,0:T(8,128)(2,1)S(1)} %reduce_sum.98), channel_id=1, source_target_pairs={{0,4},{4,8},{8,12},{12,0},{1,5},{5,9},{9,13},{13,1},{2,6},{6,10},{... | collective-permute-start | bytes 294920 | tf_op jit(solution)/shard_map/ppermute | solution.py:36
  38.7 5.1 %collective-permute-start.3 = (bf16[3,32,512]{2,1,0:T(8,128)(2,1)S(1)}, bf16[3,32,512]{2,1,0:T(8,128)(2,1)S(1)}, u32[]{:S(2)}, u32[]{:S(2)}) collective-permute-start(bf16[3,32,512]{2,1,0:T(8,128)(2,1)S(1)} %reduce_sum.98), channel_id=1, source_target_pairs={{0,8},{4,12},{8,0},{12,4},{1,9},{5,13},{9,1},{13,5},{2,10},{6,14},... | collective-permute-start | bytes 294920 | tf_op jit(solution)/shard_map/ppermute | solution.py:36
  43.8 2.4 collective-permute-start.4
  50.9 5.2 %all-to-all-start.1 = ((bf16[16,3,32,512]{3,2,1,0:T(8,128)(2,1)}), bf16[16,3,32,512]{3,2,1,0:T(8,128)(2,1)S(1)}, u32[]{:S(2)}, u32[]{:S(2)}) async-start(bf16[16,3,32,512]{3,2,1,0:T(8,128)(2,1)} %broadcast_in_dim.87), calls=%async_computation.1 | async-start | bytes 3145728 | tf_op jit(solution)/shard_map/all_to_all | solution.py:39
  56.1 2.6 %copy.42 = bf16[3,1,512,512]{2,3,0,1:T(8,128)(2,1)} copy(bf16[3,1,512,512]{3,2,1,0:T(8,128)(2,1)} %param.16) | data formatting | bytes 3145728 | tf_op args[4]
  61.1 14.0 %all-to-all-done.1 = bf16[16,3,32,512]{3,2,1,0:T(8,128)(2,1)S(1)} async-done(((bf16[16,3,32,512]{3,2,1,0:T(8,128)(2,1)}), bf16[16,3,32,512]{3,2,1,0:T(8,128)(2,1)S(1)}, u32[]{:S(2)}, u32[]{:S(2)}) %all-to-all-start.1) | async-done | bytes 1572896 | tf_op jit(solution)/shard_map/all_to_all | solution.py:39
  77.3 3.6 %copy.46 = f32[3,512,512]{1,2,0:T(8,128)} copy(f32[3,512,512]{2,1,0:T(8,128)} %bitcast.190) | data formatting | bytes 6291456 | tf_op jit(solution)/shard_map/convert_element_type | solution.py:125
  81.3 2.4 divide_convert_fusion.1
  83.7 2.2 convolution_convert_fusion.3
  85.9 5.6 %add_convert_fusion.6 = bf16[3,512,512]{1,2,0:T(8,128)(2,1)} fusion(bf16[3,512,512]{1,2,0:T(8,128)(2,1)S(1)} %divide_convert_fusion.1, bf16[3,512,512]{2,1,0:T(8,128)(2,1)} %convolution_convert_fusion.3), kind=kOutput, calls=%fused_computation.20 | convolution fusion | flops 1617690624 | bytes 4718592 | tf_op jit(solution)/shard_map/...ij,...jk->...ik/dot_general | solution.py:83
  91.4 4.2 %convolution_convert_fusion.2 = bf16[3,512,512]{2,1,0:T(8,128)(2,1)} fusion(bf16[3,512,512]{1,2,0:T(8,128)(2,1)} %add_convert_fusion.6), kind=kOutput, calls=%fused_computation.36 | convolution fusion | flops 806092800 | bytes 3145728 | tf_op jit(solution)/shard_map/...ij,...kj->...ik/dot_general | solution.py:74
  95.6 6.7 %multiply_reduce_fusion.2 = (f32[3,512]{1,0:T(4,128)S(1)}, bf16[3,512,512]{1,2,0:T(8,128)(2,1)}) fusion(bf16[3,1,512,512]{2,3,0,1:T(8,128)(2,1)S(1)} %copy-done.3, f32[]{:T(128)} %bitcast.181, bf16[3,512,512]{1,2,0:T(8,128)(2,1)} %add_convert_fusion.6, bf16[3,512,512]{2,1,0:T(8,128)(2,1)} %convolution_convert_fusion.2), kind=kOutput, calls=%fused_computation.16 | convolution fusion | flops 1622407680 | bytes 6297604 | tf_op jit(solution)/shard_map/...ij,...jk->...ik/dot_general | solution.py:83
  102.3 2.5 multiply_convert_fusion.1
  108.6 24.5 %all_to_all.21 = bf16[16,3,32,512]{3,2,1,0:T(8,128)(2,1)} all-to-all(bf16[16,3,32,512]{3,2,1,0:T(8,128)(2,1)S(1)} %copy.51), channel_id=1, replica_groups=mesh['x'=4,'y'=4,'z'=4,'w'=2,'c'=2] {'x','y'}, dimensions={0} | all-to-all | bytes 3145728 | tf_op jit(solution)/shard_map/all_to_all | solution.py:32
  134.8 2.4 collective-permute-start.5
  139.2 3.5 %collective-permute-start.7 = (bf16[3,32,512]{2,1,0:T(8,128)(2,1)S(1)}, bf16[3,32,512]{2,1,0:T(8,128)(2,1)S(1)}, u32[]{:S(2)}, u32[]{:S(2)}) collective-permute-start(bf16[3,32,512]{2,1,0:T(8,128)(2,1)S(1)} %reduce_sum.102), channel_id=1, source_target_pairs={{0,12},{4,0},{8,4},{12,8},{1,13},{5,1},{9,5},{13,9},{2,14},{6,2},{... | collective-permute-start | bytes 294920 | tf_op jit(solution)/shard_map/ppermute | solution.py:36
  148.0 4.6 %all-to-all-start.3 = ((bf16[16,3,32,512]{3,2,1,0:T(8,128)(2,1)}), bf16[16,3,32,512]{3,2,1,0:T(8,128)(2,1)}, u32[]{:S(2)}, u32[]{:S(2)}) async-start(bf16[16,3,32,512]{3,2,1,0:T(8,128)(2,1)} %broadcast_in_dim.88), calls=%async_computation.3 | async-start | bytes 3145728 | tf_op jit(solution)/shard_map/all_to_all | solution.py:39
  152.6 5.3 %collective-permute-start = (bf16[1,512,512]{2,1,0:T(8,128)(2,1)S(1)}, bf16[1,512,512]{2,1,0:T(8,128)(2,1)}, u32[]{:S(2)}, u32[]{:S(2)}) collective-permute-start(bf16[1,512,512]{2,1,0:T(8,128)(2,1)S(1)} %copy-done.14), channel_id=1, source_target_pairs={{0,4},{4,8},{8,12},{1,5},{5,9},{9,13},{2,6},{6,10},{10,14},{3,7},{... | collective-permute-start | bytes 1572872 | tf_op jit(solution)/shard_map/ppermute | solution.py:24
  157.9 3.1 %collective-permute-start.1 = (bf16[1,512,512]{2,1,0:T(8,128)(2,1)S(1)}, bf16[1,512,512]{2,1,0:T(8,128)(2,1)}, u32[]{:S(2)}, u32[]{:S(2)}) collective-permute-start(bf16[1,512,512]{2,1,0:T(8,128)(2,1)S(1)} %copy-done.15), channel_id=1, source_target_pairs={{0,4},{4,8},{8,12},{1,5},{5,9},{9,13},{2,6},{6,10},{10,14},{3,7},{... | collective-permute-start | bytes 1572872 | tf_op jit(solution)/shard_map/ppermute | solution.py:24
  163.4 2.2 fusion.73
  168.2 3.5 %copy_convert_fusion = f32[16,3,32,512]{3,2,0,1:T(8,128)} fusion(bf16[16,3,32,512]{3,2,1,0:T(8,128)(2,1)} %all-to-all-done.3), kind=kLoop, calls=%fused_computation.44 | loop fusion | flops 786432 | bytes 4718592 | tf_op jit(solution)/shard_map/convert_element_type | solution.py:125
  171.7 3.5 %copy.53 = f32[3,512,512]{1,2,0:T(8,128)} copy(f32[3,512,512]{2,1,0:T(8,128)} %bitcast.191) | data formatting | bytes 6291456 | tf_op jit(solution)/shard_map/convert_element_type | solution.py:125
  177.1 2.4 divide_convert_fusion
  180.6 2.2 convolution_convert_fusion.1
  182.8 6.4 %add_convert_fusion.2 = bf16[3,512,512]{1,2,0:T(8,128)(2,1)} fusion(bf16[3,512,512]{1,2,0:T(8,128)(2,1)} %copy-done.2, bf16[3,512,512]{2,1,0:T(8,128)(2,1)} %convolution_convert_fusion.1), kind=kOutput, calls=%fused_computation.11 | convolution fusion | flops 1617690624 | bytes 4718592 | tf_op jit(solution)/shard_map/...ij,...jk->...ik/dot_general | solution.py:83
  189.2 4.1 %convolution_convert_fusion = bf16[3,512,512]{2,1,0:T(8,128)(2,1)} fusion(bf16[3,512,512]{1,2,0:T(8,128)(2,1)} %add_convert_fusion.2), kind=kOutput, calls=%fused_computation.34 | convolution fusion | flops 806092800 | bytes 3145728 | tf_op jit(solution)/shard_map/...ij,...kj->...ik/dot_general | solution.py:74
  193.3 7.0 %fusion = (f32[3,512]{1,0:T(4,128)S(1)}, f32[3,512]{1,0:T(4,128)S(1)}, bf16[3,512,512]{1,2,0:T(8,128)(2,1)}) fusion(bf16[3,512,512]{1,2,0:T(8,128)(2,1)S(1)} %multiply_convert_fusion.1, f32[]{:T(128)} %bitcast.184, bf16[3,512,512]{1,2,0:T(8,128)(2,1)} %add_convert_fusion.2, bf16[3,512,512]{2,1,0:T(8,128)(2,1)} %convolution_convert_fusion), kind=kOutput, calls=%fused_computation.5 | convolution fusion | flops 1623979008 | bytes 6303748 | tf_op jit(solution)/shard_map/...ij,...jk->...ik/dot_general | solution.py:83
  200.4 3.3 %fusion.55 = (bf16[3,1,512,512]{2,3,0,1:T(8,128)(2,1)}, bf16[1,1,3,512,512]{3,4,2,1,0:T(8,128)(2,1)S(1)}) fusion(f32[3,512]{1,0:T(4,128)S(1)} %rsqrt_multiply_fusion, bf16[3,512,512]{1,2,0:T(8,128)(2,1)} %get-tuple-element.73, f32[]{:T(128)} %bitcast.182, bf16[3,512,512]{1,2,0:T(8,128)(2,1)S(1)} %multiply_convert_fusion.1), kind=kLoop, calls=%fused_computation.124 | loop fusion | flops 4718592 | bytes 6297604 | tf_op jit(solution)/shard_map/transpose | solution.py:184
  207.2 3.5 %fusion.11 = f32[512,512]{0,1:T(8,128)} fusion(f32[512,512]{1,0:T(8,128)} %convolution_bitcast_fusion.1, bf16[1,3,512,512]{2,3,1,0:T(8,128)(2,1)} %copy-done.7, bf16[1,512,512]{2,1,0:T(8,128)(2,1)S(1)} %copy-done.11), kind=kOutput, calls=%fused_computation.60 | convolution fusion | flops 538443776 | bytes 3670016 | tf_op jit(solution)/shard_map/hrf,hfd->hrd/dot_general | solution.py:177
  210.7 3.1 %multiply_reduce_fusion.5 = (f32[512]{0:T(512)S(1)}, f32[512,512]{0,1:T(8,128)}) fusion(f32[512,512]{0,1:T(8,128)} %fusion.11, bf16[1,512,512]{2,1,0:T(8,128)(2,1)S(1)} %copy-done.15, bf16[1,512,512]{2,1,0:T(8,128)(2,1)} %collective-permute-done.1, f32[512,1024]{0,1:T(8,128)S(1)} %copy-done.10, f32[512]{0:T(512)S(1)} %fusion.4, f32[512]{0:T(512)S(1)} %get-tuple-element.74), kind=kOutput, calls=%fused_computation.76 | convolution fusion | flops 541326848 | bytes 5249024 | tf_op jit(solution)/shard_map/while/body/eval_jaxpr/hrk,hkd->hrd/dot_general | solution.py:159
  213.9 32.6 %psum.7 = f32[512]{0:T(512)S(1)} all-reduce(f32[512]{0:T(512)S(1)} %get-tuple-element.76), channel_id=1, replica_groups=mesh['x'=4,'y'=4,'z'=4,'w'=2,'c'=2] {'w','c'}, use_global_device_ids=true, to_apply=%region_11.12 | all-reduce | flops 512 | bytes 4096 | tf_op jit(solution)/shard_map/psum | solution.py:179
  (89 shorter events, 41.4 us)
Async XLA Ops:
  0.6 1.1 copy-start
  0.6 2.6 %copy-start.5 = (bf16[3,1,512,512]{3,2,1,0:T(8,128)(2,1)S(1)}, bf16[3,1,512,512]{3,2,1,0:T(8,128)(2,1)}, u32[]{:S(2)}) copy-start(bf16[3,1,512,512]{3,2,1,0:T(8,128)(2,1)} %param.16) | copy-start | bytes 4718596
  0.7 2.5 %copy-start.13 = (f32[1,512]{1,0:T(1,128)S(1)}, f32[1,512]{1,0:T(1,128)}, u32[]{:S(2)}) copy-start(f32[1,512]{1,0:T(1,128)} %param.14) | copy-start | bytes 6148
  0.7 2.6 %copy-start.8 = (bf16[1,512,512]{2,1,0:T(8,128)(2,1)S(1)}, bf16[1,512,512]{2,1,0:T(8,128)(2,1)}, u32[]{:S(2)}) copy-start(bf16[1,512,512]{2,1,0:T(8,128)(2,1)} %param.13) | copy-start | bytes 1572868
  35.6 10.6 %collective-permute-start.2 = (bf16[3,32,512]{2,1,0:T(8,128)(2,1)S(1)}, bf16[3,32,512]{2,1,0:T(8,128)(2,1)S(1)}, u32[]{:S(2)}, u32[]{:S(2)}) collective-permute-start(bf16[3,32,512]{2,1,0:T(8,128)(2,1)S(1)} %reduce_sum.98), channel_id=1, source_target_pairs={{0,4},{4,8},{8,12},{12,0},{1,5},{5,9},{9,13},{13,1},{2,6},{6,10},{... | collective-permute-start | bytes 294920 | tf_op jit(solution)/shard_map/ppermute | solution.py:36
  38.7 9.0 %collective-permute-start.3 = (bf16[3,32,512]{2,1,0:T(8,128)(2,1)S(1)}, bf16[3,32,512]{2,1,0:T(8,128)(2,1)S(1)}, u32[]{:S(2)}, u32[]{:S(2)}) collective-permute-start(bf16[3,32,512]{2,1,0:T(8,128)(2,1)S(1)} %reduce_sum.98), channel_id=1, source_target_pairs={{0,8},{4,12},{8,0},{12,4},{1,9},{5,13},{9,1},{13,5},{2,10},{6,14},... | collective-permute-start | bytes 294920 | tf_op jit(solution)/shard_map/ppermute | solution.py:36
  43.8 5.7 %collective-permute-start.4 = (bf16[3,32,512]{2,1,0:T(8,128)(2,1)S(1)}, bf16[3,32,512]{2,1,0:T(8,128)(2,1)S(1)}, u32[]{:S(2)}, u32[]{:S(2)}) collective-permute-start(bf16[3,32,512]{2,1,0:T(8,128)(2,1)S(1)} %reduce_sum.98), channel_id=1, source_target_pairs={{0,12},{4,0},{8,4},{12,8},{1,13},{5,1},{9,5},{13,9},{2,14},{6,2},{... | collective-permute-start | bytes 294920 | tf_op jit(solution)/shard_map/ppermute | solution.py:36
  50.9 24.3 %all-to-all-start.1 = ((bf16[16,3,32,512]{3,2,1,0:T(8,128)(2,1)}), bf16[16,3,32,512]{3,2,1,0:T(8,128)(2,1)S(1)}, u32[]{:S(2)}, u32[]{:S(2)}) async-start(bf16[16,3,32,512]{3,2,1,0:T(8,128)(2,1)} %broadcast_in_dim.87), calls=%async_computation.1 | async-start | bytes 3145728 | tf_op jit(solution)/shard_map/all_to_all | solution.py:39
  91.4 4.2 %copy-start.3 = (bf16[3,1,512,512]{2,3,0,1:T(8,128)(2,1)S(1)}, bf16[3,1,512,512]{2,3,0,1:T(8,128)(2,1)}, u32[]{:S(2)}) copy-start(bf16[3,1,512,512]{2,3,0,1:T(8,128)(2,1)} %copy.42) | copy-start | bytes 4718596
  134.8 7.9 %collective-permute-start.5 = (bf16[3,32,512]{2,1,0:T(8,128)(2,1)S(1)}, bf16[3,32,512]{2,1,0:T(8,128)(2,1)S(1)}, u32[]{:S(2)}, u32[]{:S(2)}) collective-permute-start(bf16[3,32,512]{2,1,0:T(8,128)(2,1)S(1)} %reduce_sum.102), channel_id=1, source_target_pairs={{0,4},{4,8},{8,12},{12,0},{1,5},{5,9},{9,13},{13,1},{2,6},{6,10},{... | collective-permute-start | bytes 294920 | tf_op jit(solution)/shard_map/ppermute | solution.py:36
  137.2 7.5 %collective-permute-start.6 = (bf16[3,32,512]{2,1,0:T(8,128)(2,1)S(1)}, bf16[3,32,512]{2,1,0:T(8,128)(2,1)S(1)}, u32[]{:S(2)}, u32[]{:S(2)}) collective-permute-start(bf16[3,32,512]{2,1,0:T(8,128)(2,1)S(1)} %reduce_sum.102), channel_id=1, source_target_pairs={{0,8},{4,12},{8,0},{12,4},{1,9},{5,13},{9,1},{13,5},{2,10},{6,14},... | collective-permute-start | bytes 294920 | tf_op jit(solution)/shard_map/ppermute | solution.py:36
  139.2 7.4 %collective-permute-start.7 = (bf16[3,32,512]{2,1,0:T(8,128)(2,1)S(1)}, bf16[3,32,512]{2,1,0:T(8,128)(2,1)S(1)}, u32[]{:S(2)}, u32[]{:S(2)}) collective-permute-start(bf16[3,32,512]{2,1,0:T(8,128)(2,1)S(1)} %reduce_sum.102), channel_id=1, source_target_pairs={{0,12},{4,0},{8,4},{12,8},{1,13},{5,1},{9,5},{13,9},{2,14},{6,2},{... | collective-permute-start | bytes 294920 | tf_op jit(solution)/shard_map/ppermute | solution.py:36
  148.0 4.6 %copy-start.14 = (bf16[1,512,512]{2,1,0:T(8,128)(2,1)S(1)}, bf16[1,512,512]{2,1,0:T(8,128)(2,1)}, u32[]{:S(2)}) copy-start(bf16[1,512,512]{2,1,0:T(8,128)(2,1)} %param.19) | copy-start | bytes 1572868
  148.0 9.9 %copy-start.15 = (bf16[1,512,512]{2,1,0:T(8,128)(2,1)S(1)}, bf16[1,512,512]{2,1,0:T(8,128)(2,1)}, u32[]{:S(2)}) copy-start(bf16[1,512,512]{2,1,0:T(8,128)(2,1)} %param.20) | copy-start | bytes 1572868
  148.0 13.1 %copy-start.16 = (s32[16]{0:T(128)S(1)}, s32[16]{0:T(128)}, u32[]{:S(2)}) copy-start(s32[16]{0:T(128)} %param.22) | copy-start | bytes 196
  148.0 14.2 %copy-start.17 = (s32[16]{0:T(128)S(1)}, s32[16]{0:T(128)}, u32[]{:S(2)}) copy-start(s32[16]{0:T(128)} %param.21) | copy-start | bytes 196
  148.0 15.4 %copy-start.11 = (bf16[1,512,512]{2,1,0:T(8,128)(2,1)S(1)}, bf16[1,512,512]{2,1,0:T(8,128)(2,1)}, u32[]{:S(2)}) copy-start(bf16[1,512,512]{2,1,0:T(8,128)(2,1)} %param.18) | copy-start | bytes 1572868
  148.0 20.2 %all-to-all-start.3 = ((bf16[16,3,32,512]{3,2,1,0:T(8,128)(2,1)}), bf16[16,3,32,512]{3,2,1,0:T(8,128)(2,1)}, u32[]{:S(2)}, u32[]{:S(2)}) async-start(bf16[16,3,32,512]{3,2,1,0:T(8,128)(2,1)} %broadcast_in_dim.88), calls=%async_computation.3 | async-start | bytes 3145728 | tf_op jit(solution)/shard_map/all_to_all | solution.py:39
  152.6 10.8 %collective-permute-start = (bf16[1,512,512]{2,1,0:T(8,128)(2,1)S(1)}, bf16[1,512,512]{2,1,0:T(8,128)(2,1)}, u32[]{:S(2)}, u32[]{:S(2)}) collective-permute-start(bf16[1,512,512]{2,1,0:T(8,128)(2,1)S(1)} %copy-done.14), channel_id=1, source_target_pairs={{0,4},{4,8},{8,12},{1,5},{5,9},{9,13},{2,6},{6,10},{10,14},{3,7},{... | collective-permute-start | bytes 1572872 | tf_op jit(solution)/shard_map/ppermute | solution.py:24
  157.9 52.8 %collective-permute-start.1 = (bf16[1,512,512]{2,1,0:T(8,128)(2,1)S(1)}, bf16[1,512,512]{2,1,0:T(8,128)(2,1)}, u32[]{:S(2)}, u32[]{:S(2)}) collective-permute-start(bf16[1,512,512]{2,1,0:T(8,128)(2,1)S(1)} %copy-done.15), channel_id=1, source_target_pairs={{0,4},{4,8},{8,12},{1,5},{5,9},{9,13},{2,6},{6,10},{10,14},{3,7},{... | collective-permute-start | bytes 1572872 | tf_op jit(solution)/shard_map/ppermute | solution.py:24
  165.6 1.3 copy-start.9
  179.5 1.2 copy-start.2
  200.3 3.3 %copy-start.4 = (bf16[3,1,512,512]{2,3,0,1:T(8,128)(2,1)S(1)}, bf16[3,1,512,512]{2,3,0,1:T(8,128)(2,1)}, u32[]{:S(2)}) copy-start(bf16[3,1,512,512]{2,3,0,1:T(8,128)(2,1)} %copy.42) | copy-start | bytes 4718596
  204.6 1.1 copy-start.7
  207.2 3.5 %copy-start.10 = (f32[512,1024]{0,1:T(8,128)S(1)}, f32[512,1024]{0,1:T(8,128)}, u32[]{:S(2)}) copy-start(f32[512,1024]{0,1:T(8,128)} %copy-done.9) | copy-start | bytes 6291460
  210.7 35.7 %copy-start.12 = (f32[1,512]{1,0:T(1,128)S(1)}, f32[1,512]{1,0:T(1,128)}, u32[]{:S(2)}) copy-start(f32[1,512]{1,0:T(1,128)} %param.23) | copy-start | bytes 6148
  213.9 35.0 %copy-start.6 = (bf16[3,1,512,512]{2,3,0,1:T(8,128)(2,1)S(1)}, bf16[3,1,512,512]{2,3,0,1:T(8,128)(2,1)}, u32[]{:S(2)}) copy-start(bf16[3,1,512,512]{2,3,0,1:T(8,128)(2,1)} %get-tuple-element.61) | copy-start | bytes 4718596
  248.8 1.6 copy-start.1

commit v2 on v1

v2 whole, which is shorter than its diff:
```python
import functools
import jax
import jax.numpy as jnp
from jax import lax
from jax.experimental import pallas as pl
from jax.experimental.pallas import tpu as pltpu
from jax.sharding import Mesh
from jax.sharding import PartitionSpec as P

PLANE = ("x", "y")
SEQ = ("x", "y", "z")
HEAD = ("w", "c")
NS_STEPS = 2
BR_SPAN = 4

poly_one = 3.4445
poly_two = -4.775
poly_three = 2.0315
VMEM_BYTES = 40 * 1024 * 1024


def nt(left, right):
    return lax.dot_general(left, right, (((1,), (1,)), ((), ())), preferred_element_type=jnp.float32)


def nn(left, right):
    return jnp.dot(left, right, preferred_element_type=jnp.float32)


def column_of(row):
    return jnp.transpose(jnp.broadcast_to(row, (128, row.shape[1])))


def emit_gradient(weights, keys_ref, values_ref, rates, parts_ref):
    planes = parts_ref.shape[0]
    step = parts_ref.shape[2]
    keys = keys_ref[...]
    rate_columns = jnp.tile(column_of(rates), (1, keys.shape[1] // 128))
    pushed = (rate_columns * values_ref[...].astype(jnp.float32)).astype(jnp.bfloat16)
    rows = weights[0].shape[0]
    chunk = 256
    for start in range(0, rows, chunk):
        cut = slice(start, start + chunk)
        first = nt(weights[0][cut], keys)
        third = nt(weights[1][cut], keys)
        gate = jax.nn.sigmoid(first)
        silu = first * gate
        hidden = (silu * third).astype(jnp.bfloat16)
        returned = nt(weights[2][cut], pushed)
        delta_first = (returned * third * gate * (1.0 + first * (1.0 - gate))).astype(jnp.bfloat16)
        delta_third = (returned * silu).astype(jnp.bfloat16)
        for kind, grad in enumerate((nn(delta_first, keys), nn(delta_third, keys), nn(hidden, pushed))):
            grad = grad.astype(jnp.bfloat16)
            for part in range(chunk // step):
                parts_ref[start // step + part, kind] = grad[part * step : (part + 1) * step]


def emit_update(gathered_ref, weights_ref, step_size, x_ref, gram_ref, out_ref):
    planes, kinds, step, _ = gathered_ref.shape
    rows = planes * step
    for kind in range(kinds):
        wide = jnp.concatenate([gathered_ref[part, kind] for part in range(planes)], axis=0).astype(jnp.float32)
        square = jnp.sum(jnp.sum(wide * wide, axis=0, keepdims=True), axis=1, keepdims=True)
        inverse = 1.0 / (jnp.sqrt(square) + 1e-07)
        x_ref[0, kind] = (wide * inverse).astype(jnp.bfloat16)
    chunk = 256
    for sweep in range(NS_STEPS):
        now, later = sweep % 2, (sweep + 1) % 2
        for kind in range(kinds):
            full = x_ref[now, kind]
            gram_ref[kind] = nt(full, full).astype(jnp.bfloat16)
        for kind in range(kinds):
            full = x_ref[now, kind]
            gram = gram_ref[kind]
            for start in range(0, rows, chunk):
                cut = slice(start, start + chunk)
                own = gram[cut]
                poly = (poly_two * own.astype(jnp.float32) + poly_three * nn(own, gram)).astype(jnp.bfloat16)
                moved = (poly_one * full[cut].astype(jnp.float32) + nn(poly, full)).astype(jnp.bfloat16)
                if sweep < NS_STEPS - 1:
                    x_ref[later, kind, cut] = moved
                else:
                    old = weights_ref[kind, cut].astype(jnp.float32)
                    new = old + step_size * moved.astype(jnp.float32)
                    old_mean = jnp.mean(old * old, axis=-1, keepdims=True) + 1e-06
                    new_mean = jnp.mean(new * new, axis=-1, keepdims=True) + 1e-06
                    out_ref[kind, cut] = (new * (jnp.sqrt(old_mean) * lax.rsqrt(new_mean))).astype(jnp.bfloat16)


def masked_rates(rates_ref, seq_ref, split_ref, period):
    rates = rates_ref[...]
    count = rates.shape[1]
    positions = seq_ref[0] * count + lax.broadcasted_iota(jnp.int32, rates.shape, 1)
    early = positions < split_ref[0]
    return jnp.where(early if period == 0 else jnp.logical_not(early), rates, 0.0)


def first_kernel(seq_ref, split_ref, weights_ref, keys_ref, values_ref, rates_ref, parts_ref):
    rates = masked_rates(rates_ref, seq_ref, split_ref, 0)
    emit_gradient([weights_ref.at[kind] for kind in range(3)], keys_ref, values_ref, rates, parts_ref)


def second_kernel(seq_ref, split_ref, step_ref, gathered_ref, weights_ref, keys_ref, values_ref, rates_ref, state_ref, parts_ref, x_ref, gram_ref):
    emit_update(gathered_ref, weights_ref, step_ref[0], x_ref, gram_ref, state_ref)
    rates = masked_rates(rates_ref, seq_ref, split_ref, 1)
    emit_gradient([state_ref.at[kind] for kind in range(3)], keys_ref, values_ref, rates, parts_ref)


def attend_kernel(seq_ref, length_ref, query_ref, prior_keys_ref, keys_ref, prior_values_ref, values_ref, out_ref):
    rows, width = query_ref.shape
    branch = seq_ref[0] // BR_SPAN
    place = seq_ref[0] % BR_SPAN
    live = length_ref[branch] - place * rows
    scale = width ** (-0.5)
    chunk = 128
    for start in range(0, rows, chunk):
        cut = slice(start, start + chunk)
        query = query_ref[cut]
        row = start + lax.broadcasted_iota(jnp.int32, (chunk, rows), 0)
        slot = lax.broadcasted_iota(jnp.int32, (chunk, rows), 1)
        behind = slot > row
        allowed = (slot == row) | (slot < jnp.where(behind, jnp.where(place > 0, rows, 0), live))
        scores = jnp.where(behind, nt(query, prior_keys_ref[...]), nt(query, keys_ref[...])) * scale
        scores = jnp.where(allowed, scores, -1e30)
        top = jnp.max(scores, axis=-1, keepdims=True)
        power = jnp.exp(scores - top)
        share = power * (1.0 / jnp.sum(power, axis=-1, keepdims=True))
        out_ref[cut] = nn(jnp.where(behind, share, 0.0).astype(jnp.bfloat16), prior_values_ref[...]) + nn(
            jnp.where(behind, 0.0, share).astype(jnp.bfloat16), values_ref[...]
        )


def third_kernel(seq_ref, split_ref, fork_ref, step_ref, gathered_ref, weights_ref, state_ref, query_ref, attended_ref, last_ref, total_ref, energy_ref, x_ref, gram_ref, trunk_total):
    emit_update(gathered_ref, state_ref, step_ref[0], x_ref, gram_ref, last_ref)
    fork = fork_ref[seq_ref[0] // BR_SPAN]

    @pl.when(fork < split_ref[0])
    def _():
        x_ref[0] = weights_ref[...]

    @pl.when((fork >= split_ref[0]) & (fork < trunk_total))
    def _():
        x_ref[0] = state_ref[...]

    @pl.when((fork >= split_ref[0]) & (fork >= trunk_total))
    def _():
        x_ref[0] = last_ref[...]

    rows = query_ref.shape[0]
    chunk = 256
    for start in range(0, rows, chunk):
        cut = slice(start, start + chunk)
        query = query_ref[cut]
        first = nt(query, x_ref[0, 0])
        third = nt(query, x_ref[0, 1])
        hidden = (first * jax.nn.sigmoid(first) * third).astype(jnp.bfloat16)
        total = attended_ref[cut] + nn(hidden, x_ref[0, 2])
        total_ref[cut] = total
        energy = jnp.sum(total * total, axis=-1, keepdims=True)
        energy_ref[:, cut] = jnp.transpose(jnp.broadcast_to(energy, (chunk, 128)))[0:1]


def last_kernel(seq_ref, length_ref, total_ref, energy_ref, gain_ref, out_ref, width):
    rows = total_ref.shape[0]
    live = length_ref[seq_ref[0] // BR_SPAN] - (seq_ref[0] % BR_SPAN) * rows
    slot = lax.broadcasted_iota(jnp.int32, (1, rows), 1)
    inverse = jnp.where(slot < live, lax.rsqrt(energy_ref[...] / width + 1e-06), 0.0)
    columns = jnp.tile(column_of(inverse), (1, total_ref.shape[1] // 128))
    out_ref[...] = (total_ref[...] * columns * gain_ref[...]).astype(jnp.bfloat16)


SMEM = pl.BlockSpec(memory_space=pltpu.SMEM)
VMEM = pl.BlockSpec(memory_space=pltpu.VMEM)


def call(kernel, scalars, arrays, outs, scratch=(), flops=0, name=None):
    moved = sum(array.size * array.dtype.itemsize for array in (*arrays, *outs))
    return pl.pallas_call(
        kernel,
        out_shape=outs,
        in_specs=[SMEM] * len(scalars) + [VMEM] * len(arrays),
        out_specs=[VMEM] * len(outs),
        scratch_shapes=list(scratch),
        compiler_params=pltpu.CompilerParams(vmem_limit_bytes=VMEM_BYTES),
        cost_estimate=pl.CostEstimate(flops=flops, bytes_accessed=moved, transcendentals=0),
        name=name,
    )(*scalars, *arrays)


def shape(dims, kind):
    return jax.ShapeDtypeStruct(dims, kind)


def update_scratch(dims):
    return (pltpu.VMEM((2, *dims), jnp.bfloat16), pltpu.VMEM(dims, jnp.bfloat16))


def from_behind(value):
    count = lax.axis_size("z")
    return lax.ppermute(value, "z", [(source, source + 1) for source in range(count - 1)])


def sum_plane(parts):
    received = lax.all_to_all(parts, PLANE, 0, 0, tiled=False)
    return jnp.sum(received.astype(jnp.float32), axis=0).astype(jnp.bfloat16)


def sum_depth(mine):
    depth = lax.axis_size("z")
    total = mine.astype(jnp.float32)
    for step in range(1, depth):
        other = lax.ppermute(mine, "z", [(i, (i + step) % depth) for i in range(depth)])
        total = total + other.astype(jnp.float32)
    return total.astype(jnp.bfloat16)


def spread_plane(total):
    planes = lax.axis_size(PLANE)
    copies = jnp.broadcast_to(total[None], (planes, *total.shape))
    return lax.all_to_all(copies, PLANE, 0, 0, tiled=False)


def per_device(
    trunk_keys,
    trunk_values,
    trunk_rates,
    segment_end,
    fast_weights,
    step_sizes,
    branch_query,
    branch_keys,
    branch_values,
    branch_lengths,
    fork_points,
    out_gain,
):
    keys, values = trunk_keys[0], trunk_values[0]
    weights = fast_weights[:, 0]
    query, own_keys, own_values = branch_query[0], branch_keys[0], branch_values[0]
    rows, width = keys.shape
    hidden = weights.shape[1]
    planes = lax.axis_size(PLANE)
    trunk_total = rows * lax.axis_size(SEQ)
    total_width = width * lax.axis_size(HEAD)
    seq = lax.axis_index(SEQ).astype(jnp.int32).reshape(1)
    product = 2 * rows * width * hidden
    parts_shape = shape((planes, 3, hidden // planes, width), jnp.bfloat16)
    state_shape = shape(weights.shape, jnp.bfloat16)
    scratch = update_scratch(weights.shape)

    prior_keys = from_behind(own_keys)
    (parts,) = call(
        first_kernel,
        (seq, segment_end),
        (weights, keys, values, trunk_rates),
        (parts_shape,),
        flops=6 * product,
    )
    mine = sum_plane(parts)
    mine, prior_keys = lax.optimization_barrier((mine, prior_keys))
    summed, sent_values = lax.optimization_barrier((sum_depth(mine), own_values))
    prior_values = from_behind(sent_values)
    gathered, prior_values = lax.optimization_barrier((spread_plane(summed), prior_values))
    state, parts = call(
        second_kernel,
        (seq, segment_end, step_sizes),
        (gathered, weights, keys, values, trunk_rates),
        (state_shape, parts_shape),
        scratch,
        flops=24 * product,
    )
    (attended,) = call(
        attend_kernel,
        (seq, branch_lengths),
        (query, prior_keys, own_keys, prior_values, own_values),
        (shape((rows, width), jnp.float32),),
        flops=4 * product,
    )
    gathered = spread_plane(sum_depth(sum_plane(parts)))
    last, total, energy = call(
        functools.partial(third_kernel, trunk_total=trunk_total),
        (seq, segment_end, fork_points, step_sizes),
        (gathered, weights, state, query, attended),
        (state_shape, shape((rows, width), jnp.float32), shape((1, rows), jnp.float32)),
        scratch,
        flops=21 * product,
    )
    energy = lax.psum(energy, HEAD)
    (result,) = call(
        functools.partial(last_kernel, width=total_width),
        (seq, branch_lengths),
        (total, energy, out_gain),
        (shape((rows, width), jnp.bfloat16),),
    )
    return (result[None], last[:, None])


def solution(mesh):
    fine = Mesh(mesh.devices.reshape(4, 4, 4, 2, 2), (*SEQ, *HEAD))
    rows = P(HEAD, SEQ, None)
    placed = (
        rows,
        rows,
        P(HEAD, SEQ),
        P(),
        P(None, HEAD, None, None),
        P(HEAD),
        rows,
        rows,
        rows,
        P(),
        P(),
        P(HEAD, None),
    )
    return jax.shard_map(
        per_device,
        mesh=fine,
        in_specs=placed,
        out_specs=(rows, P(None, HEAD, None, None)),
        check_vma=False,
    )
```

time: 251 us -> 200 us (0.80)
  matrix products: 56.4 us -> 0 us
  blocking collectives: 86 us -> 44.3 us
  waiting for transfers between devices: 22.1 us -> 51.9 us
  Pallas kernels: 0 us -> 28.5 us
  other arithmetic: 25.4 us -> 0.62 us
  starting transfers between devices: 36.6 us -> 52.7 us
    dot_general x24 -> x0, matrix products: 56.4 us -> none  [the longest x4 25.7 us: iterate_polynomial(): jnp.einsum('...ij,...jk->...ik', polynomial, current, preferred_element_t...]
    all_to_all x2 -> x1, blocking collectives: 53.4 us -> 23 us  [sum_plane(): received = lax.all_to_all(parts, PLANE, 0, 0, tiled=False)]
    pallas_call x0 -> x5, Pallas kernels: none -> 28.5 us  [call(): pl.pallas_call(kernel, out_shape=outs, in_specs=[SMEM] * len(scalars) + [...]
    all_to_all x2 -> x3, waiting for transfers between devices: 14.9 us -> 33.1 us  [the longest x2 17.4 us: spread_plane(): return lax.all_to_all(copies, PLANE, 0, 0, tiled=False)]
    convert_element_type x8 -> x2, other arithmetic: 14.3 us -> 0.11 us  [sum_depth(): return total.astype(jnp.bfloat16)]
    psum x1, blocking collectives: 32.6 us -> 21.3 us  [per_device(): energy = lax.psum(energy, HEAD)]
    all_to_all x2 -> x3, starting transfers between devices: 9.75 us -> 18.2 us  [the longest x2 10.4 us: spread_plane(): return lax.all_to_all(copies, PLANE, 0, 0, tiled=False)]
    ppermute x2, waiting for transfers between devices: 0.01 us -> 8.21 us  [from_behind(): lax.ppermute(value, 'z', [(source, source + 1) for source in range(count...]
  transfers between devices with their start and end apart: 10 -> 11, of which waited for: 6 -> 6; matrix products, arithmetic and copies ran while one was open for 19% -> 0% of each run, Pallas kernels for 0% -> 2%
where the time goes in v2:
time: 200 us; the launch traced here: 199 us
  starting transfers between devices  52.7 us (26%)
  waiting for transfers between devices  51.9 us (26%)
  blocking collectives  44.3 us (22%)
  Pallas kernels  28.5 us (14%)
  local copies, waits for them, and re-layouts  18.8 us (9%)
  between operations  2.12 us (1%)
    pallas_call x5, Pallas kernels, call(): pl.pallas_call(kernel, out_shape=outs, in_specs=[SMEM] * len(scalars) + [...  28.5 us
    ppermute x6, starting transfers between devices, sum_depth(): lax.ppermute(mine, 'z', [(i, (i + step) % depth) for i in range(depth)])  25.3 us
    all_to_all x1, blocking collectives, sum_plane(): received = lax.all_to_all(parts, PLANE, 0, 0, tiled=False)  23 us
    psum x1, blocking collectives, per_device(): energy = lax.psum(energy, HEAD)  21.3 us
    all_to_all x2, waiting for transfers between devices, spread_plane(): return lax.all_to_all(copies, PLANE, 0, 0, tiled=False)  17.4 us
    unnamed x48, local copies, waits for them, and re-layouts  16.2 us
    all_to_all x1, waiting for transfers between devices, sum_plane(): received = lax.all_to_all(parts, PLANE, 0, 0, tiled=False)  15.7 us
    ppermute x6, waiting for transfers between devices, sum_depth(): lax.ppermute(mine, 'z', [(i, (i + step) % depth) for i in range(depth)])  10.6 us
  transfers between devices with their start and end apart: 11, of which 6 were waited for; matrix products, arithmetic and copies ran while one was open for 0% of the time, Pallas kernels for 2%

profile of v2, /device:TPU:1, one launch (start us, length us, event | category | flops | bytes accessed | tf_op | source)
XLA Modules:
  0.0 198.9 jit_solution(7169229057520830879)
XLA Ops:
  1.3 1.4 copy-done.2
  3.7 1.0 copy-done.7
  5.5 3.3 %shard_map.131 = bf16[16,3,32,512]{3,2,1,0:T(8,128)(2,1)} custom-call(s32[1]{0:T(128)} %bitcast.seq_ref, s32[1]{0:T(128)S(6)} %copy.15.split_ref, bf16[3,512,512]{2,1,0:T(8,128)(2,1)S(1)} %bitcast.11, bf16[512,512]{1,0:T(8,128)(2,1)S(1)} %bitcast.14, bf16[512,512]{1,0:T(8,128)(2,1)S(1)} %bitcast.16, f32[1,512]{1,0:T(1,128)S(1)} %copy-done.17), custom_call_target="tpu_custom_call" | custom-call | flops 1610612736 | bytes 4196352 | tf_op jit(solution)/shard_map/pallas_call | solution.py:178
  8.8 7.7 %all-to-all-start = ((bf16[16,3,32,512]{3,2,1,0:T(8,128)(2,1)}), bf16[16,3,32,512]{3,2,1,0:T(8,128)(2,1)S(1)}, u32[]{:S(2)}, u32[]{:S(2)}) async-start(bf16[16,3,32,512]{3,2,1,0:T(8,128)(2,1)} %shard_map.131), calls=%async_computation | async-start | bytes 3145728 | tf_op jit(solution)/shard_map/all_to_all | solution.py:204
  16.5 4.9 %collective-permute-start = (bf16[512,512]{1,0:T(8,128)(2,1)S(1)}, bf16[512,512]{1,0:T(8,128)(2,1)S(1)}, u32[]{:S(2)}, u32[]{:S(2)}) collective-permute-start(bf16[512,512]{1,0:T(8,128)(2,1)S(1)} %bitcast.18), channel_id=1, source_target_pairs={{0,4},{4,8},{8,12},{1,5},{5,9},{9,13},{2,6},{6,10},{10,14},{3,7},{... | collective-permute-start | bytes 1572872 | tf_op jit(solution)/shard_map/ppermute | solution.py:200
  21.4 15.7 %all-to-all-done = bf16[16,3,32,512]{3,2,1,0:T(8,128)(2,1)S(1)} async-done(((bf16[16,3,32,512]{3,2,1,0:T(8,128)(2,1)}), bf16[16,3,32,512]{3,2,1,0:T(8,128)(2,1)S(1)}, u32[]{:S(2)}, u32[]{:S(2)}) %all-to-all-start) | async-done | bytes 1572896 | tf_op jit(solution)/shard_map/all_to_all | solution.py:204
  38.2 6.0 %collective-permute-start.3 = (bf16[3,32,512]{2,1,0:T(8,128)(2,1)S(1)}, bf16[3,32,512]{2,1,0:T(8,128)(2,1)S(1)}, u32[]{:S(2)}, u32[]{:S(2)}) collective-permute-start(bf16[3,32,512]{2,1,0:T(8,128)(2,1)S(1)} %reduce_sum.24), channel_id=1, source_target_pairs={{0,12},{4,0},{8,4},{12,8},{1,13},{5,1},{9,5},{13,9},{2,14},{6,2},{... | collective-permute-start | bytes 294920 | tf_op jit(solution)/shard_map/ppermute | solution.py:212
  44.2 7.7 %collective-permute-start.2 = (bf16[3,32,512]{2,1,0:T(8,128)(2,1)S(1)}, bf16[3,32,512]{2,1,0:T(8,128)(2,1)S(1)}, u32[]{:S(2)}, u32[]{:S(2)}) collective-permute-start(bf16[3,32,512]{2,1,0:T(8,128)(2,1)S(1)} %reduce_sum.24), channel_id=1, source_target_pairs={{0,8},{4,12},{8,0},{12,4},{1,9},{5,13},{9,1},{13,5},{2,10},{6,14},... | collective-permute-start | bytes 294920 | tf_op jit(solution)/shard_map/ppermute | solution.py:212
  51.9 2.4 %collective-permute-start.1 = (bf16[3,32,512]{2,1,0:T(8,128)(2,1)S(1)}, bf16[3,32,512]{2,1,0:T(8,128)(2,1)S(1)}, u32[]{:S(2)}, u32[]{:S(2)}) collective-permute-start(bf16[3,32,512]{2,1,0:T(8,128)(2,1)S(1)} %reduce_sum.24), channel_id=1, source_target_pairs={{0,4},{4,8},{8,12},{12,0},{1,5},{5,9},{9,13},{13,1},{2,6},{6,10},{... | collective-permute-start | bytes 294920 | tf_op jit(solution)/shard_map/ppermute | solution.py:212
  54.3 6.0 %collective-permute-done.1 = bf16[3,32,512]{2,1,0:T(8,128)(2,1)S(1)} collective-permute-done((bf16[3,32,512]{2,1,0:T(8,128)(2,1)S(1)}, bf16[3,32,512]{2,1,0:T(8,128)(2,1)S(1)}, u32[]{:S(2)}, u32[]{:S(2)}) %collective-permute-start.1) | collective-permute-done | bytes 98336 | tf_op jit(solution)/shard_map/ppermute | solution.py:212
  60.3 1.3 broadcast_in_dim.8
  61.7 6.4 %all-to-all-start.1 = ((bf16[16,3,32,512]{3,2,1,0:T(8,128)(2,1)}), bf16[16,3,32,512]{3,2,1,0:T(8,128)(2,1)S(1)}, u32[]{:S(2)}, u32[]{:S(2)}) async-start(bf16[16,3,32,512]{3,2,1,0:T(8,128)(2,1)} %broadcast_in_dim.8), calls=%async_computation.1 | async-start | bytes 3145728 | tf_op jit(solution)/shard_map/all_to_all | solution.py:220
  68.0 4.3 %collective-permute-start.4 = (bf16[512,512]{1,0:T(8,128)(2,1)}, bf16[512,512]{1,0:T(8,128)(2,1)S(1)}, u32[]{:S(2)}, u32[]{:S(2)}) collective-permute-start(bf16[512,512]{1,0:T(8,128)(2,1)} %bitcast.20), channel_id=1, source_target_pairs={{0,4},{4,8},{8,12},{1,5},{5,9},{9,13},{2,6},{6,10},{10,14},{3,7},{... | collective-permute-start | bytes 1572872 | tf_op jit(solution)/shard_map/ppermute | solution.py:200
  73.0 8.2 %collective-permute-done.4.prior_values_ref = bf16[512,512]{1,0:T(8,128)(2,1)S(1)} collective-permute-done((bf16[512,512]{1,0:T(8,128)(2,1)}, bf16[512,512]{1,0:T(8,128)(2,1)S(1)}, u32[]{:S(2)}, u32[]{:S(2)}) %collective-permute-start.4) | collective-permute-done | bytes 524320 | tf_op jit(solution)/shard_map/ppermute | solution.py:200
  82.0 5.9 %all-to-all-done.1.gathered_ref = bf16[16,3,32,512]{3,2,1,0:T(8,128)(2,1)S(1)} async-done(((bf16[16,3,32,512]{3,2,1,0:T(8,128)(2,1)}), bf16[16,3,32,512]{3,2,1,0:T(8,128)(2,1)S(1)}, u32[]{:S(2)}, u32[]{:S(2)}) %all-to-all-start.1) | async-done | bytes 1572896 | tf_op jit(solution)/shard_map/all_to_all | solution.py:220
  88.0 1.0 copy-done.6
  90.1 9.4 %shard_map.132 = (bf16[3,512,512]{2,1,0:T(8,128)(2,1)S(1)}, bf16[16,3,32,512]{3,2,1,0:T(8,128)(2,1)S(1)}) custom-call(s32[1]{0:T(128)} %bitcast.seq_ref, s32[1]{0:T(128)S(6)} %copy.15.split_ref, f32[1]{0:T(128)S(6)} %copy.16.step_ref, bf16[16,3,32,512]{3,2,1,0:T(8,128)(2,1)S(1)} %all-to-all-done.1.gathered_ref, bf16[3,512,512]{2,1,0:T(8,128)(2,1)S(1)} %bitcast.12, ...), custom_call_target="tpu_custom_call" | custom-call | flops 6442450944 | bytes 7342080 | tf_op jit(solution)/shard_map/pallas_call | solution.py:178
  99.5 1.2 copy-done.22
  100.6 23.0 %all_to_all.20 = bf16[16,3,32,512]{3,2,1,0:T(8,128)(2,1)S(1)} all-to-all(bf16[16,3,32,512]{3,2,1,0:T(8,128)(2,1)S(1)} %get-tuple-element.17), channel_id=1, replica_groups=mesh['x'=4,'y'=4,'z'=4,'w'=2,'c'=2] {'x','y'}, dimensions={0} | all-to-all | bytes 3145728 | tf_op jit(solution)/shard_map/all_to_all | solution.py:204
  124.3 6.5 %collective-permute-start.6 = (bf16[3,32,512]{2,1,0:T(8,128)(2,1)S(1)}, bf16[3,32,512]{2,1,0:T(8,128)(2,1)S(1)}, u32[]{:S(2)}, u32[]{:S(2)}) collective-permute-start(bf16[3,32,512]{2,1,0:T(8,128)(2,1)S(1)} %reduce_sum.25), channel_id=1, source_target_pairs={{0,8},{4,12},{8,0},{12,4},{1,9},{5,13},{9,1},{13,5},{2,10},{6,14},... | collective-permute-start | bytes 294920 | tf_op jit(solution)/shard_map/ppermute | solution.py:212
  130.9 2.3 %collective-permute-start.5 = (bf16[3,32,512]{2,1,0:T(8,128)(2,1)S(1)}, bf16[3,32,512]{2,1,0:T(8,128)(2,1)S(1)}, u32[]{:S(2)}, u32[]{:S(2)}) collective-permute-start(bf16[3,32,512]{2,1,0:T(8,128)(2,1)S(1)} %reduce_sum.25), channel_id=1, source_target_pairs={{0,4},{4,8},{8,12},{12,0},{1,5},{5,9},{9,13},{13,1},{2,6},{6,10},{... | collective-permute-start | bytes 294920 | tf_op jit(solution)/shard_map/ppermute | solution.py:212
  133.1 4.5 %collective-permute-done.5 = bf16[3,32,512]{2,1,0:T(8,128)(2,1)S(1)} collective-permute-done((bf16[3,32,512]{2,1,0:T(8,128)(2,1)S(1)}, bf16[3,32,512]{2,1,0:T(8,128)(2,1)S(1)}, u32[]{:S(2)}, u32[]{:S(2)}) %collective-permute-start.5) | collective-permute-done | bytes 98336 | tf_op jit(solution)/shard_map/ppermute | solution.py:212
  137.7 1.3 broadcast_in_dim.9
  139.1 4.1 %all-to-all-start.3 = ((bf16[16,3,32,512]{3,2,1,0:T(8,128)(2,1)}), bf16[16,3,32,512]{3,2,1,0:T(8,128)(2,1)S(1)}, u32[]{:S(2)}, u32[]{:S(2)}) async-start(bf16[16,3,32,512]{3,2,1,0:T(8,128)(2,1)} %broadcast_in_dim.9), calls=%async_computation.3 | async-start | bytes 3145728 | tf_op jit(solution)/shard_map/all_to_all | solution.py:220
  145.3 3.8 %shard_map.133.attended_ref = f32[512,512]{1,0:T(8,128)S(1)} custom-call(s32[1]{0:T(128)} %bitcast.seq_ref, s32[16]{0:T(128)S(1)} %copy-done.1, bf16[512,512]{1,0:T(8,128)(2,1)S(1)} %bitcast.22, bf16[512,512]{1,0:T(8,128)(2,1)S(1)} %copy-done.14, bf16[512,512]{1,0:T(8,128)(2,1)S(1)} %bitcast.19, bf16[512,512]{1,0:T(8,128)(2,1)S(1)} %copy-done.16, ...), custom_call_target="tpu_custom_call" | custom-call | flops 1073741824 | bytes 3670016 | tf_op jit(solution)/shard_map/pallas_call | solution.py:178
  150.1 11.5 %all-to-all-done.3.gathered_ref = bf16[16,3,32,512]{3,2,1,0:T(8,128)(2,1)S(1)} async-done(((bf16[16,3,32,512]{3,2,1,0:T(8,128)(2,1)}), bf16[16,3,32,512]{3,2,1,0:T(8,128)(2,1)S(1)}, u32[]{:S(2)}, u32[]{:S(2)}) %all-to-all-start.3) | async-done | bytes 1572896 | tf_op jit(solution)/shard_map/all_to_all | solution.py:220
  161.6 1.4 copy-done.4
  163.0 1.2 copy-done.21
  164.2 1.4 copy-done.23
  165.7 10.5 %shard_map.134 = (bf16[3,512,512]{2,1,0:T(8,128)(2,1)}, f32[512,512]{1,0:T(8,128)S(1)}, f32[1,512]{1,0:T(1,128)S(1)}) custom-call(s32[1]{0:T(128)} %bitcast.seq_ref, s32[1]{0:T(128)S(6)} %copy.15.split_ref, s32[16]{0:T(128)S(1)} %copy-done.19, f32[1]{0:T(128)S(6)} %copy.16.step_ref, bf16[16,3,32,512]{3,2,1,0:T(8,128)(2,1)S(1)} %all-to-all-done.3.gathered_ref, ...), custom_call_target="tpu_custom_call" | custom-call | flops 5637144576 | bytes 8914944 | tf_op jit(solution)/shard_map/pallas_call | solution.py:178
  176.1 21.3 %psum.7.energy_ref = f32[1,512]{1,0:T(1,128)S(1)} all-reduce(f32[1,512]{1,0:T(1,128)S(1)} %get-tuple-element.22), channel_id=1, replica_groups=mesh['x'=4,'y'=4,'z'=4,'w'=2,'c'=2] {'w','c'}, use_global_device_ids=true, to_apply=%region_2.0 | all-reduce | flops 512 | bytes 4096 | tf_op jit(solution)/shard_map/psum | solution.py:288
  197.4 1.5 shard_map.135
  (51 shorter events, 8.5 us)
Async XLA Ops:
  1.3 1.4 copy-start.2
  2.7 1.0 copy-start.5
  3.7 1.0 copy-start.7
  8.8 7.7 %copy-start.9 = (bf16[1,512,512]{2,1,0:T(8,128)(2,1)S(1)}, bf16[1,512,512]{2,1,0:T(8,128)(2,1)}, u32[]{:S(2)}) copy-start(bf16[1,512,512]{2,1,0:T(8,128)(2,1)} %param.19) | copy-start | bytes 1572868
  8.8 28.3 %all-to-all-start = ((bf16[16,3,32,512]{3,2,1,0:T(8,128)(2,1)}), bf16[16,3,32,512]{3,2,1,0:T(8,128)(2,1)S(1)}, u32[]{:S(2)}, u32[]{:S(2)}) async-start(bf16[16,3,32,512]{3,2,1,0:T(8,128)(2,1)} %shard_map.131), calls=%async_computation | async-start | bytes 3145728 | tf_op jit(solution)/shard_map/all_to_all | solution.py:204
  16.5 20.9 %collective-permute-start = (bf16[512,512]{1,0:T(8,128)(2,1)S(1)}, bf16[512,512]{1,0:T(8,128)(2,1)S(1)}, u32[]{:S(2)}, u32[]{:S(2)}) collective-permute-start(bf16[512,512]{1,0:T(8,128)(2,1)S(1)} %bitcast.18), channel_id=1, source_target_pairs={{0,4},{4,8},{8,12},{1,5},{5,9},{9,13},{2,6},{6,10},{10,14},{3,7},{... | collective-permute-start | bytes 1572872 | tf_op jit(solution)/shard_map/ppermute | solution.py:200
  38.2 16.1 %collective-permute-start.3 = (bf16[3,32,512]{2,1,0:T(8,128)(2,1)S(1)}, bf16[3,32,512]{2,1,0:T(8,128)(2,1)S(1)}, u32[]{:S(2)}, u32[]{:S(2)}) collective-permute-start(bf16[3,32,512]{2,1,0:T(8,128)(2,1)S(1)} %reduce_sum.24), channel_id=1, source_target_pairs={{0,12},{4,0},{8,4},{12,8},{1,13},{5,1},{9,5},{13,9},{2,14},{6,2},{... | collective-permute-start | bytes 294920 | tf_op jit(solution)/shard_map/ppermute | solution.py:212
  44.2 10.1 %collective-permute-start.2 = (bf16[3,32,512]{2,1,0:T(8,128)(2,1)S(1)}, bf16[3,32,512]{2,1,0:T(8,128)(2,1)S(1)}, u32[]{:S(2)}, u32[]{:S(2)}) collective-permute-start(bf16[3,32,512]{2,1,0:T(8,128)(2,1)S(1)} %reduce_sum.24), channel_id=1, source_target_pairs={{0,8},{4,12},{8,0},{12,4},{1,9},{5,13},{9,1},{13,5},{2,10},{6,14},... | collective-permute-start | bytes 294920 | tf_op jit(solution)/shard_map/ppermute | solution.py:212
  51.9 8.4 %collective-permute-start.1 = (bf16[3,32,512]{2,1,0:T(8,128)(2,1)S(1)}, bf16[3,32,512]{2,1,0:T(8,128)(2,1)S(1)}, u32[]{:S(2)}, u32[]{:S(2)}) collective-permute-start(bf16[3,32,512]{2,1,0:T(8,128)(2,1)S(1)} %reduce_sum.24), channel_id=1, source_target_pairs={{0,4},{4,8},{8,12},{12,0},{1,5},{5,9},{9,13},{13,1},{2,6},{6,10},{... | collective-permute-start | bytes 294920 | tf_op jit(solution)/shard_map/ppermute | solution.py:212
  61.7 26.3 %copy-start.3 = (bf16[3,1,512,512]{3,2,1,0:T(8,128)(2,1)S(1)}, bf16[3,1,512,512]{3,2,1,0:T(8,128)(2,1)}, u32[]{:S(2)}) copy-start(bf16[3,1,512,512]{3,2,1,0:T(8,128)(2,1)} %param.16) | copy-start | bytes 4718596
  61.7 26.3 %copy-start.18 = (f32[1,512]{1,0:T(1,128)S(1)}, f32[1,512]{1,0:T(1,128)}, u32[]{:S(2)}) copy-start(f32[1,512]{1,0:T(1,128)} %rates_ref.3) | copy-start | bytes 6148
  61.7 26.3 %all-to-all-start.1 = ((bf16[16,3,32,512]{3,2,1,0:T(8,128)(2,1)}), bf16[16,3,32,512]{3,2,1,0:T(8,128)(2,1)S(1)}, u32[]{:S(2)}, u32[]{:S(2)}) async-start(bf16[16,3,32,512]{3,2,1,0:T(8,128)(2,1)} %broadcast_in_dim.8), calls=%async_computation.1 | async-start | bytes 3145728 | tf_op jit(solution)/shard_map/all_to_all | solution.py:220
  68.0 13.2 %collective-permute-start.4 = (bf16[512,512]{1,0:T(8,128)(2,1)}, bf16[512,512]{1,0:T(8,128)(2,1)S(1)}, u32[]{:S(2)}, u32[]{:S(2)}) collective-permute-start(bf16[512,512]{1,0:T(8,128)(2,1)} %bitcast.20), channel_id=1, source_target_pairs={{0,4},{4,8},{8,12},{1,5},{5,9},{9,13},{2,6},{6,10},{10,14},{3,7},{... | collective-permute-start | bytes 1572872 | tf_op jit(solution)/shard_map/ppermute | solution.py:200
  88.0 1.0 copy-start.6
  89.0 1.0 copy-start.8
  99.4 1.2 copy-start.22
  123.9 9.2 %collective-permute-start.7 = (bf16[3,32,512]{2,1,0:T(8,128)(2,1)S(1)}, bf16[3,32,512]{2,1,0:T(8,128)(2,1)S(1)}, u32[]{:S(2)}, u32[]{:S(2)}) collective-permute-start(bf16[3,32,512]{2,1,0:T(8,128)(2,1)S(1)} %reduce_sum.25), channel_id=1, source_target_pairs={{0,12},{4,0},{8,4},{12,8},{1,13},{5,1},{9,5},{13,9},{2,14},{6,2},{... | collective-permute-start | bytes 294920 | tf_op jit(solution)/shard_map/ppermute | solution.py:212
  124.3 8.8 %collective-permute-start.6 = (bf16[3,32,512]{2,1,0:T(8,128)(2,1)S(1)}, bf16[3,32,512]{2,1,0:T(8,128)(2,1)S(1)}, u32[]{:S(2)}, u32[]{:S(2)}) collective-permute-start(bf16[3,32,512]{2,1,0:T(8,128)(2,1)S(1)} %reduce_sum.25), channel_id=1, source_target_pairs={{0,8},{4,12},{8,0},{12,4},{1,9},{5,13},{9,1},{13,5},{2,10},{6,14},... | collective-permute-start | bytes 294920 | tf_op jit(solution)/shard_map/ppermute | solution.py:212
  130.9 6.8 %collective-permute-start.5 = (bf16[3,32,512]{2,1,0:T(8,128)(2,1)S(1)}, bf16[3,32,512]{2,1,0:T(8,128)(2,1)S(1)}, u32[]{:S(2)}, u32[]{:S(2)}) collective-permute-start(bf16[3,32,512]{2,1,0:T(8,128)(2,1)S(1)} %reduce_sum.25), channel_id=1, source_target_pairs={{0,4},{4,8},{8,12},{12,0},{1,5},{5,9},{9,13},{13,1},{2,6},{6,10},{... | collective-permute-start | bytes 294920 | tf_op jit(solution)/shard_map/ppermute | solution.py:212
  139.1 4.1 %copy-start.1 = (s32[16]{0:T(128)S(1)}, s32[16]{0:T(128)}, u32[]{:S(2)}) copy-start(s32[16]{0:T(128)} %length_ref.3) | copy-start | bytes 196
  139.1 4.1 %copy-start.10 = (bf16[1,512,512]{2,1,0:T(8,128)(2,1)S(1)}, bf16[1,512,512]{2,1,0:T(8,128)(2,1)}, u32[]{:S(2)}) copy-start(bf16[1,512,512]{2,1,0:T(8,128)(2,1)} %param.19) | copy-start | bytes 1572868
  139.1 4.1 %copy-start.11 = (bf16[1,512,512]{2,1,0:T(8,128)(2,1)S(1)}, bf16[1,512,512]{2,1,0:T(8,128)(2,1)}, u32[]{:S(2)}) copy-start(bf16[1,512,512]{2,1,0:T(8,128)(2,1)} %param.20) | copy-start | bytes 1572868
  139.1 4.1 %copy-start.12 = (bf16[1,512,512]{2,1,0:T(8,128)(2,1)S(1)}, bf16[1,512,512]{2,1,0:T(8,128)(2,1)}, u32[]{:S(2)}) copy-start(bf16[1,512,512]{2,1,0:T(8,128)(2,1)} %param.18) | copy-start | bytes 1572868
  139.1 22.5 %all-to-all-start.3 = ((bf16[16,3,32,512]{3,2,1,0:T(8,128)(2,1)}), bf16[16,3,32,512]{3,2,1,0:T(8,128)(2,1)S(1)}, u32[]{:S(2)}, u32[]{:S(2)}) async-start(bf16[16,3,32,512]{3,2,1,0:T(8,128)(2,1)} %broadcast_in_dim.9), calls=%async_computation.3 | async-start | bytes 3145728 | tf_op jit(solution)/shard_map/all_to_all | solution.py:220
  143.2 1.0 copy-start.14
  144.2 1.0 copy-start.16
  145.3 16.3 %copy-start.19 = (s32[16]{0:T(128)S(1)}, s32[16]{0:T(128)}, u32[]{:S(2)}) copy-start(s32[16]{0:T(128)} %fork_ref.1) | copy-start | bytes 196
  149.1 1.0 copy-start.20
  161.6 1.4 copy-start.4
  163.0 1.2 copy-start.21
  164.2 1.4 copy-start.23
  165.6 31.8 %copy-start = (f32[1,512]{1,0:T(1,128)S(1)}, f32[1,512]{1,0:T(1,128)}, u32[]{:S(2)}) copy-start(f32[1,512]{1,0:T(1,128)} %gain_ref.1) | copy-start | bytes 6148
  (3 other events, 2.3 us)

commit v3 on v2

v3 whole, which is shorter than its diff:
```python
import functools
import jax
import jax.numpy as jnp
from jax import lax
from jax.experimental import pallas as pl
from jax.experimental.pallas import tpu as pltpu
from jax.sharding import Mesh
from jax.sharding import PartitionSpec as P

PLANE = ("x", "y")
SEQ = ("x", "y", "z")
HEAD = ("w", "c")
NS_STEPS = 2
BR_SPAN = 4

poly_one = 3.4445
poly_two = -4.775
poly_three = 2.0315
VMEM_BYTES = 24 * 1024 * 1024
WHOLE_VMEM = 60 * 1024 * 1024
CHUNK = 256
UPDATE_CHUNK = 512


def nt(left, right):
    return lax.dot_general(left, right, (((1,), (1,)), ((), ())), preferred_element_type=jnp.float32)


def nn(left, right):
    return jnp.dot(left, right, preferred_element_type=jnp.float32)


def column_of(row):
    return jnp.transpose(jnp.broadcast_to(row, (128, row.shape[1])))


def emit_gradient(weights, keys_ref, values_ref, rates, parts_ref, parts_hbm, sems, ready=lambda name: None):
    step = parts_ref.shape[2]
    sent = []
    rows, width = weights[0].shape
    rate_columns = jnp.tile(column_of(rates), (1, width // 128))
    ready("keys")
    keys = keys_ref[...]
    pushed = None
    for start in range(0, rows, CHUNK):
        cut = slice(start, start + CHUNK)
        if start == 0:
            ready("first")
        first = nt(weights[0][cut], keys)
        if start == 0:
            ready("third")
        third = nt(weights[1][cut], keys)
        gate = jax.nn.sigmoid(first)
        silu = first * gate
        hidden = (silu * third).astype(jnp.bfloat16)
        if start == 0:
            ready("values")
            pushed = (rate_columns * values_ref[...].astype(jnp.float32)).astype(jnp.bfloat16)
            ready("second")
        returned = nt(weights[2][cut], pushed)
        delta_first = (returned * third * gate * (1.0 + first * (1.0 - gate))).astype(jnp.bfloat16)
        delta_third = (returned * silu).astype(jnp.bfloat16)
        for kind, grad in enumerate((nn(delta_first, keys), nn(delta_third, keys), nn(hidden, pushed))):
            grad = grad.astype(jnp.bfloat16)
            for part in range(CHUNK // step):
                parts_ref[start // step + part, kind] = grad[part * step : (part + 1) * step]
            slots = pl.ds(start // step, CHUNK // step)
            copy = pltpu.make_async_copy(
                parts_ref.at[slots, kind], parts_hbm.at[slots, kind], sems.at[len(sent)]
            )
            copy.start()
            sent.append(copy)
    for copy in sent:
        copy.wait()


def fetch_gathered(gathered_hbm, gathered_ref, sems):
    copies = [
        pltpu.make_async_copy(gathered_hbm.at[:, kind], gathered_ref.at[kind], sems.at[kind])
        for kind in range(gathered_ref.shape[0])
    ]
    for copy in copies:
        copy.start()
    return copies


def emit_update(fetches, gathered_ref, old_ref, step_size, x_ref, gram_ref, out_ref, begin, ready):
    kinds, planes, step, width = gathered_ref.shape
    rows = planes * step
    for kind in range(kinds):
        fetches[kind].wait()
        wide = gathered_ref[kind].reshape(rows, width).astype(jnp.float32)
        square = jnp.sum(jnp.sum(wide * wide, axis=0, keepdims=True), axis=1, keepdims=True)
        inverse = 1.0 / (jnp.sqrt(square) + 1e-07)
        x_ref[0, kind] = (wide * inverse).astype(jnp.bfloat16)
    begin()
    for sweep in range(NS_STEPS):
        now, later = sweep % 2, (sweep + 1) % 2
        if sweep == NS_STEPS - 1:
            ready()
        for kind in range(kinds):
            full = x_ref[now, kind]
            gram_ref[kind] = nt(full, full).astype(jnp.bfloat16)
        for kind in range(kinds):
            full = x_ref[now, kind]
            gram = gram_ref[kind]
            for start in range(0, rows, UPDATE_CHUNK):
                cut = slice(start, start + UPDATE_CHUNK)
                own = gram[cut]
                poly = (poly_two * own.astype(jnp.float32) + poly_three * nn(own, gram)).astype(jnp.bfloat16)
                moved = (poly_one * full[cut].astype(jnp.float32) + nn(poly, full)).astype(jnp.bfloat16)
                if sweep < NS_STEPS - 1:
                    x_ref[later, kind, cut] = moved
                else:
                    old = old_ref[kind, cut].astype(jnp.float32)
                    new = old + step_size * moved.astype(jnp.float32)
                    old_mean = jnp.mean(old * old, axis=-1, keepdims=True) + 1e-06
                    new_mean = jnp.mean(new * new, axis=-1, keepdims=True) + 1e-06
                    out_ref[kind, cut] = (new * (jnp.sqrt(old_mean) * lax.rsqrt(new_mean))).astype(jnp.bfloat16)


def masked_rates(rates_ref, seq_ref, split_ref, period):
    rates = rates_ref[...]
    count = rates.shape[1]
    positions = seq_ref[0] * count + lax.broadcasted_iota(jnp.int32, rates.shape, 1)
    early = positions < split_ref[0]
    return jnp.where(early if period == 0 else jnp.logical_not(early), rates, 0.0)


def first_kernel(
    seq_ref,
    split_ref,
    rates_ref,
    weights_hbm,
    keys_hbm,
    values_hbm,
    parts_hbm,
    weights,
    keys,
    values,
    parts,
    sems,
    parts_sems,
):
    copies = {
        "keys": pltpu.make_async_copy(keys_hbm, keys, sems.at[0]),
        "first": pltpu.make_async_copy(weights_hbm.at[0], weights.at[0], sems.at[1]),
        "third": pltpu.make_async_copy(weights_hbm.at[1], weights.at[1], sems.at[2]),
        "values": pltpu.make_async_copy(values_hbm, values, sems.at[3]),
        "second": pltpu.make_async_copy(weights_hbm.at[2], weights.at[2], sems.at[4]),
    }
    for copy in copies.values():
        copy.start()
    rates = masked_rates(rates_ref, seq_ref, split_ref, 0)
    kinds = [weights.at[kind] for kind in range(3)]
    emit_gradient(kinds, keys, values, rates, parts, parts_hbm, parts_sems, lambda name: copies[name].wait())


def second_kernel(
    seq_ref,
    split_ref,
    step_ref,
    rates_ref,
    gathered_hbm,
    weights_hbm,
    keys_hbm,
    values_hbm,
    parts_hbm,
    state_hbm,
    weights,
    keys,
    values,
    x_ref,
    gram_ref,
    state,
    gathered,
    parts,
    sems,
    gathered_sems,
    parts_sems,
):
    fetches = fetch_gathered(gathered_hbm, gathered, gathered_sems)
    fetch_weights = pltpu.make_async_copy(weights_hbm, weights, sems.at[0])
    fetch_keys = pltpu.make_async_copy(keys_hbm, keys, sems.at[1])
    fetch_values = pltpu.make_async_copy(values_hbm, values, sems.at[2])

    def begin():
        fetch_weights.start()
        fetch_keys.start()
        fetch_values.start()

    emit_update(fetches, gathered, weights, step_ref[0], x_ref, gram_ref, state, begin, fetch_weights.wait)
    keep = pltpu.make_async_copy(state, state_hbm, sems.at[3])
    keep.start()
    rates = masked_rates(rates_ref, seq_ref, split_ref, 1)
    fetch_keys.wait()
    fetch_values.wait()
    emit_gradient([state.at[kind] for kind in range(3)], keys, values, rates, parts, parts_hbm, parts_sems)
    keep.wait()


def attend_kernel(
    seq_ref, length_ref, query_ref, keys_ref, values_ref, keys_a_ref, keys_b_ref, values_b_ref, values_c_ref, out_ref
):
    rows, width = query_ref.shape
    branch = seq_ref[0] // BR_SPAN
    place = seq_ref[0] % BR_SPAN
    live = length_ref[branch] - place * rows
    scale = width ** (-0.5)
    prior_keys = jnp.concatenate([keys_a_ref[...], keys_b_ref[...]], axis=0)
    prior_values = jnp.concatenate([values_b_ref[...], values_c_ref[...]], axis=0)
    chunk = 128
    for start in range(0, rows, chunk):
        cut = slice(start, start + chunk)
        query = query_ref[cut]
        row = start + lax.broadcasted_iota(jnp.int32, (chunk, rows), 0)
        slot = lax.broadcasted_iota(jnp.int32, (chunk, rows), 1)
        behind = slot > row
        allowed = (slot == row) | (slot < jnp.where(behind, jnp.where(place > 0, rows, 0), live))
        scores = jnp.where(behind, nt(query, prior_keys), nt(query, keys_ref[...])) * scale
        scores = jnp.where(allowed, scores, -1e30)
        top = jnp.max(scores, axis=-1, keepdims=True)
        power = jnp.exp(scores - top)
        share = power * (1.0 / jnp.sum(power, axis=-1, keepdims=True))
        out_ref[cut] = nn(jnp.where(behind, share, 0.0).astype(jnp.bfloat16), prior_values) + nn(
            jnp.where(behind, 0.0, share).astype(jnp.bfloat16), values_ref[...]
        )


def third_kernel(
    seq_ref,
    split_ref,
    fork_ref,
    step_ref,
    gathered_hbm,
    weights_hbm,
    state_hbm,
    query_hbm,
    attended_hbm,
    total_ref,
    energy_ref,
    last_hbm,
    old,
    query,
    attended,
    x_ref,
    gram_ref,
    pool,
    gathered,
    sems,
    gathered_sems,
    trunk_total,
):
    fetches = fetch_gathered(gathered_hbm, gathered, gathered_sems)
    fork = fork_ref[seq_ref[0] // BR_SPAN]
    early = fork < split_ref[0]
    final = jnp.logical_and(jnp.logical_not(early), fork >= trunk_total)
    fetch_old = pltpu.make_async_copy(state_hbm, old, sems.at[0])
    fetch_query = pltpu.make_async_copy(query_hbm, query, sems.at[1])
    fetch_attended = pltpu.make_async_copy(attended_hbm, attended, sems.at[2])
    fetch_first = pltpu.make_async_copy(weights_hbm, pool.at[1], sems.at[3])
    fetch_state = pltpu.make_async_copy(state_hbm, pool.at[1], sems.at[3])

    def begin():
        fetch_old.start()
        fetch_query.start()
        fetch_attended.start()

        @pl.when(early)
        def _():
            fetch_first.start()

        @pl.when(jnp.logical_not(early))
        def _():
            fetch_state.start()

    emit_update(fetches, gathered, old, step_ref[0], x_ref, gram_ref, pool.at[0], begin, fetch_old.wait)
    keep = pltpu.make_async_copy(pool.at[0], last_hbm, sems.at[4])
    keep.start()
    fetch_query.wait()
    fetch_attended.wait()
    fetch_state.wait()
    pick = jnp.where(final, 0, 1)
    rows = query.shape[0]
    for start in range(0, rows, UPDATE_CHUNK):
        cut = slice(start, start + UPDATE_CHUNK)
        first = nt(query[cut], pool[pick, 0])
        third = nt(query[cut], pool[pick, 1])
        hidden = (first * jax.nn.sigmoid(first) * third).astype(jnp.bfloat16)
        total = attended[cut] + nn(hidden, pool[pick, 2])
        total_ref[cut] = total
        energy = jnp.sum(total * total, axis=-1, keepdims=True)
        energy_ref[:, cut] = jnp.transpose(jnp.broadcast_to(energy, (UPDATE_CHUNK, 128)))[0:1]
    keep.wait()


def last_kernel(seq_ref, length_ref, total_ref, energy_ref, gain_ref, out_ref, width):
    rows = total_ref.shape[0]
    live = length_ref[seq_ref[0] // BR_SPAN] - (seq_ref[0] % BR_SPAN) * rows
    slot = lax.broadcasted_iota(jnp.int32, (1, rows), 1)
    inverse = jnp.where(slot < live, lax.rsqrt(energy_ref[...] / width + 1e-06), 0.0)
    columns = jnp.tile(column_of(inverse), (1, total_ref.shape[1] // 128))
    out_ref[...] = (total_ref[...] * columns * gain_ref[...]).astype(jnp.bfloat16)


def replicate_kernel(*refs):
    total = refs[0][...].astype(jnp.float32)
    for ref in refs[1:-1]:
        total = total + ref[...].astype(jnp.float32)
    total = total.astype(jnp.bfloat16)
    for slot in range(refs[-1].shape[0]):
        refs[-1][slot] = total


SMEM = pl.BlockSpec(memory_space=pltpu.SMEM)
VMEM = pl.BlockSpec(memory_space=pltpu.VMEM)
HBM = pl.BlockSpec(memory_space=pltpu.HBM)


def call(kernel, scalars, arrays, outs, held=(), held_outs=(), scratch=(), flops=0, vmem=VMEM_BYTES):
    moved = sum(array.size * array.dtype.itemsize for array in (*arrays, *held, *outs, *held_outs))
    return pl.pallas_call(
        kernel,
        out_shape=(*outs, *held_outs),
        in_specs=[SMEM] * len(scalars) + [VMEM] * len(arrays) + [HBM] * len(held),
        out_specs=[VMEM] * len(outs) + [HBM] * len(held_outs),
        scratch_shapes=list(scratch),
        compiler_params=pltpu.CompilerParams(vmem_limit_bytes=vmem),
        cost_estimate=pl.CostEstimate(flops=flops, bytes_accessed=moved, transcendentals=0),
    )(*scalars, *arrays, *held)


def shape(dims, kind):
    return jax.ShapeDtypeStruct(dims, kind)


def space(dims, kind=jnp.bfloat16):
    return pltpu.VMEM(dims, kind)


def gradient_first(seq, split, rates, weights, keys, values, parts_shape):
    scratch = (
        space(weights.shape),
        space(keys.shape),
        space(values.shape),
        space(parts_shape.shape),
        pltpu.SemaphoreType.DMA((5,)),
        pltpu.SemaphoreType.DMA((3 * keys.shape[0] // CHUNK,)),
    )
    (parts,) = call(
        first_kernel,
        (seq, split),
        (rates,),
        (),
        (weights, keys, values),
        (parts_shape,),
        scratch,
        flops=12 * keys.size * weights.shape[1],
        vmem=WHOLE_VMEM,
    )
    return parts


def by_kind(gathered):
    planes, kinds, step, width = gathered.shape
    return space((kinds, planes, step, width))


def update_and_gradient(seq, split, step, gathered, rates, weights, keys, values):
    full = weights.shape
    scratch = (
        space(full),
        space(keys.shape),
        space(values.shape),
        space((2, *full)),
        space(full),
        space(full),
        by_kind(gathered),
        space(gathered.shape),
        pltpu.SemaphoreType.DMA((4,)),
        pltpu.SemaphoreType.DMA((3,)),
        pltpu.SemaphoreType.DMA((3 * full[1] // CHUNK,)),
    )
    return call(
        second_kernel,
        (seq, split, step),
        (rates,),
        (),
        (gathered, weights, keys, values),
        (shape(gathered.shape, jnp.bfloat16), shape(full, jnp.bfloat16)),
        scratch,
        flops=48 * keys.size * full[1],
        vmem=WHOLE_VMEM,
    )


def update_and_apply(seq, split, forks, step, gathered, weights, state, query, attended, trunk_total):
    full = weights.shape
    rows, width = query.shape
    scratch = (
        space(full),
        space(query.shape),
        space(query.shape, jnp.float32),
        space((2, *full)),
        space(full),
        space((2, *full)),
        by_kind(gathered),
        pltpu.SemaphoreType.DMA((5,)),
        pltpu.SemaphoreType.DMA((3,)),
    )
    return call(
        functools.partial(third_kernel, trunk_total=trunk_total),
        (seq, split, forks, step),
        (),
        (shape((rows, width), jnp.float32), shape((1, rows), jnp.float32)),
        (gathered, weights, state, query, attended),
        (shape(full, jnp.bfloat16),),
        scratch,
        flops=42 * query.size * full[1],
        vmem=WHOLE_VMEM,
    )


def from_behind(value):
    count = lax.axis_size("z")
    return lax.ppermute(value, "z", [(source, source + 1) for source in range(count - 1)])


def sum_plane(parts):
    received = lax.all_to_all(parts, PLANE, 0, 0, tiled=False)
    return jnp.sum(received.astype(jnp.float32), axis=0).astype(jnp.bfloat16)


def sum_depth(mine):
    depth, planes = lax.axis_size("z"), lax.axis_size(PLANE)
    others = [
        lax.ppermute(mine, "z", [(i, (i + step) % depth) for i in range(depth)]) for step in range(1, depth)
    ]
    (copies,) = call(replicate_kernel, (), (mine, *others), (shape((planes, *mine.shape), mine.dtype),))
    return copies


def spread_plane(copies):
    return lax.all_to_all(copies, PLANE, 0, 0, tiled=False)


def per_device(
    trunk_keys,
    trunk_values,
    trunk_rates,
    segment_end,
    fast_weights,
    step_sizes,
    branch_query,
    branch_keys,
    branch_values,
    branch_lengths,
    fork_points,
    out_gain,
):
    keys, values = trunk_keys[0], trunk_values[0]
    weights = fast_weights[:, 0]
    query, own_keys, own_values = branch_query[0], branch_keys[0], branch_values[0]
    rows, width = keys.shape
    hidden = weights.shape[1]
    planes = lax.axis_size(PLANE)
    trunk_total = rows * lax.axis_size(SEQ)
    total_width = width * lax.axis_size(HEAD)
    seq = lax.axis_index(SEQ).astype(jnp.int32).reshape(1)
    parts_shape = shape((planes, 3, hidden // planes, width), jnp.bfloat16)
    most = 3 * rows // 4
    barrier = lax.optimization_barrier

    keys_a = from_behind(own_keys[:most])
    parts = gradient_first(seq, segment_end, trunk_rates, weights, keys, values, parts_shape)
    mine, keys_a = barrier((sum_plane(parts), keys_a))
    copies, rest_keys, rest_values = barrier((sum_depth(mine), own_keys[most:], own_values[: rows - most]))
    gathered, keys_b, values_b = barrier((spread_plane(copies), from_behind(rest_keys), from_behind(rest_values)))
    parts, state = update_and_gradient(
        seq, segment_end, step_sizes, gathered, trunk_rates, weights, keys, values
    )
    parts, rest_values = barrier((parts, own_values[rows - most :]))
    mine, values_c = barrier((sum_plane(parts), from_behind(rest_values)))
    copies = sum_depth(mine)
    (attended,) = call(
        attend_kernel,
        (seq, branch_lengths),
        (query, own_keys, own_values, keys_a, keys_b, values_b, values_c),
        (shape((rows, width), jnp.float32),),
        flops=8 * rows * rows * width,
    )
    gathered = spread_plane(copies)
    total, energy, last = update_and_apply(
        seq, segment_end, fork_points, step_sizes, gathered, weights, state, query, attended, trunk_total
    )
    energy = lax.psum(energy, HEAD)
    (result,) = call(
        functools.partial(last_kernel, width=total_width),
        (seq, branch_lengths),
        (total, energy, out_gain),
        (shape((rows, width), jnp.bfloat16),),
    )
    return (result[None], last[:, None])


def solution(mesh):
    fine = Mesh(mesh.devices.reshape(4, 4, 4, 2, 2), (*SEQ, *HEAD))
    rows = P(HEAD, SEQ, None)
    placed = (
        rows,
        rows,
        P(HEAD, SEQ),
        P(),
        P(None, HEAD, None, None),
        P(HEAD),
        rows,
        rows,
        rows,
        P(),
        P(),
        P(HEAD, None),
    )
    return jax.shard_map(
        per_device,
        mesh=fine,
        in_specs=placed,
        out_specs=(rows, P(None, HEAD, None, None)),
        check_vma=False,
    )
```

time: 200 us -> 184 us (0.920)
  blocking collectives: 44.3 us -> 12.6 us
  local copies, waits for them, and re-layouts: 18.8 us -> 2.97 us
  waiting for transfers between devices: 51.9 us -> 64.8 us
  starting transfers between devices: 52.7 us -> 62.9 us
  Pallas kernels: 28.5 us -> 35.8 us
    all_to_all x1 -> x0, blocking collectives: 23 us -> none  [sum_plane(): received = lax.all_to_all(parts, PLANE, 0, 0, tiled=False)]
    all_to_all x1 -> x2, waiting for transfers between devices: 15.7 us -> 30.5 us  [sum_plane(): received = lax.all_to_all(parts, PLANE, 0, 0, tiled=False)]
    unnamed x48 -> x16, local copies, waits for them, and re-layouts: 16.2 us -> 2.24 us
    psum x1, blocking collectives: 21.3 us -> 12.6 us  [per_device(): energy = lax.psum(energy, HEAD)]
    ppermute x2 -> x4, starting transfers between devices: 9.26 us -> 17.2 us  [from_behind(): lax.ppermute(value, 'z', [(source, source + 1) for source in range(count...]
    ppermute x6, starting transfers between devices: 25.3 us -> 17.6 us  [sum_depth(): lax.ppermute(mine, 'z', [(i, (i + step) % depth) for i in range(depth)])]
    pallas_call x5 -> x7, Pallas kernels: 28.5 us -> 35.8 us  [call(): pl.pallas_call(kernel, out_shape=(*outs, *held_outs), in_specs=[SMEM] * l...]
    ppermute x2 -> x4, waiting for transfers between devices: 8.21 us -> 1.71 us  [from_behind(): lax.ppermute(value, 'z', [(source, source + 1) for source in range(count...]
  transfers between devices with their start and end apart: 11 -> 14, of which waited for: 6 -> 9; matrix products, arithmetic and copies ran while one was open for 0% -> 1% of each run, Pallas kernels for 2% -> 2%
where the time goes in v3:
time: 184 us; the launch traced here: 183 us
  waiting for transfers between devices  64.8 us (35%)
  starting transfers between devices  62.9 us (34%)
  Pallas kernels  35.8 us (19%)
  blocking collectives  12.6 us (7%)
  local copies, waits for them, and re-layouts  2.97 us (2%)
  between operations  2.16 us (1%)
  other arithmetic  1.93 us (1%)
    pallas_call x7, Pallas kernels, call(): pl.pallas_call(kernel, out_shape=(*outs, *held_outs), in_specs=[SMEM] * l...  35.8 us
    all_to_all x2, waiting for transfers between devices, sum_plane(): received = lax.all_to_all(parts, PLANE, 0, 0, tiled=False)  30.5 us
    all_to_all x2, waiting for transfers between devices, spread_plane(): return lax.all_to_all(copies, PLANE, 0, 0, tiled=False)  23.3 us
    ppermute x6, starting transfers between devices, sum_depth(): lax.ppermute(mine, 'z', [(i, (i + step) % depth) for i in range(depth)])  17.6 us
    ppermute x4, starting transfers between devices, from_behind(): lax.ppermute(value, 'z', [(source, source + 1) for source in range(count...  17.2 us
    all_to_all x2, starting transfers between devices, spread_plane(): return lax.all_to_all(copies, PLANE, 0, 0, tiled=False)  15.2 us
    all_to_all x2, starting transfers between devices, sum_plane(): received = lax.all_to_all(parts, PLANE, 0, 0, tiled=False)  13 us
    psum x1, blocking collectives, per_device(): energy = lax.psum(energy, HEAD)  12.6 us
  transfers between devices with their start and end apart: 14, of which 9 were waited for; matrix products, arithmetic and copies ran while one was open for 1% of the time, Pallas kernels for 2%

profile of v3, /device:TPU:1, one launch (start us, length us, event | category | flops | bytes accessed | tf_op | source)
XLA Modules:
  0.0 183.2 jit_solution(14597991015428527285)
XLA Ops:
  1.3 5.4 %shard_map.131 = bf16[16,3,32,512]{3,2,1,0:T(8,128)(2,1)} custom-call(s32[1]{0:T(128)} %bitcast.seq_ref, s32[1]{0:T(128)S(6)} %copy.15.split_ref, f32[1,512]{1,0:T(1,128)} %rates_ref.3, bf16[3,512,512]{2,1,0:T(8,128)(2,1)} %bitcast.24, bf16[512,512]{1,0:T(8,128)(2,1)} %bitcast.27, bf16[512,512]{1,0:T(8,128)(2,1)} %bitcast.29), custom_call_target="tpu_custom_call" | custom-call | flops 1610612736 | bytes 4196352 | tf_op jit(solution)/shard_map/pallas_call | solution.py:322
  6.7 7.7 %all-to-all-start = ((bf16[16,3,32,512]{3,2,1,0:T(8,128)(2,1)}), bf16[16,3,32,512]{3,2,1,0:T(8,128)(2,1)S(1)}, u32[]{:S(2)}, u32[]{:S(2)}) async-start(bf16[16,3,32,512]{3,2,1,0:T(8,128)(2,1)} %shard_map.131), calls=%async_computation | async-start | bytes 3145728 | tf_op jit(solution)/shard_map/all_to_all | solution.py:430
  14.5 5.0 %collective-permute-start = (bf16[384,512]{1,0:T(8,128)(2,1)S(1)}, bf16[384,512]{1,0:T(8,128)(2,1)S(1)}, u32[]{:S(2)}, u32[]{:S(2)}) collective-permute-start(bf16[384,512]{1,0:T(8,128)(2,1)S(1)} %slice_bitcast_fusion.1), channel_id=1, source_target_pairs={{0,4},{4,8},{8,12},{1,5},{5,9},{9,13},{2,6},{6,10},{10,14},{3,7},{... | collective-permute-start | bytes 1179656 | tf_op jit(solution)/shard_map/ppermute | solution.py:426
  20.2 14.9 %all-to-all-done = bf16[16,3,32,512]{3,2,1,0:T(8,128)(2,1)S(1)} async-done(((bf16[16,3,32,512]{3,2,1,0:T(8,128)(2,1)}), bf16[16,3,32,512]{3,2,1,0:T(8,128)(2,1)S(1)}, u32[]{:S(2)}, u32[]{:S(2)}) %all-to-all-start) | async-done | bytes 1572896 | tf_op jit(solution)/shard_map/all_to_all | solution.py:430
  35.4 6.0 %collective-permute-start.3 = (bf16[3,32,512]{2,1,0:T(8,128)(2,1)S(1)}, bf16[3,32,512]{2,1,0:T(8,128)(2,1)S(1)}, u32[]{:S(2)}, u32[]{:S(2)}) collective-permute-start(bf16[3,32,512]{2,1,0:T(8,128)(2,1)S(1)} %reduce_sum.24.refs_0_), channel_id=1, source_target_pairs={{0,12},{4,0},{8,4},{12,8},{1,13},{5,1},{9,5},{13,9},{2,14},{6,2},{... | collective-permute-start | bytes 294920 | tf_op jit(solution)/shard_map/ppermute | solution.py:437
  41.4 2.2 %collective-permute-start.2 = (bf16[3,32,512]{2,1,0:T(8,128)(2,1)S(1)}, bf16[3,32,512]{2,1,0:T(8,128)(2,1)S(1)}, u32[]{:S(2)}, u32[]{:S(2)}) collective-permute-start(bf16[3,32,512]{2,1,0:T(8,128)(2,1)S(1)} %reduce_sum.24.refs_0_), channel_id=1, source_target_pairs={{0,8},{4,12},{8,0},{12,4},{1,9},{5,13},{9,1},{13,5},{2,10},{6,14},... | collective-permute-start | bytes 294920 | tf_op jit(solution)/shard_map/ppermute | solution.py:437
  43.6 2.4 %collective-permute-start.1 = (bf16[3,32,512]{2,1,0:T(8,128)(2,1)S(1)}, bf16[3,32,512]{2,1,0:T(8,128)(2,1)S(1)}, u32[]{:S(2)}, u32[]{:S(2)}) collective-permute-start(bf16[3,32,512]{2,1,0:T(8,128)(2,1)S(1)} %reduce_sum.24.refs_0_), channel_id=1, source_target_pairs={{0,4},{4,8},{8,12},{12,0},{1,5},{5,9},{9,13},{13,1},{2,6},{6,10},{... | collective-permute-start | bytes 294920 | tf_op jit(solution)/shard_map/ppermute | solution.py:437
  46.0 2.9 %collective-permute-done.2.refs_2_ = bf16[3,32,512]{2,1,0:T(8,128)(2,1)S(1)} collective-permute-done((bf16[3,32,512]{2,1,0:T(8,128)(2,1)S(1)}, bf16[3,32,512]{2,1,0:T(8,128)(2,1)S(1)}, u32[]{:S(2)}, u32[]{:S(2)}) %collective-permute-start.2) | collective-permute-done | bytes 98336 | tf_op jit(solution)/shard_map/ppermute | solution.py:437
  49.0 3.0 %collective-permute-done.1.refs_1_ = bf16[3,32,512]{2,1,0:T(8,128)(2,1)S(1)} collective-permute-done((bf16[3,32,512]{2,1,0:T(8,128)(2,1)S(1)}, bf16[3,32,512]{2,1,0:T(8,128)(2,1)S(1)}, u32[]{:S(2)}, u32[]{:S(2)}) %collective-permute-start.1) | collective-permute-done | bytes 98336 | tf_op jit(solution)/shard_map/ppermute | solution.py:437
  52.0 1.3 shard_map.132
  53.3 6.4 %all-to-all-start.1 = ((bf16[16,3,32,512]{3,2,1,0:T(8,128)(2,1)}), bf16[16,3,32,512]{3,2,1,0:T(8,128)(2,1)}, u32[]{:S(2)}, u32[]{:S(2)}) async-start(bf16[16,3,32,512]{3,2,1,0:T(8,128)(2,1)} %shard_map.132), calls=%async_computation.1 | async-start | bytes 3145728 | tf_op jit(solution)/shard_map/all_to_all | solution.py:444
  60.4 3.5 %collective-permute-start.4 = (bf16[128,512]{1,0:T(8,128)(2,1)S(1)}, bf16[128,512]{1,0:T(8,128)(2,1)S(1)}, u32[]{:S(2)}, u32[]{:S(2)}) collective-permute-start(bf16[128,512]{1,0:T(8,128)(2,1)S(1)} %copy-done.7), channel_id=1, source_target_pairs={{0,4},{4,8},{8,12},{1,5},{5,9},{9,13},{2,6},{6,10},{10,14},{3,7},{... | collective-permute-start | bytes 393224 | tf_op jit(solution)/shard_map/ppermute | solution.py:426
  63.9 5.3 %collective-permute-start.5 = (bf16[128,512]{1,0:T(8,128)(2,1)S(1)}, bf16[128,512]{1,0:T(8,128)(2,1)S(1)}, u32[]{:S(2)}, u32[]{:S(2)}) collective-permute-start(bf16[128,512]{1,0:T(8,128)(2,1)S(1)} %slice_bitcast_fusion.2), channel_id=1, source_target_pairs={{0,4},{4,8},{8,12},{1,5},{5,9},{9,13},{2,6},{6,10},{10,14},{3,7},{... | collective-permute-start | bytes 393224 | tf_op jit(solution)/shard_map/ppermute | solution.py:426
  69.2 1.7 collective-permute-done.5.values_b_ref
  70.9 9.0 %all-to-all-done.1.gathered_hbm = bf16[16,3,32,512]{3,2,1,0:T(8,128)(2,1)} async-done(((bf16[16,3,32,512]{3,2,1,0:T(8,128)(2,1)}), bf16[16,3,32,512]{3,2,1,0:T(8,128)(2,1)}, u32[]{:S(2)}, u32[]{:S(2)}) %all-to-all-start.1) | async-done | bytes 1572896 | tf_op jit(solution)/shard_map/all_to_all | solution.py:444
  79.9 11.5 %shard_map.133 = (bf16[16,3,32,512]{3,2,1,0:T(8,128)(2,1)}, bf16[3,512,512]{2,1,0:T(8,128)(2,1)}) custom-call(s32[1]{0:T(128)} %bitcast.seq_ref, s32[1]{0:T(128)S(6)} %copy.15.split_ref, f32[1]{0:T(128)S(6)} %copy.16.step_ref, f32[1,512]{1,0:T(1,128)} %rates_ref.3, bf16[16,3,32,512]{3,2,1,0:T(8,128)(2,1)} %all-to-all-done.1.gathered_hbm, ...), custom_call_target="tpu_custom_call" | custom-call | flops 6442450944 | bytes 7342080 | tf_op jit(solution)/shard_map/pallas_call | solution.py:322
  91.4 5.3 %all-to-all-start.2 = ((bf16[16,3,32,512]{3,2,1,0:T(8,128)(2,1)}), bf16[16,3,32,512]{3,2,1,0:T(8,128)(2,1)}, u32[]{:S(2)}, u32[]{:S(2)}) async-start(bf16[16,3,32,512]{3,2,1,0:T(8,128)(2,1)} %get-tuple-element.25), calls=%async_computation.2 | async-start | bytes 3145728 | tf_op jit(solution)/shard_map/all_to_all | solution.py:430
  96.7 3.4 %collective-permute-start.6 = (bf16[384,512]{1,0:T(8,128)(2,1)S(1)}, bf16[384,512]{1,0:T(8,128)(2,1)S(1)}, u32[]{:S(2)}, u32[]{:S(2)}) collective-permute-start(bf16[384,512]{1,0:T(8,128)(2,1)S(1)} %slice_bitcast_fusion), channel_id=1, source_target_pairs={{0,4},{4,8},{8,12},{1,5},{5,9},{9,13},{2,6},{6,10},{10,14},{3,7},{... | collective-permute-start | bytes 1179656 | tf_op jit(solution)/shard_map/ppermute | solution.py:426
  100.1 15.7 %all-to-all-done.2 = bf16[16,3,32,512]{3,2,1,0:T(8,128)(2,1)} async-done(((bf16[16,3,32,512]{3,2,1,0:T(8,128)(2,1)}), bf16[16,3,32,512]{3,2,1,0:T(8,128)(2,1)}, u32[]{:S(2)}, u32[]{:S(2)}) %all-to-all-start.2) | async-done | bytes 1572896 | tf_op jit(solution)/shard_map/all_to_all | solution.py:430
  115.7 1.7 reduce_sum.25.refs_0_
  117.5 4.7 %collective-permute-start.8 = (bf16[3,32,512]{2,1,0:T(8,128)(2,1)S(1)}, bf16[3,32,512]{2,1,0:T(8,128)(2,1)S(1)}, u32[]{:S(2)}, u32[]{:S(2)}) collective-permute-start(bf16[3,32,512]{2,1,0:T(8,128)(2,1)S(1)} %reduce_sum.25.refs_0_), channel_id=1, source_target_pairs={{0,8},{4,12},{8,0},{12,4},{1,9},{5,13},{9,1},{13,5},{2,10},{6,14},... | collective-permute-start | bytes 294920 | tf_op jit(solution)/shard_map/ppermute | solution.py:437
  122.2 2.2 %collective-permute-start.7 = (bf16[3,32,512]{2,1,0:T(8,128)(2,1)S(1)}, bf16[3,32,512]{2,1,0:T(8,128)(2,1)S(1)}, u32[]{:S(2)}, u32[]{:S(2)}) collective-permute-start(bf16[3,32,512]{2,1,0:T(8,128)(2,1)S(1)} %reduce_sum.25.refs_0_), channel_id=1, source_target_pairs={{0,4},{4,8},{8,12},{12,0},{1,5},{5,9},{9,13},{13,1},{2,6},{6,10},{... | collective-permute-start | bytes 294920 | tf_op jit(solution)/shard_map/ppermute | solution.py:437
  125.1 2.7 %collective-permute-done.7.refs_1_ = bf16[3,32,512]{2,1,0:T(8,128)(2,1)S(1)} collective-permute-done((bf16[3,32,512]{2,1,0:T(8,128)(2,1)S(1)}, bf16[3,32,512]{2,1,0:T(8,128)(2,1)S(1)}, u32[]{:S(2)}, u32[]{:S(2)}) %collective-permute-start.7) | collective-permute-done | bytes 98336 | tf_op jit(solution)/shard_map/ppermute | solution.py:437
  127.8 1.3 shard_map.134
  129.1 8.7 %all-to-all-start.3 = ((bf16[16,3,32,512]{3,2,1,0:T(8,128)(2,1)}), bf16[16,3,32,512]{3,2,1,0:T(8,128)(2,1)}, u32[]{:S(2)}, u32[]{:S(2)}) async-start(bf16[16,3,32,512]{3,2,1,0:T(8,128)(2,1)} %shard_map.134), calls=%async_computation.3 | async-start | bytes 3145728 | tf_op jit(solution)/shard_map/all_to_all | solution.py:444
  137.9 3.8 %shard_map.135.attended_hbm = f32[512,512]{1,0:T(8,128)S(1)} custom-call(s32[1]{0:T(128)} %bitcast.seq_ref, s32[16]{0:T(128)S(1)} %copy-done.4, bf16[512,512]{1,0:T(8,128)(2,1)S(1)} %bitcast.22, bf16[512,512]{1,0:T(8,128)(2,1)S(1)} %bitcast.19, bf16[512,512]{1,0:T(8,128)(2,1)S(1)} %bitcast.20, bf16[384,512]{1,0:T(8,128)(2,1)S(1)} %collective-permute-done.keys_a_ref, ...), custom_call_target="tpu_custom_call" | custom-call | flops 1073741824 | bytes 3670016 | tf_op jit(solution)/shard_map/pallas_call | solution.py:322
  141.7 1.0 copy-done.6
  142.7 14.2 %all-to-all-done.3.gathered_hbm = bf16[16,3,32,512]{3,2,1,0:T(8,128)(2,1)} async-done(((bf16[16,3,32,512]{3,2,1,0:T(8,128)(2,1)}), bf16[16,3,32,512]{3,2,1,0:T(8,128)(2,1)}, u32[]{:S(2)}, u32[]{:S(2)}) %all-to-all-start.3) | async-done | bytes 1572896 | tf_op jit(solution)/shard_map/all_to_all | solution.py:444
  156.9 10.9 %shard_map.136 = (f32[512,512]{1,0:T(8,128)}, f32[1,512]{1,0:T(1,128)}, bf16[3,512,512]{2,1,0:T(8,128)(2,1)}) custom-call(s32[1]{0:T(128)} %bitcast.seq_ref, s32[1]{0:T(128)S(6)} %copy.15.split_ref, s32[16]{0:T(128)} %fork_ref.1, f32[1]{0:T(128)S(6)} %copy.16.step_ref, bf16[16,3,32,512]{3,2,1,0:T(8,128)(2,1)} %all-to-all-done.3.gathered_hbm, ...), custom_call_target="tpu_custom_call" | custom-call | flops 5637144576 | bytes 8914944 | tf_op jit(solution)/shard_map/pallas_call | solution.py:322
  167.9 12.6 %psum.7.energy_ref = f32[1,512]{1,0:T(1,128)S(1)} all-reduce(f32[1,512]{1,0:T(1,128)} %get-tuple-element.34), channel_id=1, replica_groups=mesh['x'=4,'y'=4,'z'=4,'w'=2,'c'=2] {'w','c'}, use_global_device_ids=true, to_apply=%region_2.0 | all-reduce | flops 512 | bytes 4096 | tf_op jit(solution)/shard_map/psum | solution.py:496
  180.4 1.2 copy-done
  181.7 1.5 shard_map.137
  (26 shorter events, 1.8 us)
Async XLA Ops:
  6.7 7.7 %copy-start.1 = (bf16[1,512,512]{2,1,0:T(8,128)(2,1)S(1)}, bf16[1,512,512]{2,1,0:T(8,128)(2,1)}, u32[]{:S(2)}) copy-start(bf16[1,512,512]{2,1,0:T(8,128)(2,1)} %param.19) | copy-start | bytes 1572868
  6.7 28.4 %all-to-all-start = ((bf16[16,3,32,512]{3,2,1,0:T(8,128)(2,1)}), bf16[16,3,32,512]{3,2,1,0:T(8,128)(2,1)S(1)}, u32[]{:S(2)}, u32[]{:S(2)}) async-start(bf16[16,3,32,512]{3,2,1,0:T(8,128)(2,1)} %shard_map.131), calls=%async_computation | async-start | bytes 3145728 | tf_op jit(solution)/shard_map/all_to_all | solution.py:430
  14.5 31.5 %copy-start.2 = (bf16[1,512,512]{2,1,0:T(8,128)(2,1)S(1)}, bf16[1,512,512]{2,1,0:T(8,128)(2,1)}, u32[]{:S(2)}) copy-start(bf16[1,512,512]{2,1,0:T(8,128)(2,1)} %param.20) | copy-start | bytes 1572868
  14.5 20.8 %collective-permute-start = (bf16[384,512]{1,0:T(8,128)(2,1)S(1)}, bf16[384,512]{1,0:T(8,128)(2,1)S(1)}, u32[]{:S(2)}, u32[]{:S(2)}) collective-permute-start(bf16[384,512]{1,0:T(8,128)(2,1)S(1)} %slice_bitcast_fusion.1), channel_id=1, source_target_pairs={{0,4},{4,8},{8,12},{1,5},{5,9},{9,13},{2,6},{6,10},{10,14},{3,7},{... | collective-permute-start | bytes 1179656 | tf_op jit(solution)/shard_map/ppermute | solution.py:426
  35.4 10.6 %collective-permute-start.3 = (bf16[3,32,512]{2,1,0:T(8,128)(2,1)S(1)}, bf16[3,32,512]{2,1,0:T(8,128)(2,1)S(1)}, u32[]{:S(2)}, u32[]{:S(2)}) collective-permute-start(bf16[3,32,512]{2,1,0:T(8,128)(2,1)S(1)} %reduce_sum.24.refs_0_), channel_id=1, source_target_pairs={{0,12},{4,0},{8,4},{12,8},{1,13},{5,1},{9,5},{13,9},{2,14},{6,2},{... | collective-permute-start | bytes 294920 | tf_op jit(solution)/shard_map/ppermute | solution.py:437
  41.4 7.5 %collective-permute-start.2 = (bf16[3,32,512]{2,1,0:T(8,128)(2,1)S(1)}, bf16[3,32,512]{2,1,0:T(8,128)(2,1)S(1)}, u32[]{:S(2)}, u32[]{:S(2)}) collective-permute-start(bf16[3,32,512]{2,1,0:T(8,128)(2,1)S(1)} %reduce_sum.24.refs_0_), channel_id=1, source_target_pairs={{0,8},{4,12},{8,0},{12,4},{1,9},{5,13},{9,1},{13,5},{2,10},{6,14},... | collective-permute-start | bytes 294920 | tf_op jit(solution)/shard_map/ppermute | solution.py:437
  43.6 8.3 %collective-permute-start.1 = (bf16[3,32,512]{2,1,0:T(8,128)(2,1)S(1)}, bf16[3,32,512]{2,1,0:T(8,128)(2,1)S(1)}, u32[]{:S(2)}, u32[]{:S(2)}) collective-permute-start(bf16[3,32,512]{2,1,0:T(8,128)(2,1)S(1)} %reduce_sum.24.refs_0_), channel_id=1, source_target_pairs={{0,4},{4,8},{8,12},{12,0},{1,5},{5,9},{9,13},{13,1},{2,6},{6,10},{... | collective-permute-start | bytes 294920 | tf_op jit(solution)/shard_map/ppermute | solution.py:437
  53.3 7.1 %copy-start.7 = (bf16[128,512]{1,0:T(8,128)(2,1)S(1)}, bf16[128,512]{1,0:T(8,128)(2,1)}, u32[]{:S(2)}) copy-start(bf16[128,512]{1,0:T(8,128)(2,1)} %slice_bitcast_fusion.3) | copy-start | bytes 393220
  53.3 26.6 %all-to-all-start.1 = ((bf16[16,3,32,512]{3,2,1,0:T(8,128)(2,1)}), bf16[16,3,32,512]{3,2,1,0:T(8,128)(2,1)}, u32[]{:S(2)}, u32[]{:S(2)}) async-start(bf16[16,3,32,512]{3,2,1,0:T(8,128)(2,1)} %shard_map.132), calls=%async_computation.1 | async-start | bytes 3145728 | tf_op jit(solution)/shard_map/all_to_all | solution.py:444
  60.4 8.8 %collective-permute-start.4 = (bf16[128,512]{1,0:T(8,128)(2,1)S(1)}, bf16[128,512]{1,0:T(8,128)(2,1)S(1)}, u32[]{:S(2)}, u32[]{:S(2)}) collective-permute-start(bf16[128,512]{1,0:T(8,128)(2,1)S(1)} %copy-done.7), channel_id=1, source_target_pairs={{0,4},{4,8},{8,12},{1,5},{5,9},{9,13},{2,6},{6,10},{10,14},{3,7},{... | collective-permute-start | bytes 393224 | tf_op jit(solution)/shard_map/ppermute | solution.py:426
  63.9 7.0 %collective-permute-start.5 = (bf16[128,512]{1,0:T(8,128)(2,1)S(1)}, bf16[128,512]{1,0:T(8,128)(2,1)S(1)}, u32[]{:S(2)}, u32[]{:S(2)}) collective-permute-start(bf16[128,512]{1,0:T(8,128)(2,1)S(1)} %slice_bitcast_fusion.2), channel_id=1, source_target_pairs={{0,4},{4,8},{8,12},{1,5},{5,9},{9,13},{2,6},{6,10},{10,14},{3,7},{... | collective-permute-start | bytes 393224 | tf_op jit(solution)/shard_map/ppermute | solution.py:426
  91.4 24.4 %all-to-all-start.2 = ((bf16[16,3,32,512]{3,2,1,0:T(8,128)(2,1)}), bf16[16,3,32,512]{3,2,1,0:T(8,128)(2,1)}, u32[]{:S(2)}, u32[]{:S(2)}) async-start(bf16[16,3,32,512]{3,2,1,0:T(8,128)(2,1)} %get-tuple-element.25), calls=%async_computation.2 | async-start | bytes 3145728 | tf_op jit(solution)/shard_map/all_to_all | solution.py:430
  96.7 20.8 %collective-permute-start.6 = (bf16[384,512]{1,0:T(8,128)(2,1)S(1)}, bf16[384,512]{1,0:T(8,128)(2,1)S(1)}, u32[]{:S(2)}, u32[]{:S(2)}) collective-permute-start(bf16[384,512]{1,0:T(8,128)(2,1)S(1)} %slice_bitcast_fusion), channel_id=1, source_target_pairs={{0,4},{4,8},{8,12},{1,5},{5,9},{9,13},{2,6},{6,10},{10,14},{3,7},{... | collective-permute-start | bytes 1179656 | tf_op jit(solution)/shard_map/ppermute | solution.py:426
  117.4 6.9 %collective-permute-start.9 = (bf16[3,32,512]{2,1,0:T(8,128)(2,1)S(1)}, bf16[3,32,512]{2,1,0:T(8,128)(2,1)S(1)}, u32[]{:S(2)}, u32[]{:S(2)}) collective-permute-start(bf16[3,32,512]{2,1,0:T(8,128)(2,1)S(1)} %reduce_sum.25.refs_0_), channel_id=1, source_target_pairs={{0,12},{4,0},{8,4},{12,8},{1,13},{5,1},{9,5},{13,9},{2,14},{6,2},{... | collective-permute-start | bytes 294920 | tf_op jit(solution)/shard_map/ppermute | solution.py:437
  117.5 7.6 %collective-permute-start.8 = (bf16[3,32,512]{2,1,0:T(8,128)(2,1)S(1)}, bf16[3,32,512]{2,1,0:T(8,128)(2,1)S(1)}, u32[]{:S(2)}, u32[]{:S(2)}) collective-permute-start(bf16[3,32,512]{2,1,0:T(8,128)(2,1)S(1)} %reduce_sum.25.refs_0_), channel_id=1, source_target_pairs={{0,8},{4,12},{8,0},{12,4},{1,9},{5,13},{9,1},{13,5},{2,10},{6,14},... | collective-permute-start | bytes 294920 | tf_op jit(solution)/shard_map/ppermute | solution.py:437
  122.2 5.6 %collective-permute-start.7 = (bf16[3,32,512]{2,1,0:T(8,128)(2,1)S(1)}, bf16[3,32,512]{2,1,0:T(8,128)(2,1)S(1)}, u32[]{:S(2)}, u32[]{:S(2)}) collective-permute-start(bf16[3,32,512]{2,1,0:T(8,128)(2,1)S(1)} %reduce_sum.25.refs_0_), channel_id=1, source_target_pairs={{0,4},{4,8},{8,12},{12,0},{1,5},{5,9},{9,13},{13,1},{2,6},{6,10},{... | collective-permute-start | bytes 294920 | tf_op jit(solution)/shard_map/ppermute | solution.py:437
  129.1 8.8 %copy-start.4 = (s32[16]{0:T(128)S(1)}, s32[16]{0:T(128)}, u32[]{:S(2)}) copy-start(s32[16]{0:T(128)} %length_ref.3) | copy-start | bytes 196
  129.1 8.8 %copy-start.5 = (bf16[1,512,512]{2,1,0:T(8,128)(2,1)S(1)}, bf16[1,512,512]{2,1,0:T(8,128)(2,1)}, u32[]{:S(2)}) copy-start(bf16[1,512,512]{2,1,0:T(8,128)(2,1)} %param.18) | copy-start | bytes 1572868
  129.1 27.8 %all-to-all-start.3 = ((bf16[16,3,32,512]{3,2,1,0:T(8,128)(2,1)}), bf16[16,3,32,512]{3,2,1,0:T(8,128)(2,1)}, u32[]{:S(2)}, u32[]{:S(2)}) async-start(bf16[16,3,32,512]{3,2,1,0:T(8,128)(2,1)} %shard_map.134), calls=%async_computation.3 | async-start | bytes 3145728 | tf_op jit(solution)/shard_map/all_to_all | solution.py:444
  141.7 1.0 copy-start.6
  156.9 23.5 %copy-start.3 = (f32[1,512]{1,0:T(1,128)S(1)}, f32[1,512]{1,0:T(1,128)}, u32[]{:S(2)}) copy-start(f32[1,512]{1,0:T(1,128)} %gain_ref.1) | copy-start | bytes 6148
  180.4 1.2 copy-start

commit v4 on v3

--- a/solution.py
+++ b/solution.py
@@ -18,6 +18,8 @@
 poly_three = 2.0315
 VMEM_BYTES = 24 * 1024 * 1024
 WHOLE_VMEM = 60 * 1024 * 1024
+LAST_VMEM = 50 * 1024 * 1024
+SECOND_VMEM = 60 * 1024 * 1024
 CHUNK = 256
 UPDATE_CHUNK = 512
 
@@ -232,17 +234,16 @@
     split_ref,
     fork_ref,
     step_ref,
+    attended_ref,
     gathered_hbm,
     weights_hbm,
     state_hbm,
     query_hbm,
-    attended_hbm,
     total_ref,
     energy_ref,
     last_hbm,
     old,
     query,
-    attended,
     x_ref,
     gram_ref,
     pool,
@@ -257,14 +258,12 @@
     final = jnp.logical_and(jnp.logical_not(early), fork >= trunk_total)
     fetch_old = pltpu.make_async_copy(state_hbm, old, sems.at[0])
     fetch_query = pltpu.make_async_copy(query_hbm, query, sems.at[1])
-    fetch_attended = pltpu.make_async_copy(attended_hbm, attended, sems.at[2])
-    fetch_first = pltpu.make_async_copy(weights_hbm, pool.at[1], sems.at[3])
-    fetch_state = pltpu.make_async_copy(state_hbm, pool.at[1], sems.at[3])
+    fetch_first = pltpu.make_async_copy(weights_hbm, pool.at[1], sems.at[2])
+    fetch_state = pltpu.make_async_copy(state_hbm, pool.at[1], sems.at[2])
 
     def begin():
         fetch_old.start()
         fetch_query.start()
-        fetch_attended.start()
 
         @pl.when(early)
         def _():
@@ -275,10 +274,9 @@
             fetch_state.start()
 
     emit_update(fetches, gathered, old, step_ref[0], x_ref, gram_ref, pool.at[0], begin, fetch_old.wait)
-    keep = pltpu.make_async_copy(pool.at[0], last_hbm, sems.at[4])
+    keep = pltpu.make_async_copy(pool.at[0], last_hbm, sems.at[3])
     keep.start()
     fetch_query.wait()
-    fetch_attended.wait()
     fetch_state.wait()
     pick = jnp.where(final, 0, 1)
     rows = query.shape[0]
@@ -287,7 +285,7 @@
         first = nt(query[cut], pool[pick, 0])
         third = nt(query[cut], pool[pick, 1])
         hidden = (first * jax.nn.sigmoid(first) * third).astype(jnp.bfloat16)
-        total = attended[cut] + nn(hidden, pool[pick, 2])
+        total = attended_ref[cut] + nn(hidden, pool[pick, 2])
         total_ref[cut] = total
         energy = jnp.sum(total * total, axis=-1, keepdims=True)
         energy_ref[:, cut] = jnp.transpose(jnp.broadcast_to(energy, (UPDATE_CHUNK, 128)))[0:1]
@@ -390,7 +388,7 @@
         (shape(gathered.shape, jnp.bfloat16), shape(full, jnp.bfloat16)),
         scratch,
         flops=48 * keys.size * full[1],
-        vmem=WHOLE_VMEM,
+        vmem=SECOND_VMEM,
     )
 
 
@@ -400,24 +398,23 @@
     scratch = (
         space(full),
         space(query.shape),
-        space(query.shape, jnp.float32),
         space((2, *full)),
         space(full),
         space((2, *full)),
         by_kind(gathered),
-        pltpu.SemaphoreType.DMA((5,)),
+        pltpu.SemaphoreType.DMA((4,)),
         pltpu.SemaphoreType.DMA((3,)),
     )
     return call(
         functools.partial(third_kernel, trunk_total=trunk_total),
         (seq, split, forks, step),
-        (),
+        (attended,),
         (shape((rows, width), jnp.float32), shape((1, rows), jnp.float32)),
-        (gathered, weights, state, query, attended),
+        (gathered, weights, state, query),
         (shape(full, jnp.bfloat16),),
         scratch,
         flops=42 * query.size * full[1],
-        vmem=WHOLE_VMEM,
+        vmem=LAST_VMEM,
     )
 
 
@@ -431,13 +428,19 @@
     return jnp.sum(received.astype(jnp.float32), axis=0).astype(jnp.bfloat16)
 
 
-def sum_depth(mine):
-    depth, planes = lax.axis_size("z"), lax.axis_size(PLANE)
-    others = [
-        lax.ppermute(mine, "z", [(i, (i + step) % depth) for i in range(depth)]) for step in range(1, depth)
-    ]
-    (copies,) = call(replicate_kernel, (), (mine, *others), (shape((planes, *mine.shape), mine.dtype),))
-    return copies
+def swap_depth(value, flip):
+    depth = lax.axis_size("z")
+    return lax.ppermute(value, "z", [(i, i ^ flip) for i in range(depth)])
+
+
+def sum_depth(mine, beside=None):
+    planes = lax.axis_size(PLANE)
+    other, beside = lax.optimization_barrier((swap_depth(mine, 1), beside))
+    pair = (mine.astype(jnp.float32) + other.astype(jnp.float32)).astype(jnp.bfloat16)
+    (copies,) = call(
+        replicate_kernel, (), (pair, swap_depth(pair, 3)), (shape((planes, *mine.shape), mine.dtype),)
+    )
+    return copies, beside
 
 
 def spread_plane(copies):
@@ -468,20 +471,20 @@
     total_width = width * lax.axis_size(HEAD)
     seq = lax.axis_index(SEQ).astype(jnp.int32).reshape(1)
     parts_shape = shape((planes, 3, hidden // planes, width), jnp.bfloat16)
+    barrier = lax.optimization_barrier
     most = 3 * rows // 4
-    barrier = lax.optimization_barrier
 
     keys_a = from_behind(own_keys[:most])
     parts = gradient_first(seq, segment_end, trunk_rates, weights, keys, values, parts_shape)
     mine, keys_a = barrier((sum_plane(parts), keys_a))
-    copies, rest_keys, rest_values = barrier((sum_depth(mine), own_keys[most:], own_values[: rows - most]))
+    copies, _ = sum_depth(mine)
+    copies, rest_keys, rest_values = barrier((copies, own_keys[most:], own_values[: rows - most]))
     gathered, keys_b, values_b = barrier((spread_plane(copies), from_behind(rest_keys), from_behind(rest_values)))
     parts, state = update_and_gradient(
         seq, segment_end, step_sizes, gathered, trunk_rates, weights, keys, values
     )
     parts, rest_values = barrier((parts, own_values[rows - most :]))
-    mine, values_c = barrier((sum_plane(parts), from_behind(rest_values)))
-    copies = sum_depth(mine)
+    mine, values_c, query = barrier((sum_plane(parts), from_behind(rest_values), query))
     (attended,) = call(
         attend_kernel,
         (seq, branch_lengths),
@@ -489,6 +492,7 @@
         (shape((rows, width), jnp.float32),),
         flops=8 * rows * rows * width,
     )
+    copies, attended = sum_depth(mine, attended)
     gathered = spread_plane(copies)
     total, energy, last = update_and_apply(
         seq, segment_end, fork_points, step_sizes, gathered, weights, state, query, attended, trunk_total

time: 184 us -> 175 us (0.951)
  blocking collectives: 12.6 us -> 33.8 us
  waiting for transfers between devices: 64.8 us -> 46.2 us
  starting transfers between devices: 62.9 us -> 56.9 us
  local copies, waits for them, and re-layouts: 2.97 us -> 0.11 us
  Pallas kernels: 35.8 us -> 33.6 us
    all_to_all x0 -> x1, blocking collectives: none -> 23.2 us  [spread_plane(): return lax.all_to_all(copies, PLANE, 0, 0, tiled=False)]
    all_to_all x2 -> x1, waiting for transfers between devices: 23.3 us -> 6.11 us  [spread_plane(): return lax.all_to_all(copies, PLANE, 0, 0, tiled=False)]
    all_to_all x2 -> x1, starting transfers between devices: 15.2 us -> 8.22 us  [spread_plane(): return lax.all_to_all(copies, PLANE, 0, 0, tiled=False)]
    ppermute x6 -> x4, starting transfers between devices: 17.6 us -> 13.8 us  [swap_depth(): return lax.ppermute(value, 'z', [(i, i ^ flip) for i in range(depth)])]
    ppermute x4, starting transfers between devices: 17.2 us -> 20.5 us  [from_behind(): lax.ppermute(value, 'z', [(source, source + 1) for source in range(count...]
    unnamed x16 -> x12, local copies, waits for them, and re-layouts: 2.24 us -> 0.04 us
    pallas_call x7, Pallas kernels: 35.8 us -> 33.6 us  [call(): pl.pallas_call(kernel, out_shape=(*outs, *held_outs), in_specs=[SMEM] * l...]
    psum x1, blocking collectives: 12.6 us -> 10.6 us  [per_device(): energy = lax.psum(energy, HEAD)]
  transfers between devices with their start and end apart: 14 -> 11, of which waited for: 9 -> 7; matrix products, arithmetic and copies ran while one was open for 1% -> 1% of each run, Pallas kernels for 2% -> 2%
where the time goes in v4:
time: 175 us
  starting transfers between devices  56.9 us (33%)
  waiting for transfers between devices  46.2 us (26%)
  blocking collectives  33.8 us (19%)
  Pallas kernels  33.6 us (19%)
  between operations  2.15 us (1%)
  other arithmetic  1.98 us (1%)
    pallas_call x7, Pallas kernels, call(): pl.pallas_call(kernel, out_shape=(*outs, *held_outs), in_specs=[SMEM] * l...  33.6 us
    all_to_all x2, waiting for transfers between devices, sum_plane(): received = lax.all_to_all(parts, PLANE, 0, 0, tiled=False)  30.4 us
    all_to_all x1, blocking collectives, spread_plane(): return lax.all_to_all(copies, PLANE, 0, 0, tiled=False)  23.2 us
    ppermute x4, starting transfers between devices, from_behind(): lax.ppermute(value, 'z', [(source, source + 1) for source in range(count...  20.5 us
    all_to_all x2, starting transfers between devices, sum_plane(): received = lax.all_to_all(parts, PLANE, 0, 0, tiled=False)  14.3 us
    ppermute x4, starting transfers between devices, swap_depth(): return lax.ppermute(value, 'z', [(i, i ^ flip) for i in range(depth)])  13.8 us
    psum x1, blocking collectives, per_device(): energy = lax.psum(energy, HEAD)  10.6 us
    all_to_all x1, starting transfers between devices, spread_plane(): return lax.all_to_all(copies, PLANE, 0, 0, tiled=False)  8.22 us
  transfers between devices with their start and end apart: 11, of which 7 were waited for; matrix products, arithmetic and copies ran while one was open for 1% of the time, Pallas kernels for 2%

profile of v4, /device:TPU:1, one launch (start us, length us, event | category | flops | bytes accessed | tf_op | source)
XLA Modules:
  0.0 174.8 jit_solution(16321458749506622158)
XLA Ops:
  1.3 5.4 %shard_map.131 = bf16[16,3,32,512]{3,2,1,0:T(8,128)(2,1)} custom-call(s32[1]{0:T(128)} %bitcast.seq_ref, s32[1]{0:T(128)S(6)} %copy.15.split_ref, f32[1,512]{1,0:T(1,128)} %rates_ref.3, bf16[3,512,512]{2,1,0:T(8,128)(2,1)} %bitcast.24, bf16[512,512]{1,0:T(8,128)(2,1)} %bitcast.27, bf16[512,512]{1,0:T(8,128)(2,1)} %bitcast.29), custom_call_target="tpu_custom_call" | custom-call | flops 1610612736 | bytes 4196352 | tf_op jit(solution)/shard_map/pallas_call | solution.py:320
  6.7 0.0 copy-start
  6.7 7.7 %all-to-all-start = ((bf16[16,3,32,512]{3,2,1,0:T(8,128)(2,1)}), bf16[16,3,32,512]{3,2,1,0:T(8,128)(2,1)S(1)}, u32[]{:S(2)}, u32[]{:S(2)}) async-start(bf16[16,3,32,512]{3,2,1,0:T(8,128)(2,1)} %shard_map.131), calls=%async_computation | async-start | bytes 3145728 | tf_op jit(solution)/shard_map/all_to_all | solution.py:427
  14.5 0.0 copy-start.1
  14.5 5.0 %collective-permute-start = (bf16[384,512]{1,0:T(8,128)(2,1)S(1)}, bf16[384,512]{1,0:T(8,128)(2,1)S(1)}, u32[]{:S(2)}, u32[]{:S(2)}) collective-permute-start(bf16[384,512]{1,0:T(8,128)(2,1)S(1)} %slice_bitcast_fusion.1), channel_id=1, source_target_pairs={{0,4},{4,8},{8,12},{1,5},{5,9},{9,13},{2,6},{6,10},{10,14},{3,7},{... | collective-permute-start | bytes 1179656 | tf_op jit(solution)/shard_map/ppermute | solution.py:423
  19.6 15.5 %all-to-all-done = bf16[16,3,32,512]{3,2,1,0:T(8,128)(2,1)S(1)} async-done(((bf16[16,3,32,512]{3,2,1,0:T(8,128)(2,1)}), bf16[16,3,32,512]{3,2,1,0:T(8,128)(2,1)S(1)}, u32[]{:S(2)}, u32[]{:S(2)}) %all-to-all-start) | async-done | bytes 1572896 | tf_op jit(solution)/shard_map/all_to_all | solution.py:427
  35.1 0.3 reduce_sum.24
  35.4 4.1 %collective-permute-start.1 = (bf16[3,32,512]{2,1,0:T(8,128)(2,1)S(1)}, bf16[3,32,512]{2,1,0:T(8,128)(2,1)S(1)}, u32[]{:S(2)}, u32[]{:S(2)}) collective-permute-start(bf16[3,32,512]{2,1,0:T(8,128)(2,1)S(1)} %reduce_sum.24), channel_id=1, source_target_pairs={{0,4},{4,0},{8,12},{12,8},{1,5},{5,1},{9,13},{13,9},{2,6},{6,2},{1... | collective-permute-start | bytes 294920 | tf_op jit(solution)/shard_map/ppermute | solution.py:433
  39.5 2.0 %collective-permute-done.1 = bf16[3,32,512]{2,1,0:T(8,128)(2,1)S(1)} collective-permute-done((bf16[3,32,512]{2,1,0:T(8,128)(2,1)S(1)}, bf16[3,32,512]{2,1,0:T(8,128)(2,1)S(1)}, u32[]{:S(2)}, u32[]{:S(2)}) %collective-permute-start.1) | collective-permute-done | bytes 98336 | tf_op jit(solution)/shard_map/ppermute | solution.py:433
  41.5 4.6 %collective-permute-start.2 = (bf16[3,32,512]{2,1,0:T(8,128)(2,1)S(1)}, bf16[3,32,512]{2,1,0:T(8,128)(2,1)S(1)}, u32[]{:S(2)}, u32[]{:S(2)}) collective-permute-start(bf16[3,32,512]{2,1,0:T(8,128)(2,1)S(1)} %add_convert_fusion.1.refs_0_), channel_id=1, source_target_pairs={{0,12},{4,8},{8,4},{12,0},{1,13},{5,9},{9,5},{13,1},{2,14},{6,10},... | collective-permute-start | bytes 294920 | tf_op jit(solution)/shard_map/ppermute | solution.py:433
  46.2 2.0 %collective-permute-done.2.refs_1_ = bf16[3,32,512]{2,1,0:T(8,128)(2,1)S(1)} collective-permute-done((bf16[3,32,512]{2,1,0:T(8,128)(2,1)S(1)}, bf16[3,32,512]{2,1,0:T(8,128)(2,1)S(1)}, u32[]{:S(2)}, u32[]{:S(2)}) %collective-permute-start.2) | collective-permute-done | bytes 98336 | tf_op jit(solution)/shard_map/ppermute | solution.py:433
  48.2 1.3 shard_map.132
  49.5 8.2 %all-to-all-start.1 = ((bf16[16,3,32,512]{3,2,1,0:T(8,128)(2,1)}), bf16[16,3,32,512]{3,2,1,0:T(8,128)(2,1)}, u32[]{:S(2)}, u32[]{:S(2)}) async-start(bf16[16,3,32,512]{3,2,1,0:T(8,128)(2,1)} %shard_map.132), calls=%async_computation.1 | async-start | bytes 3145728 | tf_op jit(solution)/shard_map/all_to_all | solution.py:447
  58.3 4.9 %collective-permute-start.3 = (bf16[128,512]{1,0:T(8,128)(2,1)S(1)}, bf16[128,512]{1,0:T(8,128)(2,1)S(1)}, u32[]{:S(2)}, u32[]{:S(2)}) collective-permute-start(bf16[128,512]{1,0:T(8,128)(2,1)S(1)} %slice_bitcast_fusion.3), channel_id=1, source_target_pairs={{0,4},{4,8},{8,12},{1,5},{5,9},{9,13},{2,6},{6,10},{10,14},{3,7},{... | collective-permute-start | bytes 393224 | tf_op jit(solution)/shard_map/ppermute | solution.py:423
  63.3 5.5 %collective-permute-start.4 = (bf16[128,512]{1,0:T(8,128)(2,1)S(1)}, bf16[128,512]{1,0:T(8,128)(2,1)S(1)}, u32[]{:S(2)}, u32[]{:S(2)}) collective-permute-start(bf16[128,512]{1,0:T(8,128)(2,1)S(1)} %slice_bitcast_fusion.2), channel_id=1, source_target_pairs={{0,4},{4,8},{8,12},{1,5},{5,9},{9,13},{2,6},{6,10},{10,14},{3,7},{... | collective-permute-start | bytes 393224 | tf_op jit(solution)/shard_map/ppermute | solution.py:423
  68.9 1.7 collective-permute-done.4.values_b_ref
  70.6 6.1 %all-to-all-done.1.gathered_hbm = bf16[16,3,32,512]{3,2,1,0:T(8,128)(2,1)} async-done(((bf16[16,3,32,512]{3,2,1,0:T(8,128)(2,1)}), bf16[16,3,32,512]{3,2,1,0:T(8,128)(2,1)}, u32[]{:S(2)}, u32[]{:S(2)}) %all-to-all-start.1) | async-done | bytes 1572896 | tf_op jit(solution)/shard_map/all_to_all | solution.py:447
  76.7 11.5 %shard_map.133 = (bf16[16,3,32,512]{3,2,1,0:T(8,128)(2,1)}, bf16[3,512,512]{2,1,0:T(8,128)(2,1)}) custom-call(s32[1]{0:T(128)} %bitcast.seq_ref, s32[1]{0:T(128)S(6)} %copy.15.split_ref, f32[1]{0:T(128)S(6)} %copy.16.step_ref, f32[1,512]{1,0:T(1,128)} %rates_ref.3, bf16[16,3,32,512]{3,2,1,0:T(8,128)(2,1)} %all-to-all-done.1.gathered_hbm, ...), custom_call_target="tpu_custom_call" | custom-call | flops 6442450944 | bytes 7342080 | tf_op jit(solution)/shard_map/pallas_call | solution.py:320
  88.2 6.6 %all-to-all-start.2 = ((bf16[16,3,32,512]{3,2,1,0:T(8,128)(2,1)}), bf16[16,3,32,512]{3,2,1,0:T(8,128)(2,1)}, u32[]{:S(2)}, u32[]{:S(2)}) async-start(bf16[16,3,32,512]{3,2,1,0:T(8,128)(2,1)} %get-tuple-element.28), calls=%async_computation.2 | async-start | bytes 3145728 | tf_op jit(solution)/shard_map/all_to_all | solution.py:427
  94.8 5.0 %collective-permute-start.5 = (bf16[384,512]{1,0:T(8,128)(2,1)S(1)}, bf16[384,512]{1,0:T(8,128)(2,1)S(1)}, u32[]{:S(2)}, u32[]{:S(2)}) collective-permute-start(bf16[384,512]{1,0:T(8,128)(2,1)S(1)} %slice_bitcast_fusion), channel_id=1, source_target_pairs={{0,4},{4,8},{8,12},{1,5},{5,9},{9,13},{2,6},{6,10},{10,14},{3,7},{... | collective-permute-start | bytes 1179656 | tf_op jit(solution)/shard_map/ppermute | solution.py:423
  99.8 14.9 %all-to-all-done.2 = bf16[16,3,32,512]{3,2,1,0:T(8,128)(2,1)} async-done(((bf16[16,3,32,512]{3,2,1,0:T(8,128)(2,1)}), bf16[16,3,32,512]{3,2,1,0:T(8,128)(2,1)}, u32[]{:S(2)}, u32[]{:S(2)}) %all-to-all-start.2) | async-done | bytes 1572896 | tf_op jit(solution)/shard_map/all_to_all | solution.py:427
  114.7 1.7 reduce_sum.25
  116.3 2.8 %collective-permute-start.6 = (bf16[3,32,512]{2,1,0:T(8,128)(2,1)S(1)}, bf16[3,32,512]{2,1,0:T(8,128)(2,1)S(1)}, u32[]{:S(2)}, u32[]{:S(2)}) collective-permute-start(bf16[3,32,512]{2,1,0:T(8,128)(2,1)S(1)} %reduce_sum.25), channel_id=1, source_target_pairs={{0,4},{4,0},{8,12},{12,8},{1,5},{5,1},{9,13},{13,9},{2,6},{6,2},{1... | collective-permute-start | bytes 294920 | tf_op jit(solution)/shard_map/ppermute | solution.py:433
  119.1 3.8 %shard_map.134.attended_ref = f32[512,512]{1,0:T(8,128)S(1)} custom-call(s32[1]{0:T(128)} %bitcast.seq_ref, s32[16]{0:T(128)S(1)} %copy-done.3, bf16[512,512]{1,0:T(8,128)(2,1)S(1)} %bitcast.21, bf16[512,512]{1,0:T(8,128)(2,1)S(1)} %bitcast.19, bf16[512,512]{1,0:T(8,128)(2,1)S(1)} %bitcast.20, bf16[384,512]{1,0:T(8,128)(2,1)S(1)} %collective-permute-done.keys_a_ref, ...), custom_call_target="tpu_custom_call" | custom-call | flops 1073741824 | bytes 3670016 | tf_op jit(solution)/shard_map/pallas_call | solution.py:320
  123.0 2.3 %collective-permute-start.7 = (bf16[3,32,512]{2,1,0:T(8,128)(2,1)S(1)}, bf16[3,32,512]{2,1,0:T(8,128)(2,1)S(1)}, u32[]{:S(2)}, u32[]{:S(2)}) collective-permute-start(bf16[3,32,512]{2,1,0:T(8,128)(2,1)S(1)} %add_convert_fusion.refs_0_), channel_id=1, source_target_pairs={{0,12},{4,8},{8,4},{12,0},{1,13},{5,9},{9,5},{13,1},{2,14},{6,10},... | collective-permute-start | bytes 294920 | tf_op jit(solution)/shard_map/ppermute | solution.py:433
  125.3 4.0 %collective-permute-done.7.refs_1_ = bf16[3,32,512]{2,1,0:T(8,128)(2,1)S(1)} collective-permute-done((bf16[3,32,512]{2,1,0:T(8,128)(2,1)S(1)}, bf16[3,32,512]{2,1,0:T(8,128)(2,1)S(1)}, u32[]{:S(2)}, u32[]{:S(2)}) %collective-permute-start.7) | collective-permute-done | bytes 98336 | tf_op jit(solution)/shard_map/ppermute | solution.py:433
  129.4 0.1 shard_map.135
  129.5 0.0 copy-start.5
  129.5 23.2 %all_to_all.20.gathered_hbm = bf16[16,3,32,512]{3,2,1,0:T(8,128)(2,1)} all-to-all(bf16[16,3,32,512]{3,2,1,0:T(8,128)(2,1)S(1)} %shard_map.135), channel_id=1, replica_groups=mesh['x'=4,'y'=4,'z'=4,'w'=2,'c'=2] {'x','y'}, dimensions={0} | all-to-all | bytes 3145728 | tf_op jit(solution)/shard_map/all_to_all | solution.py:447
  152.8 9.9 %shard_map.136 = (f32[512,512]{1,0:T(8,128)S(1)}, f32[1,512]{1,0:T(1,128)S(1)}, bf16[3,512,512]{2,1,0:T(8,128)(2,1)}) custom-call(s32[1]{0:T(128)} %bitcast.seq_ref, s32[1]{0:T(128)S(6)} %copy.15.split_ref, s32[16]{0:T(128)S(1)} %copy-done.5, f32[1]{0:T(128)S(6)} %copy.16.step_ref, f32[512,512]{1,0:T(8,128)S(1)} %shard_map.134.attended_ref, ...), custom_call_target="tpu_custom_call" | custom-call | flops 5637144576 | bytes 8914944 | tf_op jit(solution)/shard_map/pallas_call | solution.py:320
  162.7 10.6 %psum.7.energy_ref = f32[1,512]{1,0:T(1,128)S(1)} all-reduce(f32[1,512]{1,0:T(1,128)S(1)} %get-tuple-element.40), channel_id=1, replica_groups=mesh['x'=4,'y'=4,'z'=4,'w'=2,'c'=2] {'w','c'}, use_global_device_ids=true, to_apply=%region_2.0 | all-reduce | flops 512 | bytes 4096 | tf_op jit(solution)/shard_map/psum | solution.py:500
  173.3 1.5 shard_map.137
  (19 shorter events, 0.2 us)
Async XLA Ops:
  6.7 7.7 %copy-start = (bf16[1,512,512]{2,1,0:T(8,128)(2,1)S(1)}, bf16[1,512,512]{2,1,0:T(8,128)(2,1)}, u32[]{:S(2)}) copy-start(bf16[1,512,512]{2,1,0:T(8,128)(2,1)} %param.19) | copy-start | bytes 1572868
  6.7 28.4 %all-to-all-start = ((bf16[16,3,32,512]{3,2,1,0:T(8,128)(2,1)}), bf16[16,3,32,512]{3,2,1,0:T(8,128)(2,1)S(1)}, u32[]{:S(2)}, u32[]{:S(2)}) async-start(bf16[16,3,32,512]{3,2,1,0:T(8,128)(2,1)} %shard_map.131), calls=%async_computation | async-start | bytes 3145728 | tf_op jit(solution)/shard_map/all_to_all | solution.py:427
  14.5 31.7 %copy-start.1 = (bf16[1,512,512]{2,1,0:T(8,128)(2,1)S(1)}, bf16[1,512,512]{2,1,0:T(8,128)(2,1)}, u32[]{:S(2)}) copy-start(bf16[1,512,512]{2,1,0:T(8,128)(2,1)} %param.20) | copy-start | bytes 1572868
  14.5 20.8 %collective-permute-start = (bf16[384,512]{1,0:T(8,128)(2,1)S(1)}, bf16[384,512]{1,0:T(8,128)(2,1)S(1)}, u32[]{:S(2)}, u32[]{:S(2)}) collective-permute-start(bf16[384,512]{1,0:T(8,128)(2,1)S(1)} %slice_bitcast_fusion.1), channel_id=1, source_target_pairs={{0,4},{4,8},{8,12},{1,5},{5,9},{9,13},{2,6},{6,10},{10,14},{3,7},{... | collective-permute-start | bytes 1179656 | tf_op jit(solution)/shard_map/ppermute | solution.py:423
  35.4 6.1 %collective-permute-start.1 = (bf16[3,32,512]{2,1,0:T(8,128)(2,1)S(1)}, bf16[3,32,512]{2,1,0:T(8,128)(2,1)S(1)}, u32[]{:S(2)}, u32[]{:S(2)}) collective-permute-start(bf16[3,32,512]{2,1,0:T(8,128)(2,1)S(1)} %reduce_sum.24), channel_id=1, source_target_pairs={{0,4},{4,0},{8,12},{12,8},{1,5},{5,1},{9,13},{13,9},{2,6},{6,2},{1... | collective-permute-start | bytes 294920 | tf_op jit(solution)/shard_map/ppermute | solution.py:433
  41.5 6.6 %collective-permute-start.2 = (bf16[3,32,512]{2,1,0:T(8,128)(2,1)S(1)}, bf16[3,32,512]{2,1,0:T(8,128)(2,1)S(1)}, u32[]{:S(2)}, u32[]{:S(2)}) collective-permute-start(bf16[3,32,512]{2,1,0:T(8,128)(2,1)S(1)} %add_convert_fusion.1.refs_0_), channel_id=1, source_target_pairs={{0,12},{4,8},{8,4},{12,0},{1,13},{5,9},{9,5},{13,1},{2,14},{6,10},... | collective-permute-start | bytes 294920 | tf_op jit(solution)/shard_map/ppermute | solution.py:433
  49.5 27.2 %all-to-all-start.1 = ((bf16[16,3,32,512]{3,2,1,0:T(8,128)(2,1)}), bf16[16,3,32,512]{3,2,1,0:T(8,128)(2,1)}, u32[]{:S(2)}, u32[]{:S(2)}) async-start(bf16[16,3,32,512]{3,2,1,0:T(8,128)(2,1)} %shard_map.132), calls=%async_computation.1 | async-start | bytes 3145728 | tf_op jit(solution)/shard_map/all_to_all | solution.py:447
  58.3 10.5 %collective-permute-start.3 = (bf16[128,512]{1,0:T(8,128)(2,1)S(1)}, bf16[128,512]{1,0:T(8,128)(2,1)S(1)}, u32[]{:S(2)}, u32[]{:S(2)}) collective-permute-start(bf16[128,512]{1,0:T(8,128)(2,1)S(1)} %slice_bitcast_fusion.3), channel_id=1, source_target_pairs={{0,4},{4,8},{8,12},{1,5},{5,9},{9,13},{2,6},{6,10},{10,14},{3,7},{... | collective-permute-start | bytes 393224 | tf_op jit(solution)/shard_map/ppermute | solution.py:423
  63.3 7.3 %collective-permute-start.4 = (bf16[128,512]{1,0:T(8,128)(2,1)S(1)}, bf16[128,512]{1,0:T(8,128)(2,1)S(1)}, u32[]{:S(2)}, u32[]{:S(2)}) collective-permute-start(bf16[128,512]{1,0:T(8,128)(2,1)S(1)} %slice_bitcast_fusion.2), channel_id=1, source_target_pairs={{0,4},{4,8},{8,12},{1,5},{5,9},{9,13},{2,6},{6,10},{10,14},{3,7},{... | collective-permute-start | bytes 393224 | tf_op jit(solution)/shard_map/ppermute | solution.py:423
  88.2 26.5 %all-to-all-start.2 = ((bf16[16,3,32,512]{3,2,1,0:T(8,128)(2,1)}), bf16[16,3,32,512]{3,2,1,0:T(8,128)(2,1)}, u32[]{:S(2)}, u32[]{:S(2)}) async-start(bf16[16,3,32,512]{3,2,1,0:T(8,128)(2,1)} %get-tuple-element.28), calls=%async_computation.2 | async-start | bytes 3145728 | tf_op jit(solution)/shard_map/all_to_all | solution.py:427
  94.8 24.4 %copy-start.3 = (s32[16]{0:T(128)S(1)}, s32[16]{0:T(128)}, u32[]{:S(2)}) copy-start(s32[16]{0:T(128)} %length_ref.3) | copy-start | bytes 196
  94.8 24.4 %copy-start.4 = (bf16[1,512,512]{2,1,0:T(8,128)(2,1)S(1)}, bf16[1,512,512]{2,1,0:T(8,128)(2,1)}, u32[]{:S(2)}) copy-start(bf16[1,512,512]{2,1,0:T(8,128)(2,1)} %param.18) | copy-start | bytes 1572868
  94.8 21.6 %collective-permute-start.5 = (bf16[384,512]{1,0:T(8,128)(2,1)S(1)}, bf16[384,512]{1,0:T(8,128)(2,1)S(1)}, u32[]{:S(2)}, u32[]{:S(2)}) collective-permute-start(bf16[384,512]{1,0:T(8,128)(2,1)S(1)} %slice_bitcast_fusion), channel_id=1, source_target_pairs={{0,4},{4,8},{8,12},{1,5},{5,9},{9,13},{2,6},{6,10},{10,14},{3,7},{... | collective-permute-start | bytes 1179656 | tf_op jit(solution)/shard_map/ppermute | solution.py:423
  116.3 6.6 %collective-permute-start.6 = (bf16[3,32,512]{2,1,0:T(8,128)(2,1)S(1)}, bf16[3,32,512]{2,1,0:T(8,128)(2,1)S(1)}, u32[]{:S(2)}, u32[]{:S(2)}) collective-permute-start(bf16[3,32,512]{2,1,0:T(8,128)(2,1)S(1)} %reduce_sum.25), channel_id=1, source_target_pairs={{0,4},{4,0},{8,12},{12,8},{1,5},{5,1},{9,13},{13,9},{2,6},{6,2},{1... | collective-permute-start | bytes 294920 | tf_op jit(solution)/shard_map/ppermute | solution.py:433
  123.0 6.3 %collective-permute-start.7 = (bf16[3,32,512]{2,1,0:T(8,128)(2,1)S(1)}, bf16[3,32,512]{2,1,0:T(8,128)(2,1)S(1)}, u32[]{:S(2)}, u32[]{:S(2)}) collective-permute-start(bf16[3,32,512]{2,1,0:T(8,128)(2,1)S(1)} %add_convert_fusion.refs_0_), channel_id=1, source_target_pairs={{0,12},{4,8},{8,4},{12,0},{1,13},{5,9},{9,5},{13,1},{2,14},{6,10},... | collective-permute-start | bytes 294920 | tf_op jit(solution)/shard_map/ppermute | solution.py:433
  129.5 23.2 %copy-start.5 = (s32[16]{0:T(128)S(1)}, s32[16]{0:T(128)}, u32[]{:S(2)}) copy-start(s32[16]{0:T(128)} %fork_ref.1) | copy-start | bytes 196
  152.7 20.6 %copy-start.2 = (f32[1,512]{1,0:T(1,128)S(1)}, f32[1,512]{1,0:T(1,128)}, u32[]{:S(2)}) copy-start(f32[1,512]{1,0:T(1,128)} %gain_ref.1) | copy-start | bytes 6148

commit v5 on v4

--- a/solution.py
+++ b/solution.py
@@ -18,7 +18,7 @@
 poly_three = 2.0315
 VMEM_BYTES = 24 * 1024 * 1024
 WHOLE_VMEM = 60 * 1024 * 1024
-LAST_VMEM = 50 * 1024 * 1024
+LAST_VMEM = 46 * 1024 * 1024
 SECOND_VMEM = 60 * 1024 * 1024
 CHUNK = 256
 UPDATE_CHUNK = 512
@@ -86,12 +86,10 @@
     return copies
 
 
-def emit_update(fetches, gathered_ref, old_ref, step_size, x_ref, gram_ref, out_ref, begin, ready):
-    kinds, planes, step, width = gathered_ref.shape
-    rows = planes * step
+def emit_update(load, old_ref, step_size, x_ref, gram_ref, out_ref, begin, ready):
+    kinds, rows, width = out_ref.shape
     for kind in range(kinds):
-        fetches[kind].wait()
-        wide = gathered_ref[kind].reshape(rows, width).astype(jnp.float32)
+        wide = load(kind).reshape(rows, width).astype(jnp.float32)
         square = jnp.sum(jnp.sum(wide * wide, axis=0, keepdims=True), axis=1, keepdims=True)
         inverse = 1.0 / (jnp.sqrt(square) + 1e-07)
         x_ref[0, kind] = (wide * inverse).astype(jnp.bfloat16)
@@ -191,7 +189,11 @@
         fetch_keys.start()
         fetch_values.start()
 
-    emit_update(fetches, gathered, weights, step_ref[0], x_ref, gram_ref, state, begin, fetch_weights.wait)
+    def load(kind):
+        fetches[kind].wait()
+        return gathered[kind]
+
+    emit_update(load, weights, step_ref[0], x_ref, gram_ref, state, begin, fetch_weights.wait)
     keep = pltpu.make_async_copy(state, state_hbm, sems.at[3])
     keep.start()
     rates = masked_rates(rates_ref, seq_ref, split_ref, 1)
@@ -234,8 +236,8 @@
     split_ref,
     fork_ref,
     step_ref,
+    gathered_ref,
     attended_ref,
-    gathered_hbm,
     weights_hbm,
     state_hbm,
     query_hbm,
@@ -247,12 +249,9 @@
     x_ref,
     gram_ref,
     pool,
-    gathered,
     sems,
-    gathered_sems,
     trunk_total,
 ):
-    fetches = fetch_gathered(gathered_hbm, gathered, gathered_sems)
     fork = fork_ref[seq_ref[0] // BR_SPAN]
     early = fork < split_ref[0]
     final = jnp.logical_and(jnp.logical_not(early), fork >= trunk_total)
@@ -273,7 +272,7 @@
         def _():
             fetch_state.start()
 
-    emit_update(fetches, gathered, old, step_ref[0], x_ref, gram_ref, pool.at[0], begin, fetch_old.wait)
+    emit_update(lambda kind: gathered_ref[:, kind], old, step_ref[0], x_ref, gram_ref, pool.at[0], begin, fetch_old.wait)
     keep = pltpu.make_async_copy(pool.at[0], last_hbm, sems.at[3])
     keep.start()
     fetch_query.wait()
@@ -401,16 +400,14 @@
         space((2, *full)),
         space(full),
         space((2, *full)),
-        by_kind(gathered),
         pltpu.SemaphoreType.DMA((4,)),
-        pltpu.SemaphoreType.DMA((3,)),
     )
     return call(
         functools.partial(third_kernel, trunk_total=trunk_total),
         (seq, split, forks, step),
-        (attended,),
+        (gathered, attended),
         (shape((rows, width), jnp.float32), shape((1, rows), jnp.float32)),
-        (gathered, weights, state, query),
+        (weights, state, query),
         (shape(full, jnp.bfloat16),),
         scratch,
         flops=42 * query.size * full[1],

time: 175 us -> 174 us (level)
  no operation moved by 1% of the time
where the time goes in v5:
time: 174 us
  starting transfers between devices  56.9 us (33%)
  waiting for transfers between devices  46.3 us (27%)
  blocking collectives  33.9 us (19%)
  Pallas kernels  32.5 us (19%)
  between operations  2.18 us (1%)
  other arithmetic  1.98 us (1%)
    pallas_call x7, Pallas kernels, call(): pl.pallas_call(kernel, out_shape=(*outs, *held_outs), in_specs=[SMEM] * l...  32.5 us
    all_to_all x2, waiting for transfers between devices, sum_plane(): received = lax.all_to_all(parts, PLANE, 0, 0, tiled=False)  30.4 us
    all_to_all x1, blocking collectives, spread_plane(): return lax.all_to_all(copies, PLANE, 0, 0, tiled=False)  23.4 us
    ppermute x4, starting transfers between devices, from_behind(): lax.ppermute(value, 'z', [(source, source + 1) for source in range(count...  20.5 us
    all_to_all x2, starting transfers between devices, sum_plane(): received = lax.all_to_all(parts, PLANE, 0, 0, tiled=False)  14.3 us
    ppermute x4, starting transfers between devices, swap_depth(): return lax.ppermute(value, 'z', [(i, i ^ flip) for i in range(depth)])  13.8 us
    psum x1, blocking collectives, per_device(): energy = lax.psum(energy, HEAD)  10.5 us
    all_to_all x1, starting transfers between devices, spread_plane(): return lax.all_to_all(copies, PLANE, 0, 0, tiled=False)  8.22 us
  transfers between devices with their start and end apart: 11, of which 7 were waited for; matrix products, arithmetic and copies ran while one was open for 1% of the time, Pallas kernels for 2%

profile of v5, /device:TPU:1, one launch (start us, length us, event | category | flops | bytes accessed | tf_op | source)
XLA Modules:
  0.0 173.9 jit_solution(8199202818217894618)
XLA Ops:
  1.3 5.4 %shard_map.131 = bf16[16,3,32,512]{3,2,1,0:T(8,128)(2,1)} custom-call(s32[1]{0:T(128)} %bitcast.seq_ref, s32[1]{0:T(128)S(6)} %copy.15.split_ref, f32[1,512]{1,0:T(1,128)} %rates_ref.3, bf16[3,512,512]{2,1,0:T(8,128)(2,1)} %bitcast.21, bf16[512,512]{1,0:T(8,128)(2,1)} %bitcast.27, bf16[512,512]{1,0:T(8,128)(2,1)} %bitcast.29), custom_call_target="tpu_custom_call" | custom-call | flops 1610612736 | bytes 4196352 | tf_op jit(solution)/shard_map/pallas_call | solution.py:319
  6.7 0.0 copy-start
  6.7 7.7 %all-to-all-start = ((bf16[16,3,32,512]{3,2,1,0:T(8,128)(2,1)}), bf16[16,3,32,512]{3,2,1,0:T(8,128)(2,1)S(1)}, u32[]{:S(2)}, u32[]{:S(2)}) async-start(bf16[16,3,32,512]{3,2,1,0:T(8,128)(2,1)} %shard_map.131), calls=%async_computation | async-start | bytes 3145728 | tf_op jit(solution)/shard_map/all_to_all | solution.py:424
  14.5 0.0 copy-start.1
  14.5 5.0 %collective-permute-start = (bf16[384,512]{1,0:T(8,128)(2,1)S(1)}, bf16[384,512]{1,0:T(8,128)(2,1)S(1)}, u32[]{:S(2)}, u32[]{:S(2)}) collective-permute-start(bf16[384,512]{1,0:T(8,128)(2,1)S(1)} %slice_bitcast_fusion.1), channel_id=1, source_target_pairs={{0,4},{4,8},{8,12},{1,5},{5,9},{9,13},{2,6},{6,10},{10,14},{3,7},{... | collective-permute-start | bytes 1179656 | tf_op jit(solution)/shard_map/ppermute | solution.py:420
  19.6 15.5 %all-to-all-done = bf16[16,3,32,512]{3,2,1,0:T(8,128)(2,1)S(1)} async-done(((bf16[16,3,32,512]{3,2,1,0:T(8,128)(2,1)}), bf16[16,3,32,512]{3,2,1,0:T(8,128)(2,1)S(1)}, u32[]{:S(2)}, u32[]{:S(2)}) %all-to-all-start) | async-done | bytes 1572896 | tf_op jit(solution)/shard_map/all_to_all | solution.py:424
  35.1 0.3 reduce_sum.24
  35.4 4.1 %collective-permute-start.1 = (bf16[3,32,512]{2,1,0:T(8,128)(2,1)S(1)}, bf16[3,32,512]{2,1,0:T(8,128)(2,1)S(1)}, u32[]{:S(2)}, u32[]{:S(2)}) collective-permute-start(bf16[3,32,512]{2,1,0:T(8,128)(2,1)S(1)} %reduce_sum.24), channel_id=1, source_target_pairs={{0,4},{4,0},{8,12},{12,8},{1,5},{5,1},{9,13},{13,9},{2,6},{6,2},{1... | collective-permute-start | bytes 294920 | tf_op jit(solution)/shard_map/ppermute | solution.py:430
  39.5 2.0 %collective-permute-done.1 = bf16[3,32,512]{2,1,0:T(8,128)(2,1)S(1)} collective-permute-done((bf16[3,32,512]{2,1,0:T(8,128)(2,1)S(1)}, bf16[3,32,512]{2,1,0:T(8,128)(2,1)S(1)}, u32[]{:S(2)}, u32[]{:S(2)}) %collective-permute-start.1) | collective-permute-done | bytes 98336 | tf_op jit(solution)/shard_map/ppermute | solution.py:430
  41.5 4.6 %collective-permute-start.2 = (bf16[3,32,512]{2,1,0:T(8,128)(2,1)S(1)}, bf16[3,32,512]{2,1,0:T(8,128)(2,1)S(1)}, u32[]{:S(2)}, u32[]{:S(2)}) collective-permute-start(bf16[3,32,512]{2,1,0:T(8,128)(2,1)S(1)} %add_convert_fusion.1.refs_0_), channel_id=1, source_target_pairs={{0,12},{4,8},{8,4},{12,0},{1,13},{5,9},{9,5},{13,1},{2,14},{6,10},... | collective-permute-start | bytes 294920 | tf_op jit(solution)/shard_map/ppermute | solution.py:430
  46.2 2.0 %collective-permute-done.2.refs_1_ = bf16[3,32,512]{2,1,0:T(8,128)(2,1)S(1)} collective-permute-done((bf16[3,32,512]{2,1,0:T(8,128)(2,1)S(1)}, bf16[3,32,512]{2,1,0:T(8,128)(2,1)S(1)}, u32[]{:S(2)}, u32[]{:S(2)}) %collective-permute-start.2) | collective-permute-done | bytes 98336 | tf_op jit(solution)/shard_map/ppermute | solution.py:430
  48.2 1.3 shard_map.132
  49.5 8.2 %all-to-all-start.1 = ((bf16[16,3,32,512]{3,2,1,0:T(8,128)(2,1)}), bf16[16,3,32,512]{3,2,1,0:T(8,128)(2,1)}, u32[]{:S(2)}, u32[]{:S(2)}) async-start(bf16[16,3,32,512]{3,2,1,0:T(8,128)(2,1)} %shard_map.132), calls=%async_computation.1 | async-start | bytes 3145728 | tf_op jit(solution)/shard_map/all_to_all | solution.py:444
  58.3 4.9 %collective-permute-start.3 = (bf16[128,512]{1,0:T(8,128)(2,1)S(1)}, bf16[128,512]{1,0:T(8,128)(2,1)S(1)}, u32[]{:S(2)}, u32[]{:S(2)}) collective-permute-start(bf16[128,512]{1,0:T(8,128)(2,1)S(1)} %slice_bitcast_fusion.3), channel_id=1, source_target_pairs={{0,4},{4,8},{8,12},{1,5},{5,9},{9,13},{2,6},{6,10},{10,14},{3,7},{... | collective-permute-start | bytes 393224 | tf_op jit(solution)/shard_map/ppermute | solution.py:420
  63.3 5.5 %collective-permute-start.4 = (bf16[128,512]{1,0:T(8,128)(2,1)S(1)}, bf16[128,512]{1,0:T(8,128)(2,1)S(1)}, u32[]{:S(2)}, u32[]{:S(2)}) collective-permute-start(bf16[128,512]{1,0:T(8,128)(2,1)S(1)} %slice_bitcast_fusion.2), channel_id=1, source_target_pairs={{0,4},{4,8},{8,12},{1,5},{5,9},{9,13},{2,6},{6,10},{10,14},{3,7},{... | collective-permute-start | bytes 393224 | tf_op jit(solution)/shard_map/ppermute | solution.py:420
  68.9 1.7 collective-permute-done.4.values_b_ref
  70.6 6.1 %all-to-all-done.1.gathered_hbm = bf16[16,3,32,512]{3,2,1,0:T(8,128)(2,1)} async-done(((bf16[16,3,32,512]{3,2,1,0:T(8,128)(2,1)}), bf16[16,3,32,512]{3,2,1,0:T(8,128)(2,1)}, u32[]{:S(2)}, u32[]{:S(2)}) %all-to-all-start.1) | async-done | bytes 1572896 | tf_op jit(solution)/shard_map/all_to_all | solution.py:444
  76.7 11.5 %shard_map.133 = (bf16[16,3,32,512]{3,2,1,0:T(8,128)(2,1)}, bf16[3,512,512]{2,1,0:T(8,128)(2,1)}) custom-call(s32[1]{0:T(128)} %bitcast.seq_ref, s32[1]{0:T(128)S(6)} %copy.15.split_ref, f32[1]{0:T(128)S(6)} %copy.16.step_ref, f32[1,512]{1,0:T(1,128)} %rates_ref.3, bf16[16,3,32,512]{3,2,1,0:T(8,128)(2,1)} %all-to-all-done.1.gathered_hbm, ...), custom_call_target="tpu_custom_call" | custom-call | flops 6442450944 | bytes 7342080 | tf_op jit(solution)/shard_map/pallas_call | solution.py:319
  88.2 6.6 %all-to-all-start.2 = ((bf16[16,3,32,512]{3,2,1,0:T(8,128)(2,1)}), bf16[16,3,32,512]{3,2,1,0:T(8,128)(2,1)}, u32[]{:S(2)}, u32[]{:S(2)}) async-start(bf16[16,3,32,512]{3,2,1,0:T(8,128)(2,1)} %get-tuple-element.28), calls=%async_computation.2 | async-start | bytes 3145728 | tf_op jit(solution)/shard_map/all_to_all | solution.py:424
  94.8 0.0 copy-start.3
  94.8 5.0 %collective-permute-start.5 = (bf16[384,512]{1,0:T(8,128)(2,1)S(1)}, bf16[384,512]{1,0:T(8,128)(2,1)S(1)}, u32[]{:S(2)}, u32[]{:S(2)}) collective-permute-start(bf16[384,512]{1,0:T(8,128)(2,1)S(1)} %slice_bitcast_fusion), channel_id=1, source_target_pairs={{0,4},{4,8},{8,12},{1,5},{5,9},{9,13},{2,6},{6,10},{10,14},{3,7},{... | collective-permute-start | bytes 1179656 | tf_op jit(solution)/shard_map/ppermute | solution.py:420
  99.8 14.9 %all-to-all-done.2 = bf16[16,3,32,512]{3,2,1,0:T(8,128)(2,1)} async-done(((bf16[16,3,32,512]{3,2,1,0:T(8,128)(2,1)}), bf16[16,3,32,512]{3,2,1,0:T(8,128)(2,1)}, u32[]{:S(2)}, u32[]{:S(2)}) %all-to-all-start.2) | async-done | bytes 1572896 | tf_op jit(solution)/shard_map/all_to_all | solution.py:424
  114.7 1.7 reduce_sum.25
  116.4 2.8 %collective-permute-start.6 = (bf16[3,32,512]{2,1,0:T(8,128)(2,1)S(1)}, bf16[3,32,512]{2,1,0:T(8,128)(2,1)S(1)}, u32[]{:S(2)}, u32[]{:S(2)}) collective-permute-start(bf16[3,32,512]{2,1,0:T(8,128)(2,1)S(1)} %reduce_sum.25), channel_id=1, source_target_pairs={{0,4},{4,0},{8,12},{12,8},{1,5},{5,1},{9,13},{13,9},{2,6},{6,2},{1... | collective-permute-start | bytes 294920 | tf_op jit(solution)/shard_map/ppermute | solution.py:430
  119.2 3.8 %shard_map.134.attended_ref = f32[512,512]{1,0:T(8,128)S(1)} custom-call(s32[1]{0:T(128)} %bitcast.seq_ref, s32[16]{0:T(128)S(1)} %copy-done.3, bf16[512,512]{1,0:T(8,128)(2,1)S(1)} %bitcast.24, bf16[512,512]{1,0:T(8,128)(2,1)S(1)} %bitcast.19, bf16[512,512]{1,0:T(8,128)(2,1)S(1)} %bitcast.20, bf16[384,512]{1,0:T(8,128)(2,1)S(1)} %collective-permute-done.keys_a_ref, ...), custom_call_target="tpu_custom_call" | custom-call | flops 1073741824 | bytes 3670016 | tf_op jit(solution)/shard_map/pallas_call | solution.py:319
  123.1 2.3 %collective-permute-start.7 = (bf16[3,32,512]{2,1,0:T(8,128)(2,1)S(1)}, bf16[3,32,512]{2,1,0:T(8,128)(2,1)S(1)}, u32[]{:S(2)}, u32[]{:S(2)}) collective-permute-start(bf16[3,32,512]{2,1,0:T(8,128)(2,1)S(1)} %add_convert_fusion.refs_0_), channel_id=1, source_target_pairs={{0,12},{4,8},{8,4},{12,0},{1,13},{5,9},{9,5},{13,1},{2,14},{6,10},... | collective-permute-start | bytes 294920 | tf_op jit(solution)/shard_map/ppermute | solution.py:430
  125.3 4.1 %collective-permute-done.7.refs_1_ = bf16[3,32,512]{2,1,0:T(8,128)(2,1)S(1)} collective-permute-done((bf16[3,32,512]{2,1,0:T(8,128)(2,1)S(1)}, bf16[3,32,512]{2,1,0:T(8,128)(2,1)S(1)}, u32[]{:S(2)}, u32[]{:S(2)}) %collective-permute-start.7) | collective-permute-done | bytes 98336 | tf_op jit(solution)/shard_map/ppermute | solution.py:430
  129.4 0.1 shard_map.135
  129.6 23.4 %all_to_all.20.gathered_ref = bf16[16,3,32,512]{3,2,1,0:T(8,128)(2,1)S(1)} all-to-all(bf16[16,3,32,512]{3,2,1,0:T(8,128)(2,1)S(1)} %shard_map.135), channel_id=1, replica_groups=mesh['x'=4,'y'=4,'z'=4,'w'=2,'c'=2] {'x','y'}, dimensions={0} | all-to-all | bytes 3145728 | tf_op jit(solution)/shard_map/all_to_all | solution.py:444
  153.0 8.9 %shard_map.136 = (f32[512,512]{1,0:T(8,128)S(1)}, f32[1,512]{1,0:T(1,128)S(1)}, bf16[3,512,512]{2,1,0:T(8,128)(2,1)}) custom-call(s32[1]{0:T(128)} %bitcast.seq_ref, s32[1]{0:T(128)S(6)} %copy.15.split_ref, s32[16]{0:T(128)S(1)} %copy-done.6, f32[1]{0:T(128)S(6)} %copy.16.step_ref, bf16[16,3,32,512]{3,2,1,0:T(8,128)(2,1)S(1)} %all_to_all.20.gathered_ref, ...), custom_call_target="tpu_custom_call" | custom-call | flops 5637144576 | bytes 8914944 | tf_op jit(solution)/shard_map/pallas_call | solution.py:319
  161.9 10.5 %psum.7.energy_ref = f32[1,512]{1,0:T(1,128)S(1)} all-reduce(f32[1,512]{1,0:T(1,128)S(1)} %get-tuple-element.40), channel_id=1, replica_groups=mesh['x'=4,'y'=4,'z'=4,'w'=2,'c'=2] {'w','c'}, use_global_device_ids=true, to_apply=%region_2.0 | all-reduce | flops 512 | bytes 4096 | tf_op jit(solution)/shard_map/psum | solution.py:497
  172.4 1.5 shard_map.137
  (23 shorter events, 0.2 us)
Async XLA Ops:
  6.7 7.7 %copy-start = (bf16[1,512,512]{2,1,0:T(8,128)(2,1)S(1)}, bf16[1,512,512]{2,1,0:T(8,128)(2,1)}, u32[]{:S(2)}) copy-start(bf16[1,512,512]{2,1,0:T(8,128)(2,1)} %param.19) | copy-start | bytes 1572868
  6.7 28.4 %all-to-all-start = ((bf16[16,3,32,512]{3,2,1,0:T(8,128)(2,1)}), bf16[16,3,32,512]{3,2,1,0:T(8,128)(2,1)S(1)}, u32[]{:S(2)}, u32[]{:S(2)}) async-start(bf16[16,3,32,512]{3,2,1,0:T(8,128)(2,1)} %shard_map.131), calls=%async_computation | async-start | bytes 3145728 | tf_op jit(solution)/shard_map/all_to_all | solution.py:424
  14.5 31.7 %copy-start.1 = (bf16[1,512,512]{2,1,0:T(8,128)(2,1)S(1)}, bf16[1,512,512]{2,1,0:T(8,128)(2,1)}, u32[]{:S(2)}) copy-start(bf16[1,512,512]{2,1,0:T(8,128)(2,1)} %param.20) | copy-start | bytes 1572868
  14.5 20.8 %collective-permute-start = (bf16[384,512]{1,0:T(8,128)(2,1)S(1)}, bf16[384,512]{1,0:T(8,128)(2,1)S(1)}, u32[]{:S(2)}, u32[]{:S(2)}) collective-permute-start(bf16[384,512]{1,0:T(8,128)(2,1)S(1)} %slice_bitcast_fusion.1), channel_id=1, source_target_pairs={{0,4},{4,8},{8,12},{1,5},{5,9},{9,13},{2,6},{6,10},{10,14},{3,7},{... | collective-permute-start | bytes 1179656 | tf_op jit(solution)/shard_map/ppermute | solution.py:420
  35.4 6.1 %collective-permute-start.1 = (bf16[3,32,512]{2,1,0:T(8,128)(2,1)S(1)}, bf16[3,32,512]{2,1,0:T(8,128)(2,1)S(1)}, u32[]{:S(2)}, u32[]{:S(2)}) collective-permute-start(bf16[3,32,512]{2,1,0:T(8,128)(2,1)S(1)} %reduce_sum.24), channel_id=1, source_target_pairs={{0,4},{4,0},{8,12},{12,8},{1,5},{5,1},{9,13},{13,9},{2,6},{6,2},{1... | collective-permute-start | bytes 294920 | tf_op jit(solution)/shard_map/ppermute | solution.py:430
  41.5 6.6 %collective-permute-start.2 = (bf16[3,32,512]{2,1,0:T(8,128)(2,1)S(1)}, bf16[3,32,512]{2,1,0:T(8,128)(2,1)S(1)}, u32[]{:S(2)}, u32[]{:S(2)}) collective-permute-start(bf16[3,32,512]{2,1,0:T(8,128)(2,1)S(1)} %add_convert_fusion.1.refs_0_), channel_id=1, source_target_pairs={{0,12},{4,8},{8,4},{12,0},{1,13},{5,9},{9,5},{13,1},{2,14},{6,10},... | collective-permute-start | bytes 294920 | tf_op jit(solution)/shard_map/ppermute | solution.py:430
  49.5 27.2 %all-to-all-start.1 = ((bf16[16,3,32,512]{3,2,1,0:T(8,128)(2,1)}), bf16[16,3,32,512]{3,2,1,0:T(8,128)(2,1)}, u32[]{:S(2)}, u32[]{:S(2)}) async-start(bf16[16,3,32,512]{3,2,1,0:T(8,128)(2,1)} %shard_map.132), calls=%async_computation.1 | async-start | bytes 3145728 | tf_op jit(solution)/shard_map/all_to_all | solution.py:444
  58.3 10.5 %collective-permute-start.3 = (bf16[128,512]{1,0:T(8,128)(2,1)S(1)}, bf16[128,512]{1,0:T(8,128)(2,1)S(1)}, u32[]{:S(2)}, u32[]{:S(2)}) collective-permute-start(bf16[128,512]{1,0:T(8,128)(2,1)S(1)} %slice_bitcast_fusion.3), channel_id=1, source_target_pairs={{0,4},{4,8},{8,12},{1,5},{5,9},{9,13},{2,6},{6,10},{10,14},{3,7},{... | collective-permute-start | bytes 393224 | tf_op jit(solution)/shard_map/ppermute | solution.py:420
  63.3 7.3 %collective-permute-start.4 = (bf16[128,512]{1,0:T(8,128)(2,1)S(1)}, bf16[128,512]{1,0:T(8,128)(2,1)S(1)}, u32[]{:S(2)}, u32[]{:S(2)}) collective-permute-start(bf16[128,512]{1,0:T(8,128)(2,1)S(1)} %slice_bitcast_fusion.2), channel_id=1, source_target_pairs={{0,4},{4,8},{8,12},{1,5},{5,9},{9,13},{2,6},{6,10},{10,14},{3,7},{... | collective-permute-start | bytes 393224 | tf_op jit(solution)/shard_map/ppermute | solution.py:420
  88.2 26.5 %all-to-all-start.2 = ((bf16[16,3,32,512]{3,2,1,0:T(8,128)(2,1)}), bf16[16,3,32,512]{3,2,1,0:T(8,128)(2,1)}, u32[]{:S(2)}, u32[]{:S(2)}) async-start(bf16[16,3,32,512]{3,2,1,0:T(8,128)(2,1)} %get-tuple-element.28), calls=%async_computation.2 | async-start | bytes 3145728 | tf_op jit(solution)/shard_map/all_to_all | solution.py:424
  94.8 24.4 %copy-start.3 = (s32[16]{0:T(128)S(1)}, s32[16]{0:T(128)}, u32[]{:S(2)}) copy-start(s32[16]{0:T(128)} %length_ref.3) | copy-start | bytes 196
  94.8 24.4 %copy-start.5 = (bf16[1,512,512]{2,1,0:T(8,128)(2,1)S(1)}, bf16[1,512,512]{2,1,0:T(8,128)(2,1)}, u32[]{:S(2)}) copy-start(bf16[1,512,512]{2,1,0:T(8,128)(2,1)} %param.18) | copy-start | bytes 1572868
  94.8 21.6 %collective-permute-start.5 = (bf16[384,512]{1,0:T(8,128)(2,1)S(1)}, bf16[384,512]{1,0:T(8,128)(2,1)S(1)}, u32[]{:S(2)}, u32[]{:S(2)}) collective-permute-start(bf16[384,512]{1,0:T(8,128)(2,1)S(1)} %slice_bitcast_fusion), channel_id=1, source_target_pairs={{0,4},{4,8},{8,12},{1,5},{5,9},{9,13},{2,6},{6,10},{10,14},{3,7},{... | collective-permute-start | bytes 1179656 | tf_op jit(solution)/shard_map/ppermute | solution.py:420
  116.4 6.7 %collective-permute-start.6 = (bf16[3,32,512]{2,1,0:T(8,128)(2,1)S(1)}, bf16[3,32,512]{2,1,0:T(8,128)(2,1)S(1)}, u32[]{:S(2)}, u32[]{:S(2)}) collective-permute-start(bf16[3,32,512]{2,1,0:T(8,128)(2,1)S(1)} %reduce_sum.25), channel_id=1, source_target_pairs={{0,4},{4,0},{8,12},{12,8},{1,5},{5,1},{9,13},{13,9},{2,6},{6,2},{1... | collective-permute-start | bytes 294920 | tf_op jit(solution)/shard_map/ppermute | solution.py:430
  123.1 6.3 %collective-permute-start.7 = (bf16[3,32,512]{2,1,0:T(8,128)(2,1)S(1)}, bf16[3,32,512]{2,1,0:T(8,128)(2,1)S(1)}, u32[]{:S(2)}, u32[]{:S(2)}) collective-permute-start(bf16[3,32,512]{2,1,0:T(8,128)(2,1)S(1)} %add_convert_fusion.refs_0_), channel_id=1, source_target_pairs={{0,12},{4,8},{8,4},{12,0},{1,13},{5,9},{9,5},{13,1},{2,14},{6,10},... | collective-permute-start | bytes 294920 | tf_op jit(solution)/shard_map/ppermute | solution.py:430
  129.6 23.4 %copy-start.4 = (bf16[3,1,512,512]{3,2,1,0:T(8,128)(2,1)S(1)}, bf16[3,1,512,512]{3,2,1,0:T(8,128)(2,1)}, u32[]{:S(2)}) copy-start(bf16[3,1,512,512]{3,2,1,0:T(8,128)(2,1)} %param.16) | copy-start | bytes 4718596
  129.6 23.4 %copy-start.6 = (s32[16]{0:T(128)S(1)}, s32[16]{0:T(128)}, u32[]{:S(2)}) copy-start(s32[16]{0:T(128)} %fork_ref.1) | copy-start | bytes 196
  129.6 23.4 %copy-start.7 = (bf16[3,512,512]{2,1,0:T(8,128)(2,1)S(1)}, bf16[3,512,512]{2,1,0:T(8,128)(2,1)}, u32[]{:S(2)}) copy-start(bf16[3,512,512]{2,1,0:T(8,128)(2,1)} %get-tuple-element.38.state_hbm) | copy-start | bytes 4718596
  153.0 19.4 %copy-start.2 = (f32[1,512]{1,0:T(1,128)S(1)}, f32[1,512]{1,0:T(1,128)}, u32[]{:S(2)}) copy-start(f32[1,512]{1,0:T(1,128)} %gain_ref.1) | copy-start | bytes 6148

commit v6 on v5

--- a/solution.py
+++ b/solution.py
@@ -40,7 +40,6 @@
     step = parts_ref.shape[2]
     sent = []
     rows, width = weights[0].shape
-    rate_columns = jnp.tile(column_of(rates), (1, width // 128))
     ready("keys")
     keys = keys_ref[...]
     pushed = None
@@ -56,6 +55,8 @@
         silu = first * gate
         hidden = (silu * third).astype(jnp.bfloat16)
         if start == 0:
+            ready("rates")
+            rate_columns = jnp.tile(column_of(rates()), (1, width // 128))
             ready("values")
             pushed = (rate_columns * values_ref[...].astype(jnp.float32)).astype(jnp.bfloat16)
             ready("second")
@@ -119,22 +120,25 @@
                     out_ref[kind, cut] = (new * (jnp.sqrt(old_mean) * lax.rsqrt(new_mean))).astype(jnp.bfloat16)
 
 
-def masked_rates(rates_ref, seq_ref, split_ref, period):
-    rates = rates_ref[...]
+def place_in_seq():
+    return lax.axis_index(SEQ).astype(jnp.int32)
+
+
+def masked_rates(rates, split_ref, period):
     count = rates.shape[1]
-    positions = seq_ref[0] * count + lax.broadcasted_iota(jnp.int32, rates.shape, 1)
+    positions = place_in_seq() * count + lax.broadcasted_iota(jnp.int32, rates.shape, 1)
     early = positions < split_ref[0]
     return jnp.where(early if period == 0 else jnp.logical_not(early), rates, 0.0)
 
 
 def first_kernel(
-    seq_ref,
     split_ref,
-    rates_ref,
+    rates_hbm,
     weights_hbm,
     keys_hbm,
     values_hbm,
     parts_hbm,
+    rates,
     weights,
     keys,
     values,
@@ -148,25 +152,25 @@
         "third": pltpu.make_async_copy(weights_hbm.at[1], weights.at[1], sems.at[2]),
         "values": pltpu.make_async_copy(values_hbm, values, sems.at[3]),
         "second": pltpu.make_async_copy(weights_hbm.at[2], weights.at[2], sems.at[4]),
+        "rates": pltpu.make_async_copy(rates_hbm, rates, sems.at[5]),
     }
     for copy in copies.values():
         copy.start()
-    rates = masked_rates(rates_ref, seq_ref, split_ref, 0)
     kinds = [weights.at[kind] for kind in range(3)]
-    emit_gradient(kinds, keys, values, rates, parts, parts_hbm, parts_sems, lambda name: copies[name].wait())
+    emit_gradient(kinds, keys, values, lambda: masked_rates(rates[...], split_ref, 0), parts, parts_hbm, parts_sems, lambda name: copies[name].wait())
 
 
 def second_kernel(
-    seq_ref,
     split_ref,
     step_ref,
-    rates_ref,
+    rates_hbm,
     gathered_hbm,
     weights_hbm,
     keys_hbm,
     values_hbm,
     parts_hbm,
     state_hbm,
+    rates,
     weights,
     keys,
     values,
@@ -183,11 +187,13 @@
     fetch_weights = pltpu.make_async_copy(weights_hbm, weights, sems.at[0])
     fetch_keys = pltpu.make_async_copy(keys_hbm, keys, sems.at[1])
     fetch_values = pltpu.make_async_copy(values_hbm, values, sems.at[2])
+    fetch_rates = pltpu.make_async_copy(rates_hbm, rates, sems.at[4])
 
     def begin():
         fetch_weights.start()
         fetch_keys.start()
         fetch_values.start()
+        fetch_rates.start()
 
     def load(kind):
         fetches[kind].wait()
@@ -196,23 +202,26 @@
     emit_update(load, weights, step_ref[0], x_ref, gram_ref, state, begin, fetch_weights.wait)
     keep = pltpu.make_async_copy(state, state_hbm, sems.at[3])
     keep.start()
-    rates = masked_rates(rates_ref, seq_ref, split_ref, 1)
     fetch_keys.wait()
     fetch_values.wait()
-    emit_gradient([state.at[kind] for kind in range(3)], keys, values, rates, parts, parts_hbm, parts_sems)
+    fetch_rates.wait()
+    kinds = [state.at[kind] for kind in range(3)]
+    emit_gradient(kinds, keys, values, lambda: masked_rates(rates[...], split_ref, 1), parts, parts_hbm, parts_sems)
     keep.wait()
 
 
 def attend_kernel(
-    seq_ref, length_ref, query_ref, keys_ref, values_ref, keys_a_ref, keys_b_ref, values_b_ref, values_c_ref, out_ref
+    length_ref, query_ref, keys_ref, values_ref, keys_a_ref, both_b_ref, values_c_ref, out_ref
 ):
     rows, width = query_ref.shape
-    branch = seq_ref[0] // BR_SPAN
-    place = seq_ref[0] % BR_SPAN
+    seq = place_in_seq()
+    branch = seq // BR_SPAN
+    place = seq % BR_SPAN
     live = length_ref[branch] - place * rows
     scale = width ** (-0.5)
-    prior_keys = jnp.concatenate([keys_a_ref[...], keys_b_ref[...]], axis=0)
-    prior_values = jnp.concatenate([values_b_ref[...], values_c_ref[...]], axis=0)
+    rest = rows - keys_a_ref.shape[0]
+    prior_keys = jnp.concatenate([keys_a_ref[...], both_b_ref[:rest]], axis=0)
+    prior_values = jnp.concatenate([both_b_ref[rest:], values_c_ref[...]], axis=0)
     chunk = 128
     for start in range(0, rows, chunk):
         cut = slice(start, start + chunk)
@@ -232,7 +241,6 @@
 
 
 def third_kernel(
-    seq_ref,
     split_ref,
     fork_ref,
     step_ref,
@@ -252,7 +260,7 @@
     sems,
     trunk_total,
 ):
-    fork = fork_ref[seq_ref[0] // BR_SPAN]
+    fork = fork_ref[place_in_seq() // BR_SPAN]
     early = fork < split_ref[0]
     final = jnp.logical_and(jnp.logical_not(early), fork >= trunk_total)
     fetch_old = pltpu.make_async_copy(state_hbm, old, sems.at[0])
@@ -291,9 +299,10 @@
     keep.wait()
 
 
-def last_kernel(seq_ref, length_ref, total_ref, energy_ref, gain_ref, out_ref, width):
+def last_kernel(length_ref, total_ref, energy_ref, gain_ref, out_ref, width):
     rows = total_ref.shape[0]
-    live = length_ref[seq_ref[0] // BR_SPAN] - (seq_ref[0] % BR_SPAN) * rows
+    seq = place_in_seq()
+    live = length_ref[seq // BR_SPAN] - (seq % BR_SPAN) * rows
     slot = lax.broadcasted_iota(jnp.int32, (1, rows), 1)
     inverse = jnp.where(slot < live, lax.rsqrt(energy_ref[...] / width + 1e-06), 0.0)
     columns = jnp.tile(column_of(inverse), (1, total_ref.shape[1] // 128))
@@ -335,21 +344,22 @@
     return pltpu.VMEM(dims, kind)
 
 
-def gradient_first(seq, split, rates, weights, keys, values, parts_shape):
+def gradient_first(split, rates, weights, keys, values, parts_shape):
     scratch = (
+        space(rates.shape, rates.dtype),
         space(weights.shape),
         space(keys.shape),
         space(values.shape),
         space(parts_shape.shape),
-        pltpu.SemaphoreType.DMA((5,)),
+        pltpu.SemaphoreType.DMA((6,)),
         pltpu.SemaphoreType.DMA((3 * keys.shape[0] // CHUNK,)),
     )
     (parts,) = call(
         first_kernel,
-        (seq, split),
-        (rates,),
+        (split,),
         (),
-        (weights, keys, values),
+        (),
+        (rates, weights, keys, values),
         (parts_shape,),
         scratch,
         flops=12 * keys.size * weights.shape[1],
@@ -363,9 +373,10 @@
     return space((kinds, planes, step, width))
 
 
-def update_and_gradient(seq, split, step, gathered, rates, weights, keys, values):
+def update_and_gradient(split, step, gathered, rates, weights, keys, values):
     full = weights.shape
     scratch = (
+        space(rates.shape, rates.dtype),
         space(full),
         space(keys.shape),
         space(values.shape),
@@ -374,16 +385,16 @@
         space(full),
         by_kind(gathered),
         space(gathered.shape),
-        pltpu.SemaphoreType.DMA((4,)),
+        pltpu.SemaphoreType.DMA((5,)),
         pltpu.SemaphoreType.DMA((3,)),
         pltpu.SemaphoreType.DMA((3 * full[1] // CHUNK,)),
     )
     return call(
         second_kernel,
-        (seq, split, step),
-        (rates,),
+        (split, step),
         (),
-        (gathered, weights, keys, values),
+        (),
+        (rates, gathered, weights, keys, values),
         (shape(gathered.shape, jnp.bfloat16), shape(full, jnp.bfloat16)),
         scratch,
         flops=48 * keys.size * full[1],
@@ -391,7 +402,7 @@
     )
 
 
-def update_and_apply(seq, split, forks, step, gathered, weights, state, query, attended, trunk_total):
+def update_and_apply(split, forks, step, gathered, weights, state, query, attended, trunk_total):
     full = weights.shape
     rows, width = query.shape
     scratch = (
@@ -404,7 +415,7 @@
     )
     return call(
         functools.partial(third_kernel, trunk_total=trunk_total),
-        (seq, split, forks, step),
+        (split, forks, step),
         (gathered, attended),
         (shape((rows, width), jnp.float32), shape((1, rows), jnp.float32)),
         (weights, state, query),
@@ -466,38 +477,37 @@
     planes = lax.axis_size(PLANE)
     trunk_total = rows * lax.axis_size(SEQ)
     total_width = width * lax.axis_size(HEAD)
-    seq = lax.axis_index(SEQ).astype(jnp.int32).reshape(1)
     parts_shape = shape((planes, 3, hidden // planes, width), jnp.bfloat16)
     barrier = lax.optimization_barrier
     most = 3 * rows // 4
 
     keys_a = from_behind(own_keys[:most])
-    parts = gradient_first(seq, segment_end, trunk_rates, weights, keys, values, parts_shape)
+    parts = gradient_first(segment_end, trunk_rates, weights, keys, values, parts_shape)
     mine, keys_a = barrier((sum_plane(parts), keys_a))
     copies, _ = sum_depth(mine)
-    copies, rest_keys, rest_values = barrier((copies, own_keys[most:], own_values[: rows - most]))
-    gathered, keys_b, values_b = barrier((spread_plane(copies), from_behind(rest_keys), from_behind(rest_values)))
+    copies, rest = barrier((copies, jnp.concatenate([own_keys[most:], own_values[: rows - most]], axis=0)))
+    gathered, both_b = barrier((spread_plane(copies), from_behind(rest)))
     parts, state = update_and_gradient(
-        seq, segment_end, step_sizes, gathered, trunk_rates, weights, keys, values
+        segment_end, step_sizes, gathered, trunk_rates, weights, keys, values
     )
     parts, rest_values = barrier((parts, own_values[rows - most :]))
     mine, values_c, query = barrier((sum_plane(parts), from_behind(rest_values), query))
     (attended,) = call(
         attend_kernel,
-        (seq, branch_lengths),
-        (query, own_keys, own_values, keys_a, keys_b, values_b, values_c),
+        (branch_lengths,),
+        (query, own_keys, own_values, keys_a, both_b, values_c),
         (shape((rows, width), jnp.float32),),
         flops=8 * rows * rows * width,
     )
     copies, attended = sum_depth(mine, attended)
     gathered = spread_plane(copies)
     total, energy, last = update_and_apply(
-        seq, segment_end, fork_points, step_sizes, gathered, weights, state, query, attended, trunk_total
+        segment_end, fork_points, step_sizes, gathered, weights, state, query, attended, trunk_total
     )
     energy = lax.psum(energy, HEAD)
     (result,) = call(
         functools.partial(last_kernel, width=total_width),
-        (seq, branch_lengths),
+        (branch_lengths,),
         (total, energy, out_gain),
         (shape((rows, width), jnp.bfloat16),),
     )

time: 174 us -> 174 us (level)
  starting transfers between devices: 56.9 us -> 50.1 us
  waiting for transfers between devices: 46.3 us -> 52.4 us
    all_to_all x1, waiting for transfers between devices: 6.11 us -> 11.9 us  [spread_plane(): return lax.all_to_all(copies, PLANE, 0, 0, tiled=False)]
    ppermute x4 -> x3, starting transfers between devices: 20.5 us -> 15.1 us  [from_behind(): lax.ppermute(value, 'z', [(source, source + 1) for source in range(count...]
  transfers between devices with their start and end apart: 11 -> 10, of which waited for: 7 -> 7; matrix products, arithmetic and copies ran while one was open for 1% -> 2% of each run, Pallas kernels for 2% -> 2%
where the time goes in v6:
time: 174 us; the launch traced here: 173 us
  waiting for transfers between devices  52.4 us (30%)
  starting transfers between devices  50.1 us (29%)
  blocking collectives  33.6 us (19%)
  Pallas kernels  31.3 us (18%)
  other arithmetic  3.54 us (2%)
  between operations  2.16 us (1%)
    pallas_call x7, Pallas kernels, call(): pl.pallas_call(kernel, out_shape=(*outs, *held_outs), in_specs=[SMEM] * l...  31.3 us
    all_to_all x2, waiting for transfers between devices, sum_plane(): received = lax.all_to_all(parts, PLANE, 0, 0, tiled=False)  29.2 us
    all_to_all x1, blocking collectives, spread_plane(): return lax.all_to_all(copies, PLANE, 0, 0, tiled=False)  22.4 us
    ppermute x3, starting transfers between devices, from_behind(): lax.ppermute(value, 'z', [(source, source + 1) for source in range(count...  15.1 us
    ppermute x4, starting transfers between devices, swap_depth(): return lax.ppermute(value, 'z', [(i, i ^ flip) for i in range(depth)])  14.9 us
    all_to_all x2, starting transfers between devices, sum_plane(): received = lax.all_to_all(parts, PLANE, 0, 0, tiled=False)  12.8 us
    all_to_all x1, waiting for transfers between devices, spread_plane(): return lax.all_to_all(copies, PLANE, 0, 0, tiled=False)  11.9 us
    psum x1, blocking collectives, per_device(): energy = lax.psum(energy, HEAD)  11.3 us
  transfers between devices with their start and end apart: 10, of which 7 were waited for; matrix products, arithmetic and copies ran while one was open for 2% of the time, Pallas kernels for 2%

profile of v6, /device:TPU:1, one launch (start us, length us, event | category | flops | bytes accessed | tf_op | source)
XLA Modules:
  0.0 173.3 jit_solution(16851933238582590765)
XLA Ops:
  1.3 4.9 %shard_map.131 = bf16[16,3,32,512]{3,2,1,0:T(8,128)(2,1)} custom-call(s32[1]{0:T(128)S(6)} %copy.15.split_ref, f32[1,512]{1,0:T(1,128)} %rates_hbm.3, bf16[3,512,512]{2,1,0:T(8,128)(2,1)} %bitcast.20, bf16[512,512]{1,0:T(8,128)(2,1)} %bitcast.26, bf16[512,512]{1,0:T(8,128)(2,1)} %bitcast.28), custom_call_target="tpu_custom_call" | custom-call | flops 1610612736 | bytes 4196352 | tf_op jit(solution)/shard_map/pallas_call | solution.py:328
  6.2 0.0 copy-start
  6.2 7.7 %all-to-all-start = ((bf16[16,3,32,512]{3,2,1,0:T(8,128)(2,1)}), bf16[16,3,32,512]{3,2,1,0:T(8,128)(2,1)S(1)}, u32[]{:S(2)}, u32[]{:S(2)}) async-start(bf16[16,3,32,512]{3,2,1,0:T(8,128)(2,1)} %shard_map.131), calls=%async_computation | async-start | bytes 3145728 | tf_op jit(solution)/shard_map/all_to_all | solution.py:435
  13.9 0.0 copy-start.1
  14.0 5.0 %collective-permute-start = (bf16[384,512]{1,0:T(8,128)(2,1)S(1)}, bf16[384,512]{1,0:T(8,128)(2,1)S(1)}, u32[]{:S(2)}, u32[]{:S(2)}) collective-permute-start(bf16[384,512]{1,0:T(8,128)(2,1)S(1)} %slice_bitcast_fusion.1), channel_id=1, source_target_pairs={{0,4},{4,8},{8,12},{1,5},{5,9},{9,13},{2,6},{6,10},{10,14},{3,7},{... | collective-permute-start | bytes 1179656 | tf_op jit(solution)/shard_map/ppermute | solution.py:431
  19.1 15.5 %all-to-all-done = bf16[16,3,32,512]{3,2,1,0:T(8,128)(2,1)S(1)} async-done(((bf16[16,3,32,512]{3,2,1,0:T(8,128)(2,1)}), bf16[16,3,32,512]{3,2,1,0:T(8,128)(2,1)S(1)}, u32[]{:S(2)}, u32[]{:S(2)}) %all-to-all-start) | async-done | bytes 1572896 | tf_op jit(solution)/shard_map/all_to_all | solution.py:435
  34.5 0.9 reduce_sum.24
  35.4 3.5 %collective-permute-start.1 = (bf16[3,32,512]{2,1,0:T(8,128)(2,1)}, bf16[3,32,512]{2,1,0:T(8,128)(2,1)S(1)}, u32[]{:S(2)}, u32[]{:S(2)}) collective-permute-start(bf16[3,32,512]{2,1,0:T(8,128)(2,1)} %reduce_sum.24), channel_id=1, source_target_pairs={{0,4},{4,0},{8,12},{12,8},{1,5},{5,1},{9,13},{13,9},{2,6},{6,2},{1... | collective-permute-start | bytes 294920 | tf_op jit(solution)/shard_map/ppermute | solution.py:441
  38.9 2.2 %collective-permute-done.1 = bf16[3,32,512]{2,1,0:T(8,128)(2,1)S(1)} collective-permute-done((bf16[3,32,512]{2,1,0:T(8,128)(2,1)}, bf16[3,32,512]{2,1,0:T(8,128)(2,1)S(1)}, u32[]{:S(2)}, u32[]{:S(2)}) %collective-permute-start.1) | collective-permute-done | bytes 98336 | tf_op jit(solution)/shard_map/ppermute | solution.py:441
  41.1 0.9 add_convert_fusion.1.refs_0_
  42.1 5.1 %collective-permute-start.2 = (bf16[3,32,512]{2,1,0:T(8,128)(2,1)S(1)}, bf16[3,32,512]{2,1,0:T(8,128)(2,1)S(1)}, u32[]{:S(2)}, u32[]{:S(2)}) collective-permute-start(bf16[3,32,512]{2,1,0:T(8,128)(2,1)S(1)} %add_convert_fusion.1.refs_0_), channel_id=1, source_target_pairs={{0,12},{4,8},{8,4},{12,0},{1,13},{5,9},{9,5},{13,1},{2,14},{6,10},... | collective-permute-start | bytes 294920 | tf_op jit(solution)/shard_map/ppermute | solution.py:441
  47.2 2.5 %collective-permute-done.2.refs_1_ = bf16[3,32,512]{2,1,0:T(8,128)(2,1)S(1)} collective-permute-done((bf16[3,32,512]{2,1,0:T(8,128)(2,1)S(1)}, bf16[3,32,512]{2,1,0:T(8,128)(2,1)S(1)}, u32[]{:S(2)}, u32[]{:S(2)}) %collective-permute-start.2) | collective-permute-done | bytes 98336 | tf_op jit(solution)/shard_map/ppermute | solution.py:441
  49.7 1.3 shard_map.132
  51.0 7.3 %all-to-all-start.1 = ((bf16[16,3,32,512]{3,2,1,0:T(8,128)(2,1)}), bf16[16,3,32,512]{3,2,1,0:T(8,128)(2,1)}, u32[]{:S(2)}, u32[]{:S(2)}) async-start(bf16[16,3,32,512]{3,2,1,0:T(8,128)(2,1)} %shard_map.132), calls=%async_computation.1 | async-start | bytes 3145728 | tf_op jit(solution)/shard_map/all_to_all | solution.py:455
  58.3 4.7 %collective-permute-start.3 = (bf16[256,512]{1,0:T(8,128)(2,1)S(1)}, bf16[256,512]{1,0:T(8,128)(2,1)S(1)}, u32[]{:S(2)}, u32[]{:S(2)}) collective-permute-start(bf16[256,512]{1,0:T(8,128)(2,1)S(1)} %pad_maximum_fusion), channel_id=1, source_target_pairs={{0,4},{4,8},{8,12},{1,5},{5,9},{9,13},{2,6},{6,10},{10,14},{3,7},{... | collective-permute-start | bytes 786440 | tf_op jit(solution)/shard_map/ppermute | solution.py:431
  63.7 2.5 %collective-permute-done.3.both_b_ref = bf16[256,512]{1,0:T(8,128)(2,1)S(1)} collective-permute-done((bf16[256,512]{1,0:T(8,128)(2,1)S(1)}, bf16[256,512]{1,0:T(8,128)(2,1)S(1)}, u32[]{:S(2)}, u32[]{:S(2)}) %collective-permute-start.3) | collective-permute-done | bytes 262176 | tf_op jit(solution)/shard_map/ppermute | solution.py:431
  66.2 11.9 %all-to-all-done.1.gathered_hbm = bf16[16,3,32,512]{3,2,1,0:T(8,128)(2,1)} async-done(((bf16[16,3,32,512]{3,2,1,0:T(8,128)(2,1)}), bf16[16,3,32,512]{3,2,1,0:T(8,128)(2,1)}, u32[]{:S(2)}, u32[]{:S(2)}) %all-to-all-start.1) | async-done | bytes 1572896 | tf_op jit(solution)/shard_map/all_to_all | solution.py:455
  78.1 10.8 %shard_map.133 = (bf16[16,3,32,512]{3,2,1,0:T(8,128)(2,1)}, bf16[3,512,512]{2,1,0:T(8,128)(2,1)}) custom-call(s32[1]{0:T(128)S(6)} %copy.15.split_ref, f32[1]{0:T(128)S(6)} %copy.16.step_ref, f32[1,512]{1,0:T(1,128)} %rates_hbm.3, bf16[16,3,32,512]{3,2,1,0:T(8,128)(2,1)} %all-to-all-done.1.gathered_hbm, bf16[3,512,512]{2,1,0:T(8,128)(2,1)} %bitcast.21, ...), custom_call_target="tpu_custom_call" | custom-call | flops 6442450944 | bytes 7342080 | tf_op jit(solution)/shard_map/pallas_call | solution.py:328
  88.9 5.1 %all-to-all-start.2 = ((bf16[16,3,32,512]{3,2,1,0:T(8,128)(2,1)}), bf16[16,3,32,512]{3,2,1,0:T(8,128)(2,1)}, u32[]{:S(2)}, u32[]{:S(2)}) async-start(bf16[16,3,32,512]{3,2,1,0:T(8,128)(2,1)} %get-tuple-element.25), calls=%async_computation.2 | async-start | bytes 3145728 | tf_op jit(solution)/shard_map/all_to_all | solution.py:435
  94.0 0.0 copy-start.5
  94.0 5.3 %collective-permute-start.4 = (bf16[384,512]{1,0:T(8,128)(2,1)S(1)}, bf16[384,512]{1,0:T(8,128)(2,1)S(1)}, u32[]{:S(2)}, u32[]{:S(2)}) collective-permute-start(bf16[384,512]{1,0:T(8,128)(2,1)S(1)} %slice_bitcast_fusion), channel_id=1, source_target_pairs={{0,4},{4,8},{8,12},{1,5},{5,9},{9,13},{2,6},{6,10},{10,14},{3,7},{... | collective-permute-start | bytes 1179656 | tf_op jit(solution)/shard_map/ppermute | solution.py:431
  99.3 13.7 %all-to-all-done.2 = bf16[16,3,32,512]{3,2,1,0:T(8,128)(2,1)} async-done(((bf16[16,3,32,512]{3,2,1,0:T(8,128)(2,1)}), bf16[16,3,32,512]{3,2,1,0:T(8,128)(2,1)}, u32[]{:S(2)}, u32[]{:S(2)}) %all-to-all-start.2) | async-done | bytes 1572896 | tf_op jit(solution)/shard_map/all_to_all | solution.py:435
  113.1 1.7 reduce_sum.25
  114.7 4.0 %collective-permute-start.5 = (bf16[3,32,512]{2,1,0:T(8,128)(2,1)S(1)}, bf16[3,32,512]{2,1,0:T(8,128)(2,1)S(1)}, u32[]{:S(2)}, u32[]{:S(2)}) collective-permute-start(bf16[3,32,512]{2,1,0:T(8,128)(2,1)S(1)} %reduce_sum.25), channel_id=1, source_target_pairs={{0,4},{4,0},{8,12},{12,8},{1,5},{5,1},{9,13},{13,9},{2,6},{6,2},{1... | collective-permute-start | bytes 294920 | tf_op jit(solution)/shard_map/ppermute | solution.py:441
  118.8 3.8 %shard_map.134.attended_ref = f32[512,512]{1,0:T(8,128)S(1)} custom-call(s32[16]{0:T(128)S(1)} %copy-done.3, bf16[512,512]{1,0:T(8,128)(2,1)S(1)} %bitcast.23, bf16[512,512]{1,0:T(8,128)(2,1)S(1)} %bitcast.18, bf16[512,512]{1,0:T(8,128)(2,1)S(1)} %bitcast.19, bf16[384,512]{1,0:T(8,128)(2,1)S(1)} %collective-permute-done.keys_a_ref, ...), custom_call_target="tpu_custom_call" | custom-call | flops 1073741824 | bytes 3670016 | tf_op jit(solution)/shard_map/pallas_call | solution.py:328
  122.7 2.3 %collective-permute-start.6 = (bf16[3,32,512]{2,1,0:T(8,128)(2,1)S(1)}, bf16[3,32,512]{2,1,0:T(8,128)(2,1)S(1)}, u32[]{:S(2)}, u32[]{:S(2)}) collective-permute-start(bf16[3,32,512]{2,1,0:T(8,128)(2,1)S(1)} %add_convert_fusion.refs_0_), channel_id=1, source_target_pairs={{0,12},{4,8},{8,4},{12,0},{1,13},{5,9},{9,5},{13,1},{2,14},{6,10},... | collective-permute-start | bytes 294920 | tf_op jit(solution)/shard_map/ppermute | solution.py:441
  124.9 4.1 %collective-permute-done.6.refs_1_ = bf16[3,32,512]{2,1,0:T(8,128)(2,1)S(1)} collective-permute-done((bf16[3,32,512]{2,1,0:T(8,128)(2,1)S(1)}, bf16[3,32,512]{2,1,0:T(8,128)(2,1)S(1)}, u32[]{:S(2)}, u32[]{:S(2)}) %collective-permute-start.6) | collective-permute-done | bytes 98336 | tf_op jit(solution)/shard_map/ppermute | solution.py:441
  129.0 0.1 shard_map.135
  129.2 22.4 %all_to_all.20.gathered_ref = bf16[16,3,32,512]{3,2,1,0:T(8,128)(2,1)S(1)} all-to-all(bf16[16,3,32,512]{3,2,1,0:T(8,128)(2,1)S(1)} %shard_map.135), channel_id=1, replica_groups=mesh['x'=4,'y'=4,'z'=4,'w'=2,'c'=2] {'x','y'}, dimensions={0} | all-to-all | bytes 3145728 | tf_op jit(solution)/shard_map/all_to_all | solution.py:455
  151.6 8.9 %shard_map.136 = (f32[512,512]{1,0:T(8,128)S(1)}, f32[1,512]{1,0:T(1,128)S(1)}, bf16[3,512,512]{2,1,0:T(8,128)(2,1)}) custom-call(s32[1]{0:T(128)S(6)} %copy.15.split_ref, s32[16]{0:T(128)S(1)} %copy-done.6, f32[1]{0:T(128)S(6)} %copy.16.step_ref, bf16[16,3,32,512]{3,2,1,0:T(8,128)(2,1)S(1)} %all_to_all.20.gathered_ref, ...), custom_call_target="tpu_custom_call" | custom-call | flops 5637144576 | bytes 8914944 | tf_op jit(solution)/shard_map/pallas_call | solution.py:328
  160.5 11.3 %psum.7.energy_ref = f32[1,512]{1,0:T(1,128)S(1)} all-reduce(f32[1,512]{1,0:T(1,128)S(1)} %get-tuple-element.36), channel_id=1, replica_groups=mesh['x'=4,'y'=4,'z'=4,'w'=2,'c'=2] {'w','c'}, use_global_device_ids=true, to_apply=%region_2.0 | all-reduce | flops 512 | bytes 4096 | tf_op jit(solution)/shard_map/psum | solution.py:507
  171.8 1.5 shard_map.137
  (22 shorter events, 0.2 us)
Async XLA Ops:
  6.2 7.8 %copy-start = (bf16[1,512,512]{2,1,0:T(8,128)(2,1)S(1)}, bf16[1,512,512]{2,1,0:T(8,128)(2,1)}, u32[]{:S(2)}) copy-start(bf16[1,512,512]{2,1,0:T(8,128)(2,1)} %param.19) | copy-start | bytes 1572868
  6.2 28.4 %all-to-all-start = ((bf16[16,3,32,512]{3,2,1,0:T(8,128)(2,1)}), bf16[16,3,32,512]{3,2,1,0:T(8,128)(2,1)S(1)}, u32[]{:S(2)}, u32[]{:S(2)}) async-start(bf16[16,3,32,512]{3,2,1,0:T(8,128)(2,1)} %shard_map.131), calls=%async_computation | async-start | bytes 3145728 | tf_op jit(solution)/shard_map/all_to_all | solution.py:435
  13.9 25.0 %copy-start.1 = (bf16[1,512,512]{2,1,0:T(8,128)(2,1)S(1)}, bf16[1,512,512]{2,1,0:T(8,128)(2,1)}, u32[]{:S(2)}) copy-start(bf16[1,512,512]{2,1,0:T(8,128)(2,1)} %param.20) | copy-start | bytes 1572868
  14.0 21.5 %collective-permute-start = (bf16[384,512]{1,0:T(8,128)(2,1)S(1)}, bf16[384,512]{1,0:T(8,128)(2,1)S(1)}, u32[]{:S(2)}, u32[]{:S(2)}) collective-permute-start(bf16[384,512]{1,0:T(8,128)(2,1)S(1)} %slice_bitcast_fusion.1), channel_id=1, source_target_pairs={{0,4},{4,8},{8,12},{1,5},{5,9},{9,13},{2,6},{6,10},{10,14},{3,7},{... | collective-permute-start | bytes 1179656 | tf_op jit(solution)/shard_map/ppermute | solution.py:431
  35.4 5.7 %collective-permute-start.1 = (bf16[3,32,512]{2,1,0:T(8,128)(2,1)}, bf16[3,32,512]{2,1,0:T(8,128)(2,1)S(1)}, u32[]{:S(2)}, u32[]{:S(2)}) collective-permute-start(bf16[3,32,512]{2,1,0:T(8,128)(2,1)} %reduce_sum.24), channel_id=1, source_target_pairs={{0,4},{4,0},{8,12},{12,8},{1,5},{5,1},{9,13},{13,9},{2,6},{6,2},{1... | collective-permute-start | bytes 294920 | tf_op jit(solution)/shard_map/ppermute | solution.py:441
  42.1 7.6 %collective-permute-start.2 = (bf16[3,32,512]{2,1,0:T(8,128)(2,1)S(1)}, bf16[3,32,512]{2,1,0:T(8,128)(2,1)S(1)}, u32[]{:S(2)}, u32[]{:S(2)}) collective-permute-start(bf16[3,32,512]{2,1,0:T(8,128)(2,1)S(1)} %add_convert_fusion.1.refs_0_), channel_id=1, source_target_pairs={{0,12},{4,8},{8,4},{12,0},{1,13},{5,9},{9,5},{13,1},{2,14},{6,10},... | collective-permute-start | bytes 294920 | tf_op jit(solution)/shard_map/ppermute | solution.py:441
  51.0 27.1 %all-to-all-start.1 = ((bf16[16,3,32,512]{3,2,1,0:T(8,128)(2,1)}), bf16[16,3,32,512]{3,2,1,0:T(8,128)(2,1)}, u32[]{:S(2)}, u32[]{:S(2)}) async-start(bf16[16,3,32,512]{3,2,1,0:T(8,128)(2,1)} %shard_map.132), calls=%async_computation.1 | async-start | bytes 3145728 | tf_op jit(solution)/shard_map/all_to_all | solution.py:455
  58.3 7.8 %collective-permute-start.3 = (bf16[256,512]{1,0:T(8,128)(2,1)S(1)}, bf16[256,512]{1,0:T(8,128)(2,1)S(1)}, u32[]{:S(2)}, u32[]{:S(2)}) collective-permute-start(bf16[256,512]{1,0:T(8,128)(2,1)S(1)} %pad_maximum_fusion), channel_id=1, source_target_pairs={{0,4},{4,8},{8,12},{1,5},{5,9},{9,13},{2,6},{6,10},{10,14},{3,7},{... | collective-permute-start | bytes 786440 | tf_op jit(solution)/shard_map/ppermute | solution.py:431
  88.9 24.1 %all-to-all-start.2 = ((bf16[16,3,32,512]{3,2,1,0:T(8,128)(2,1)}), bf16[16,3,32,512]{3,2,1,0:T(8,128)(2,1)}, u32[]{:S(2)}, u32[]{:S(2)}) async-start(bf16[16,3,32,512]{3,2,1,0:T(8,128)(2,1)} %get-tuple-element.25), calls=%async_computation.2 | async-start | bytes 3145728 | tf_op jit(solution)/shard_map/all_to_all | solution.py:435
  94.0 24.8 %copy-start.3 = (s32[16]{0:T(128)S(1)}, s32[16]{0:T(128)}, u32[]{:S(2)}) copy-start(s32[16]{0:T(128)} %length_ref.3) | copy-start | bytes 196
  94.0 24.8 %copy-start.5 = (bf16[1,512,512]{2,1,0:T(8,128)(2,1)S(1)}, bf16[1,512,512]{2,1,0:T(8,128)(2,1)}, u32[]{:S(2)}) copy-start(bf16[1,512,512]{2,1,0:T(8,128)(2,1)} %param.18) | copy-start | bytes 1572868
  94.0 20.7 %collective-permute-start.4 = (bf16[384,512]{1,0:T(8,128)(2,1)S(1)}, bf16[384,512]{1,0:T(8,128)(2,1)S(1)}, u32[]{:S(2)}, u32[]{:S(2)}) collective-permute-start(bf16[384,512]{1,0:T(8,128)(2,1)S(1)} %slice_bitcast_fusion), channel_id=1, source_target_pairs={{0,4},{4,8},{8,12},{1,5},{5,9},{9,13},{2,6},{6,10},{10,14},{3,7},{... | collective-permute-start | bytes 1179656 | tf_op jit(solution)/shard_map/ppermute | solution.py:431
  114.7 7.9 %collective-permute-start.5 = (bf16[3,32,512]{2,1,0:T(8,128)(2,1)S(1)}, bf16[3,32,512]{2,1,0:T(8,128)(2,1)S(1)}, u32[]{:S(2)}, u32[]{:S(2)}) collective-permute-start(bf16[3,32,512]{2,1,0:T(8,128)(2,1)S(1)} %reduce_sum.25), channel_id=1, source_target_pairs={{0,4},{4,0},{8,12},{12,8},{1,5},{5,1},{9,13},{13,9},{2,6},{6,2},{1... | collective-permute-start | bytes 294920 | tf_op jit(solution)/shard_map/ppermute | solution.py:441
  122.7 6.4 %collective-permute-start.6 = (bf16[3,32,512]{2,1,0:T(8,128)(2,1)S(1)}, bf16[3,32,512]{2,1,0:T(8,128)(2,1)S(1)}, u32[]{:S(2)}, u32[]{:S(2)}) collective-permute-start(bf16[3,32,512]{2,1,0:T(8,128)(2,1)S(1)} %add_convert_fusion.refs_0_), channel_id=1, source_target_pairs={{0,12},{4,8},{8,4},{12,0},{1,13},{5,9},{9,5},{13,1},{2,14},{6,10},... | collective-permute-start | bytes 294920 | tf_op jit(solution)/shard_map/ppermute | solution.py:441
  129.2 22.4 %copy-start.4 = (bf16[3,1,512,512]{3,2,1,0:T(8,128)(2,1)S(1)}, bf16[3,1,512,512]{3,2,1,0:T(8,128)(2,1)}, u32[]{:S(2)}) copy-start(bf16[3,1,512,512]{3,2,1,0:T(8,128)(2,1)} %param.16) | copy-start | bytes 4718596
  129.2 22.4 %copy-start.6 = (s32[16]{0:T(128)S(1)}, s32[16]{0:T(128)}, u32[]{:S(2)}) copy-start(s32[16]{0:T(128)} %fork_ref.1) | copy-start | bytes 196
  129.2 22.4 %copy-start.7 = (bf16[3,512,512]{2,1,0:T(8,128)(2,1)S(1)}, bf16[3,512,512]{2,1,0:T(8,128)(2,1)}, u32[]{:S(2)}) copy-start(bf16[3,512,512]{2,1,0:T(8,128)(2,1)} %get-tuple-element.34.state_hbm) | copy-start | bytes 4718596
  151.6 20.2 %copy-start.2 = (f32[1,512]{1,0:T(1,128)S(1)}, f32[1,512]{1,0:T(1,128)}, u32[]{:S(2)}) copy-start(f32[1,512]{1,0:T(1,128)} %gain_ref.1) | copy-start | bytes 6148

commit v7 on v6

--- a/solution.py
+++ b/solution.py
@@ -19,7 +19,7 @@
 VMEM_BYTES = 24 * 1024 * 1024
 WHOLE_VMEM = 60 * 1024 * 1024
 LAST_VMEM = 46 * 1024 * 1024
-SECOND_VMEM = 60 * 1024 * 1024
+SECOND_VMEM = 61 * 1024 * 1024
 CHUNK = 256
 UPDATE_CHUNK = 512
 
@@ -211,7 +211,7 @@
 
 
 def attend_kernel(
-    length_ref, query_ref, keys_ref, values_ref, keys_a_ref, both_b_ref, values_c_ref, out_ref
+    length_ref, query_ref, keys_ref, values_ref, keys_a_ref, keys_b_ref, values_b_ref, values_c_ref, out_ref
 ):
     rows, width = query_ref.shape
     seq = place_in_seq()
@@ -219,9 +219,8 @@
     place = seq % BR_SPAN
     live = length_ref[branch] - place * rows
     scale = width ** (-0.5)
-    rest = rows - keys_a_ref.shape[0]
-    prior_keys = jnp.concatenate([keys_a_ref[...], both_b_ref[:rest]], axis=0)
-    prior_values = jnp.concatenate([both_b_ref[rest:], values_c_ref[...]], axis=0)
+    prior_keys = jnp.concatenate([keys_a_ref[...], keys_b_ref[...]], axis=0)
+    prior_values = jnp.concatenate([values_b_ref[...], values_c_ref[...]], axis=0)
     chunk = 128
     for start in range(0, rows, chunk):
         cut = slice(start, start + chunk)
@@ -318,6 +317,10 @@
         refs[-1][slot] = total
 
 
+def plane_kernel(received_ref, mine_ref):
+    mine_ref[...] = jnp.sum(received_ref[...].astype(jnp.float32), axis=0).astype(jnp.bfloat16)
+
+
 SMEM = pl.BlockSpec(memory_space=pltpu.SMEM)
 VMEM = pl.BlockSpec(memory_space=pltpu.VMEM)
 HBM = pl.BlockSpec(memory_space=pltpu.HBM)
@@ -429,6 +432,12 @@
 def from_behind(value):
     count = lax.axis_size("z")
     return lax.ppermute(value, "z", [(source, source + 1) for source in range(count - 1)])
+
+
+def sum_plane_in_kernel(parts):
+    received = lax.all_to_all(parts, PLANE, 0, 0, tiled=False)
+    (mine,) = call(plane_kernel, (), (received,), (shape(received.shape[1:], jnp.bfloat16),))
+    return mine
 
 
 def sum_plane(parts):
@@ -485,17 +494,17 @@
     parts = gradient_first(segment_end, trunk_rates, weights, keys, values, parts_shape)
     mine, keys_a = barrier((sum_plane(parts), keys_a))
     copies, _ = sum_depth(mine)
-    copies, rest = barrier((copies, jnp.concatenate([own_keys[most:], own_values[: rows - most]], axis=0)))
-    gathered, both_b = barrier((spread_plane(copies), from_behind(rest)))
+    copies, rest_keys, rest_values = barrier((copies, own_keys[most:], own_values[: rows - most]))
+    gathered, keys_b, values_b = barrier((spread_plane(copies), from_behind(rest_keys), from_behind(rest_values)))
     parts, state = update_and_gradient(
         segment_end, step_sizes, gathered, trunk_rates, weights, keys, values
     )
     parts, rest_values = barrier((parts, own_values[rows - most :]))
-    mine, values_c, query = barrier((sum_plane(parts), from_behind(rest_values), query))
+    mine, values_c, query = barrier((sum_plane_in_kernel(parts), from_behind(rest_values), query))
     (attended,) = call(
         attend_kernel,
         (branch_lengths,),
-        (query, own_keys, own_values, keys_a, both_b, values_c),
+        (query, own_keys, own_values, keys_a, keys_b, values_b, values_c),
         (shape((rows, width), jnp.float32),),
         flops=8 * rows * rows * width,
     )

time: 174 us -> 173 us (level)
  waiting for transfers between devices: 52.4 us -> 45.1 us
  starting transfers between devices: 50.1 us -> 57 us
  other arithmetic: 3.54 us -> 0.31 us
    all_to_all x0 -> x1, waiting for transfers between devices: none -> 14.4 us  [sum_plane_in_kernel(): received = lax.all_to_all(parts, PLANE, 0, 0, tiled=False)]
    all_to_all x2 -> x1, waiting for transfers between devices: 29.2 us -> 15.5 us  [sum_plane(): received = lax.all_to_all(parts, PLANE, 0, 0, tiled=False)]
    all_to_all x0 -> x1, starting transfers between devices: none -> 6.55 us  [sum_plane_in_kernel(): received = lax.all_to_all(parts, PLANE, 0, 0, tiled=False)]
    ppermute x3 -> x4, starting transfers between devices: 15.1 us -> 21.2 us  [from_behind(): lax.ppermute(value, 'z', [(source, source + 1) for source in range(count...]
    all_to_all x1, waiting for transfers between devices: 11.9 us -> 6.16 us  [spread_plane(): return lax.all_to_all(copies, PLANE, 0, 0, tiled=False)]
    all_to_all x2 -> x1, starting transfers between devices: 12.8 us -> 7.73 us  [sum_plane(): received = lax.all_to_all(parts, PLANE, 0, 0, tiled=False)]
    reduce_sum x2 -> x1, other arithmetic: 2.57 us -> 0.26 us  [sum_plane(): return jnp.sum(received.astype(jnp.float32), axis=0).astype(jnp.bfloat16)]
    pallas_call x7 -> x8, Pallas kernels: 31.3 us -> 32 us  [call(): pl.pallas_call(kernel, out_shape=(*outs, *held_outs), in_specs=[SMEM] * l...]
  transfers between devices with their start and end apart: 10 -> 11, of which waited for: 7 -> 7; matrix products, arithmetic and copies ran while one was open for 2% -> 1% of each run, Pallas kernels for 2% -> 3%
where the time goes in v7:
time: 173 us
  starting transfers between devices  57 us (33%)
  waiting for transfers between devices  45.1 us (26%)
  blocking collectives  35.1 us (20%)
  Pallas kernels  32 us (18%)
  between operations  2.18 us (1%)
    pallas_call x8, Pallas kernels, call(): pl.pallas_call(kernel, out_shape=(*outs, *held_outs), in_specs=[SMEM] * l...  32 us
    all_to_all x1, blocking collectives, spread_plane(): return lax.all_to_all(copies, PLANE, 0, 0, tiled=False)  23.6 us
    ppermute x4, starting transfers between devices, from_behind(): lax.ppermute(value, 'z', [(source, source + 1) for source in range(count...  21.2 us
    all_to_all x1, waiting for transfers between devices, sum_plane(): received = lax.all_to_all(parts, PLANE, 0, 0, tiled=False)  15.5 us
    all_to_all x1, waiting for transfers between devices, sum_plane_in_kernel(): received = lax.all_to_all(parts, PLANE, 0, 0, tiled=False)  14.4 us
    ppermute x4, starting transfers between devices, swap_depth(): return lax.ppermute(value, 'z', [(i, i ^ flip) for i in range(depth)])  13.4 us
    psum x1, blocking collectives, per_device(): energy = lax.psum(energy, HEAD)  11.4 us
    all_to_all x1, starting transfers between devices, spread_plane(): return lax.all_to_all(copies, PLANE, 0, 0, tiled=False)  8.21 us
  transfers between devices with their start and end apart: 11, of which 7 were waited for; matrix products, arithmetic and copies ran while one was open for 1% of the time, Pallas kernels for 3%

profile of v7, /device:TPU:1, one launch (start us, length us, event | category | flops | bytes accessed | tf_op | source)
XLA Modules:
  0.0 172.6 jit_solution(16711739420412986361)
XLA Ops:
  1.3 4.9 %shard_map.131 = bf16[16,3,32,512]{3,2,1,0:T(8,128)(2,1)} custom-call(s32[1]{0:T(128)S(6)} %copy.15.split_ref, f32[1,512]{1,0:T(1,128)} %rates_hbm.3, bf16[3,512,512]{2,1,0:T(8,128)(2,1)} %bitcast.20, bf16[512,512]{1,0:T(8,128)(2,1)} %bitcast.26, bf16[512,512]{1,0:T(8,128)(2,1)} %bitcast.28), custom_call_target="tpu_custom_call" | custom-call | flops 1610612736 | bytes 4196352 | tf_op jit(solution)/shard_map/pallas_call | solution.py:331
  6.2 0.0 copy-start
  6.2 7.7 %all-to-all-start = ((bf16[16,3,32,512]{3,2,1,0:T(8,128)(2,1)}), bf16[16,3,32,512]{3,2,1,0:T(8,128)(2,1)S(1)}, u32[]{:S(2)}, u32[]{:S(2)}) async-start(bf16[16,3,32,512]{3,2,1,0:T(8,128)(2,1)} %shard_map.131), calls=%async_computation | async-start | bytes 3145728 | tf_op jit(solution)/shard_map/all_to_all | solution.py:444
  13.9 0.0 copy-start.1
  14.0 5.0 %collective-permute-start = (bf16[384,512]{1,0:T(8,128)(2,1)S(1)}, bf16[384,512]{1,0:T(8,128)(2,1)S(1)}, u32[]{:S(2)}, u32[]{:S(2)}) collective-permute-start(bf16[384,512]{1,0:T(8,128)(2,1)S(1)} %slice_bitcast_fusion.1), channel_id=1, source_target_pairs={{0,4},{4,8},{8,12},{1,5},{5,9},{9,13},{2,6},{6,10},{10,14},{3,7},{... | collective-permute-start | bytes 1179656 | tf_op jit(solution)/shard_map/ppermute | solution.py:434
  19.0 15.5 %all-to-all-done = bf16[16,3,32,512]{3,2,1,0:T(8,128)(2,1)S(1)} async-done(((bf16[16,3,32,512]{3,2,1,0:T(8,128)(2,1)}), bf16[16,3,32,512]{3,2,1,0:T(8,128)(2,1)S(1)}, u32[]{:S(2)}, u32[]{:S(2)}) %all-to-all-start) | async-done | bytes 1572896 | tf_op jit(solution)/shard_map/all_to_all | solution.py:444
  34.5 0.3 reduce_sum.12
  34.8 4.1 %collective-permute-start.1 = (bf16[3,32,512]{2,1,0:T(8,128)(2,1)S(1)}, bf16[3,32,512]{2,1,0:T(8,128)(2,1)S(1)}, u32[]{:S(2)}, u32[]{:S(2)}) collective-permute-start(bf16[3,32,512]{2,1,0:T(8,128)(2,1)S(1)} %reduce_sum.12), channel_id=1, source_target_pairs={{0,4},{4,0},{8,12},{12,8},{1,5},{5,1},{9,13},{13,9},{2,6},{6,2},{1... | collective-permute-start | bytes 294920 | tf_op jit(solution)/shard_map/ppermute | solution.py:450
  38.9 2.0 %collective-permute-done.1 = bf16[3,32,512]{2,1,0:T(8,128)(2,1)S(1)} collective-permute-done((bf16[3,32,512]{2,1,0:T(8,128)(2,1)S(1)}, bf16[3,32,512]{2,1,0:T(8,128)(2,1)S(1)}, u32[]{:S(2)}, u32[]{:S(2)}) %collective-permute-start.1) | collective-permute-done | bytes 98336 | tf_op jit(solution)/shard_map/ppermute | solution.py:450
  41.0 4.6 %collective-permute-start.2 = (bf16[3,32,512]{2,1,0:T(8,128)(2,1)S(1)}, bf16[3,32,512]{2,1,0:T(8,128)(2,1)S(1)}, u32[]{:S(2)}, u32[]{:S(2)}) collective-permute-start(bf16[3,32,512]{2,1,0:T(8,128)(2,1)S(1)} %add_convert_fusion.1.refs_0_), channel_id=1, source_target_pairs={{0,12},{4,8},{8,4},{12,0},{1,13},{5,9},{9,5},{13,1},{2,14},{6,10},... | collective-permute-start | bytes 294920 | tf_op jit(solution)/shard_map/ppermute | solution.py:450
  45.6 2.0 %collective-permute-done.2.refs_1_ = bf16[3,32,512]{2,1,0:T(8,128)(2,1)S(1)} collective-permute-done((bf16[3,32,512]{2,1,0:T(8,128)(2,1)S(1)}, bf16[3,32,512]{2,1,0:T(8,128)(2,1)S(1)}, u32[]{:S(2)}, u32[]{:S(2)}) %collective-permute-start.2) | collective-permute-done | bytes 98336 | tf_op jit(solution)/shard_map/ppermute | solution.py:450
  47.6 1.3 shard_map.132
  48.9 8.2 %all-to-all-start.1 = ((bf16[16,3,32,512]{3,2,1,0:T(8,128)(2,1)}), bf16[16,3,32,512]{3,2,1,0:T(8,128)(2,1)}, u32[]{:S(2)}, u32[]{:S(2)}) async-start(bf16[16,3,32,512]{3,2,1,0:T(8,128)(2,1)} %shard_map.132), calls=%async_computation.1 | async-start | bytes 3145728 | tf_op jit(solution)/shard_map/all_to_all | solution.py:464
  57.8 4.9 %collective-permute-start.3 = (bf16[128,512]{1,0:T(8,128)(2,1)S(1)}, bf16[128,512]{1,0:T(8,128)(2,1)S(1)}, u32[]{:S(2)}, u32[]{:S(2)}) collective-permute-start(bf16[128,512]{1,0:T(8,128)(2,1)S(1)} %slice_bitcast_fusion.3), channel_id=1, source_target_pairs={{0,4},{4,8},{8,12},{1,5},{5,9},{9,13},{2,6},{6,10},{10,14},{3,7},{... | collective-permute-start | bytes 393224 | tf_op jit(solution)/shard_map/ppermute | solution.py:434
  62.7 5.5 %collective-permute-start.4 = (bf16[128,512]{1,0:T(8,128)(2,1)S(1)}, bf16[128,512]{1,0:T(8,128)(2,1)S(1)}, u32[]{:S(2)}, u32[]{:S(2)}) collective-permute-start(bf16[128,512]{1,0:T(8,128)(2,1)S(1)} %slice_bitcast_fusion.2), channel_id=1, source_target_pairs={{0,4},{4,8},{8,12},{1,5},{5,9},{9,13},{2,6},{6,10},{10,14},{3,7},{... | collective-permute-start | bytes 393224 | tf_op jit(solution)/shard_map/ppermute | solution.py:434
  68.3 0.8 slice_bitcast_fusion
  69.0 1.0 collective-permute-done.4.values_b_ref
  70.0 6.2 %all-to-all-done.1.gathered_hbm = bf16[16,3,32,512]{3,2,1,0:T(8,128)(2,1)} async-done(((bf16[16,3,32,512]{3,2,1,0:T(8,128)(2,1)}), bf16[16,3,32,512]{3,2,1,0:T(8,128)(2,1)}, u32[]{:S(2)}, u32[]{:S(2)}) %all-to-all-start.1) | async-done | bytes 1572896 | tf_op jit(solution)/shard_map/all_to_all | solution.py:464
  76.2 10.8 %shard_map.133 = (bf16[16,3,32,512]{3,2,1,0:T(8,128)(2,1)}, bf16[3,512,512]{2,1,0:T(8,128)(2,1)}) custom-call(s32[1]{0:T(128)S(6)} %copy.15.split_ref, f32[1]{0:T(128)S(6)} %copy.16.step_ref, f32[1,512]{1,0:T(1,128)} %rates_hbm.3, bf16[16,3,32,512]{3,2,1,0:T(8,128)(2,1)} %all-to-all-done.1.gathered_hbm, bf16[3,512,512]{2,1,0:T(8,128)(2,1)} %bitcast.21, ...), custom_call_target="tpu_custom_call" | custom-call | flops 6442450944 | bytes 7342080 | tf_op jit(solution)/shard_map/pallas_call | solution.py:331
  87.0 6.5 %all-to-all-start.2 = ((bf16[16,3,32,512]{3,2,1,0:T(8,128)(2,1)}), bf16[16,3,32,512]{3,2,1,0:T(8,128)(2,1)S(1)}, u32[]{:S(2)}, u32[]{:S(2)}) async-start(bf16[16,3,32,512]{3,2,1,0:T(8,128)(2,1)} %get-tuple-element.28), calls=%async_computation.2 | async-start | bytes 3145728 | tf_op jit(solution)/shard_map/all_to_all | solution.py:438
  93.6 5.7 %collective-permute-start.5 = (bf16[384,512]{1,0:T(8,128)(2,1)}, bf16[384,512]{1,0:T(8,128)(2,1)}, u32[]{:S(2)}, u32[]{:S(2)}) collective-permute-start(bf16[384,512]{1,0:T(8,128)(2,1)} %slice_bitcast_fusion), channel_id=1, source_target_pairs={{0,4},{4,8},{8,12},{1,5},{5,9},{9,13},{2,6},{6,10},{10,14},{3,7},{... | collective-permute-start | bytes 1179656 | tf_op jit(solution)/shard_map/ppermute | solution.py:434
  99.2 14.4 %all-to-all-done.2.received_ref = bf16[16,3,32,512]{3,2,1,0:T(8,128)(2,1)S(1)} async-done(((bf16[16,3,32,512]{3,2,1,0:T(8,128)(2,1)}), bf16[16,3,32,512]{3,2,1,0:T(8,128)(2,1)S(1)}, u32[]{:S(2)}, u32[]{:S(2)}) %all-to-all-start.2) | async-done | bytes 1572896 | tf_op jit(solution)/shard_map/all_to_all | solution.py:438
  113.7 0.2 shard_map.134
  113.9 2.9 %collective-permute-start.6 = (bf16[3,32,512]{2,1,0:T(8,128)(2,1)S(1)}, bf16[3,32,512]{2,1,0:T(8,128)(2,1)S(1)}, u32[]{:S(2)}, u32[]{:S(2)}) collective-permute-start(bf16[3,32,512]{2,1,0:T(8,128)(2,1)S(1)} %shard_map.134), channel_id=1, source_target_pairs={{0,4},{4,0},{8,12},{12,8},{1,5},{5,1},{9,13},{13,9},{2,6},{6,2},{1... | collective-permute-start | bytes 294920 | tf_op jit(solution)/shard_map/ppermute | solution.py:450
  116.8 4.3 %shard_map.135.attended_ref = f32[512,512]{1,0:T(8,128)S(1)} custom-call(s32[16]{0:T(128)S(1)} %copy-done.3, bf16[512,512]{1,0:T(8,128)(2,1)S(1)} %bitcast.23, bf16[512,512]{1,0:T(8,128)(2,1)S(1)} %bitcast.18, bf16[512,512]{1,0:T(8,128)(2,1)S(1)} %bitcast.19, bf16[384,512]{1,0:T(8,128)(2,1)S(1)} %collective-permute-done.keys_a_ref, ...), custom_call_target="tpu_custom_call" | custom-call | flops 1073741824 | bytes 3670016 | tf_op jit(solution)/shard_map/pallas_call | solution.py:331
  121.1 1.7 collective-permute-start.7
  122.8 4.1 %collective-permute-done.7.refs_1_ = bf16[3,32,512]{2,1,0:T(8,128)(2,1)S(1)} collective-permute-done((bf16[3,32,512]{2,1,0:T(8,128)(2,1)S(1)}, bf16[3,32,512]{2,1,0:T(8,128)(2,1)S(1)}, u32[]{:S(2)}, u32[]{:S(2)}) %collective-permute-start.7) | collective-permute-done | bytes 98336 | tf_op jit(solution)/shard_map/ppermute | solution.py:450
  126.9 0.1 shard_map.136
  127.1 23.6 %all_to_all.20.gathered_ref = bf16[16,3,32,512]{3,2,1,0:T(8,128)(2,1)S(1)} all-to-all(bf16[16,3,32,512]{3,2,1,0:T(8,128)(2,1)S(1)} %shard_map.136), channel_id=1, replica_groups=mesh['x'=4,'y'=4,'z'=4,'w'=2,'c'=2] {'x','y'}, dimensions={0} | all-to-all | bytes 3145728 | tf_op jit(solution)/shard_map/all_to_all | solution.py:464
  150.7 8.9 %shard_map.137 = (f32[512,512]{1,0:T(8,128)S(1)}, f32[1,512]{1,0:T(1,128)S(1)}, bf16[3,512,512]{2,1,0:T(8,128)(2,1)}) custom-call(s32[1]{0:T(128)S(6)} %copy.15.split_ref, s32[16]{0:T(128)S(1)} %copy-done.10, f32[1]{0:T(128)S(6)} %copy.16.step_ref, bf16[16,3,32,512]{3,2,1,0:T(8,128)(2,1)S(1)} %all_to_all.20.gathered_ref, ...), custom_call_target="tpu_custom_call" | custom-call | flops 5637144576 | bytes 8914944 | tf_op jit(solution)/shard_map/pallas_call | solution.py:331
  159.6 11.4 %psum.7.energy_ref = f32[1,512]{1,0:T(1,128)S(1)} all-reduce(f32[1,512]{1,0:T(1,128)S(1)} %get-tuple-element.40), channel_id=1, replica_groups=mesh['x'=4,'y'=4,'z'=4,'w'=2,'c'=2] {'w','c'}, use_global_device_ids=true, to_apply=%region_1.0 | all-reduce | flops 512 | bytes 4096 | tf_op jit(solution)/shard_map/psum | solution.py:516
  171.0 1.5 shard_map.138
  (31 shorter events, 0.2 us)
Async XLA Ops:
  6.2 7.8 %copy-start = (bf16[1,512,512]{2,1,0:T(8,128)(2,1)S(1)}, bf16[1,512,512]{2,1,0:T(8,128)(2,1)}, u32[]{:S(2)}) copy-start(bf16[1,512,512]{2,1,0:T(8,128)(2,1)} %param.19) | copy-start | bytes 1572868
  6.2 28.4 %all-to-all-start = ((bf16[16,3,32,512]{3,2,1,0:T(8,128)(2,1)}), bf16[16,3,32,512]{3,2,1,0:T(8,128)(2,1)S(1)}, u32[]{:S(2)}, u32[]{:S(2)}) async-start(bf16[16,3,32,512]{3,2,1,0:T(8,128)(2,1)} %shard_map.131), calls=%async_computation | async-start | bytes 3145728 | tf_op jit(solution)/shard_map/all_to_all | solution.py:444
  13.9 31.7 %copy-start.1 = (bf16[1,512,512]{2,1,0:T(8,128)(2,1)S(1)}, bf16[1,512,512]{2,1,0:T(8,128)(2,1)}, u32[]{:S(2)}) copy-start(bf16[1,512,512]{2,1,0:T(8,128)(2,1)} %param.20) | copy-start | bytes 1572868
  14.0 20.8 %collective-permute-start = (bf16[384,512]{1,0:T(8,128)(2,1)S(1)}, bf16[384,512]{1,0:T(8,128)(2,1)S(1)}, u32[]{:S(2)}, u32[]{:S(2)}) collective-permute-start(bf16[384,512]{1,0:T(8,128)(2,1)S(1)} %slice_bitcast_fusion.1), channel_id=1, source_target_pairs={{0,4},{4,8},{8,12},{1,5},{5,9},{9,13},{2,6},{6,10},{10,14},{3,7},{... | collective-permute-start | bytes 1179656 | tf_op jit(solution)/shard_map/ppermute | solution.py:434
  34.8 6.1 %collective-permute-start.1 = (bf16[3,32,512]{2,1,0:T(8,128)(2,1)S(1)}, bf16[3,32,512]{2,1,0:T(8,128)(2,1)S(1)}, u32[]{:S(2)}, u32[]{:S(2)}) collective-permute-start(bf16[3,32,512]{2,1,0:T(8,128)(2,1)S(1)} %reduce_sum.12), channel_id=1, source_target_pairs={{0,4},{4,0},{8,12},{12,8},{1,5},{5,1},{9,13},{13,9},{2,6},{6,2},{1... | collective-permute-start | bytes 294920 | tf_op jit(solution)/shard_map/ppermute | solution.py:450
  41.0 6.6 %collective-permute-start.2 = (bf16[3,32,512]{2,1,0:T(8,128)(2,1)S(1)}, bf16[3,32,512]{2,1,0:T(8,128)(2,1)S(1)}, u32[]{:S(2)}, u32[]{:S(2)}) collective-permute-start(bf16[3,32,512]{2,1,0:T(8,128)(2,1)S(1)} %add_convert_fusion.1.refs_0_), channel_id=1, source_target_pairs={{0,12},{4,8},{8,4},{12,0},{1,13},{5,9},{9,5},{13,1},{2,14},{6,10},... | collective-permute-start | bytes 294920 | tf_op jit(solution)/shard_map/ppermute | solution.py:450
  48.9 27.2 %all-to-all-start.1 = ((bf16[16,3,32,512]{3,2,1,0:T(8,128)(2,1)}), bf16[16,3,32,512]{3,2,1,0:T(8,128)(2,1)}, u32[]{:S(2)}, u32[]{:S(2)}) async-start(bf16[16,3,32,512]{3,2,1,0:T(8,128)(2,1)} %shard_map.132), calls=%async_computation.1 | async-start | bytes 3145728 | tf_op jit(solution)/shard_map/all_to_all | solution.py:464
  57.8 11.2 %collective-permute-start.3 = (bf16[128,512]{1,0:T(8,128)(2,1)S(1)}, bf16[128,512]{1,0:T(8,128)(2,1)S(1)}, u32[]{:S(2)}, u32[]{:S(2)}) collective-permute-start(bf16[128,512]{1,0:T(8,128)(2,1)S(1)} %slice_bitcast_fusion.3), channel_id=1, source_target_pairs={{0,4},{4,8},{8,12},{1,5},{5,9},{9,13},{2,6},{6,10},{10,14},{3,7},{... | collective-permute-start | bytes 393224 | tf_op jit(solution)/shard_map/ppermute | solution.py:434
  62.7 7.3 %collective-permute-start.4 = (bf16[128,512]{1,0:T(8,128)(2,1)S(1)}, bf16[128,512]{1,0:T(8,128)(2,1)S(1)}, u32[]{:S(2)}, u32[]{:S(2)}) collective-permute-start(bf16[128,512]{1,0:T(8,128)(2,1)S(1)} %slice_bitcast_fusion.2), channel_id=1, source_target_pairs={{0,4},{4,8},{8,12},{1,5},{5,9},{9,13},{2,6},{6,10},{10,14},{3,7},{... | collective-permute-start | bytes 393224 | tf_op jit(solution)/shard_map/ppermute | solution.py:434
  69.0 17.9 %copy-start.6 = (bf16[128,512]{1,0:T(8,128)(2,1)}, bf16[128,512]{1,0:T(8,128)(2,1)S(1)}, u32[]{:S(2)}) copy-start(bf16[128,512]{1,0:T(8,128)(2,1)S(1)} %collective-permute-done.3.keys_b_ref) | copy-start | bytes 393220
  70.0 17.0 %copy-start.8 = (bf16[128,512]{1,0:T(8,128)(2,1)}, bf16[128,512]{1,0:T(8,128)(2,1)S(1)}, u32[]{:S(2)}) copy-start(bf16[128,512]{1,0:T(8,128)(2,1)S(1)} %collective-permute-done.4.values_b_ref) | copy-start | bytes 393220
  87.0 26.7 %all-to-all-start.2 = ((bf16[16,3,32,512]{3,2,1,0:T(8,128)(2,1)}), bf16[16,3,32,512]{3,2,1,0:T(8,128)(2,1)S(1)}, u32[]{:S(2)}, u32[]{:S(2)}) async-start(bf16[16,3,32,512]{3,2,1,0:T(8,128)(2,1)} %get-tuple-element.28), calls=%async_computation.2 | async-start | bytes 3145728 | tf_op jit(solution)/shard_map/all_to_all | solution.py:438
  93.5 23.2 %copy-start.3 = (s32[16]{0:T(128)S(1)}, s32[16]{0:T(128)}, u32[]{:S(2)}) copy-start(s32[16]{0:T(128)} %length_ref.3) | copy-start | bytes 196
  93.6 23.2 %copy-start.5 = (bf16[1,512,512]{2,1,0:T(8,128)(2,1)S(1)}, bf16[1,512,512]{2,1,0:T(8,128)(2,1)}, u32[]{:S(2)}) copy-start(bf16[1,512,512]{2,1,0:T(8,128)(2,1)} %param.18) | copy-start | bytes 1572868
  93.6 20.3 %collective-permute-start.5 = (bf16[384,512]{1,0:T(8,128)(2,1)}, bf16[384,512]{1,0:T(8,128)(2,1)}, u32[]{:S(2)}, u32[]{:S(2)}) collective-permute-start(bf16[384,512]{1,0:T(8,128)(2,1)} %slice_bitcast_fusion), channel_id=1, source_target_pairs={{0,4},{4,8},{8,12},{1,5},{5,9},{9,13},{2,6},{6,10},{10,14},{3,7},{... | collective-permute-start | bytes 1179656 | tf_op jit(solution)/shard_map/ppermute | solution.py:434
  113.7 3.1 %copy-start.7 = (bf16[128,512]{1,0:T(8,128)(2,1)S(1)}, bf16[128,512]{1,0:T(8,128)(2,1)}, u32[]{:S(2)}) copy-start(bf16[128,512]{1,0:T(8,128)(2,1)} %copy-done.6) | copy-start | bytes 393220
  113.7 3.1 %copy-start.9 = (bf16[128,512]{1,0:T(8,128)(2,1)S(1)}, bf16[128,512]{1,0:T(8,128)(2,1)}, u32[]{:S(2)}) copy-start(bf16[128,512]{1,0:T(8,128)(2,1)} %copy-done.8) | copy-start | bytes 393220
  113.9 7.2 %collective-permute-start.6 = (bf16[3,32,512]{2,1,0:T(8,128)(2,1)S(1)}, bf16[3,32,512]{2,1,0:T(8,128)(2,1)S(1)}, u32[]{:S(2)}, u32[]{:S(2)}) collective-permute-start(bf16[3,32,512]{2,1,0:T(8,128)(2,1)S(1)} %shard_map.134), channel_id=1, source_target_pairs={{0,4},{4,0},{8,12},{12,8},{1,5},{5,1},{9,13},{13,9},{2,6},{6,2},{1... | collective-permute-start | bytes 294920 | tf_op jit(solution)/shard_map/ppermute | solution.py:450
  121.1 5.8 %collective-permute-start.7 = (bf16[3,32,512]{2,1,0:T(8,128)(2,1)S(1)}, bf16[3,32,512]{2,1,0:T(8,128)(2,1)S(1)}, u32[]{:S(2)}, u32[]{:S(2)}) collective-permute-start(bf16[3,32,512]{2,1,0:T(8,128)(2,1)S(1)} %add_convert_fusion.refs_0_), channel_id=1, source_target_pairs={{0,12},{4,8},{8,4},{12,0},{1,13},{5,9},{9,5},{13,1},{2,14},{6,10},... | collective-permute-start | bytes 294920 | tf_op jit(solution)/shard_map/ppermute | solution.py:450
  127.0 23.7 %copy-start.4 = (bf16[3,1,512,512]{3,2,1,0:T(8,128)(2,1)S(1)}, bf16[3,1,512,512]{3,2,1,0:T(8,128)(2,1)}, u32[]{:S(2)}) copy-start(bf16[3,1,512,512]{3,2,1,0:T(8,128)(2,1)} %param.16) | copy-start | bytes 4718596
  127.1 23.7 %copy-start.10 = (s32[16]{0:T(128)S(1)}, s32[16]{0:T(128)}, u32[]{:S(2)}) copy-start(s32[16]{0:T(128)} %fork_ref.1) | copy-start | bytes 196
  127.1 23.7 %copy-start.11 = (bf16[3,512,512]{2,1,0:T(8,128)(2,1)S(1)}, bf16[3,512,512]{2,1,0:T(8,128)(2,1)}, u32[]{:S(2)}) copy-start(bf16[3,512,512]{2,1,0:T(8,128)(2,1)} %get-tuple-element.38.state_hbm) | copy-start | bytes 4718596
  150.7 20.3 %copy-start.2 = (f32[1,512]{1,0:T(1,128)S(1)}, f32[1,512]{1,0:T(1,128)}, u32[]{:S(2)}) copy-start(f32[1,512]{1,0:T(1,128)} %gain_ref.1) | copy-start | bytes 6148

commit v8 on v7

--- a/solution.py
+++ b/solution.py
@@ -488,18 +488,18 @@
     total_width = width * lax.axis_size(HEAD)
     parts_shape = shape((planes, 3, hidden // planes, width), jnp.bfloat16)
     barrier = lax.optimization_barrier
-    most = 3 * rows // 4
+    most, few = 5 * rows // 8, rows // 4
 
     keys_a = from_behind(own_keys[:most])
     parts = gradient_first(segment_end, trunk_rates, weights, keys, values, parts_shape)
-    mine, keys_a = barrier((sum_plane(parts), keys_a))
+    mine, keys_a = barrier((sum_plane_in_kernel(parts), keys_a))
     copies, _ = sum_depth(mine)
-    copies, rest_keys, rest_values = barrier((copies, own_keys[most:], own_values[: rows - most]))
+    copies, rest_keys, rest_values = barrier((copies, own_keys[most:], own_values[:few]))
     gathered, keys_b, values_b = barrier((spread_plane(copies), from_behind(rest_keys), from_behind(rest_values)))
     parts, state = update_and_gradient(
         segment_end, step_sizes, gathered, trunk_rates, weights, keys, values
     )
-    parts, rest_values = barrier((parts, own_values[rows - most :]))
+    parts, rest_values = barrier((parts, own_values[few:]))
     mine, values_c, query = barrier((sum_plane_in_kernel(parts), from_behind(rest_values), query))
     (attended,) = call(
         attend_kernel,

time: 173 us -> 171 us (0.988)
  starting transfers between devices: 57 us -> 50 us
  blocking collectives: 35.1 us -> 37.6 us
  waiting for transfers between devices: 45.1 us -> 46.9 us
    all_to_all x1 -> x2, waiting for transfers between devices: 14.4 us -> 30.1 us  [sum_plane_in_kernel(): received = lax.all_to_all(parts, PLANE, 0, 0, tiled=False)]
    all_to_all x1 -> x0, waiting for transfers between devices: 15.5 us -> none  [sum_plane(): received = lax.all_to_all(parts, PLANE, 0, 0, tiled=False)]
    all_to_all x1 -> x0, starting transfers between devices: 7.73 us -> none  [sum_plane(): received = lax.all_to_all(parts, PLANE, 0, 0, tiled=False)]
    all_to_all x1 -> x2, starting transfers between devices: 6.55 us -> 13.9 us  [sum_plane_in_kernel(): received = lax.all_to_all(parts, PLANE, 0, 0, tiled=False)]
    psum x1, blocking collectives: 11.4 us -> 14.3 us  [per_device(): energy = lax.psum(energy, HEAD)]
    ppermute x4, starting transfers between devices: 21.2 us -> 18.7 us  [from_behind(): lax.ppermute(value, 'z', [(source, source + 1) for source in range(count...]
    all_to_all x1, starting transfers between devices: 8.21 us -> 5.85 us  [spread_plane(): return lax.all_to_all(copies, PLANE, 0, 0, tiled=False)]
    ppermute x4, waiting for transfers between devices: 8.05 us -> 10 us  [swap_depth(): return lax.ppermute(value, 'z', [(i, i ^ flip) for i in range(depth)])]
  transfers between devices with their start and end apart: 11 -> 11, of which waited for: 7 -> 7; matrix products, arithmetic and copies ran while one was open for 1% -> 0% of each run, Pallas kernels for 3% -> 2%
where the time goes in v8:
time: 171 us
  starting transfers between devices  50 us (29%)
  waiting for transfers between devices  46.9 us (27%)
  blocking collectives  37.6 us (22%)
  Pallas kernels  31.7 us (19%)
  local copies, waits for them, and re-layouts  2.21 us (1%)
  between operations  2.18 us (1%)
    pallas_call x9, Pallas kernels, call(): pl.pallas_call(kernel, out_shape=(*outs, *held_outs), in_specs=[SMEM] * l...  31.7 us
    all_to_all x2, waiting for transfers between devices, sum_plane_in_kernel(): received = lax.all_to_all(parts, PLANE, 0, 0, tiled=False)  30.1 us
    all_to_all x1, blocking collectives, spread_plane(): return lax.all_to_all(copies, PLANE, 0, 0, tiled=False)  23.2 us
    ppermute x4, starting transfers between devices, from_behind(): lax.ppermute(value, 'z', [(source, source + 1) for source in range(count...  18.7 us
    psum x1, blocking collectives, per_device(): energy = lax.psum(energy, HEAD)  14.3 us
    all_to_all x2, starting transfers between devices, sum_plane_in_kernel(): received = lax.all_to_all(parts, PLANE, 0, 0, tiled=False)  13.9 us
    ppermute x4, starting transfers between devices, swap_depth(): return lax.ppermute(value, 'z', [(i, i ^ flip) for i in range(depth)])  11.6 us
    ppermute x4, waiting for transfers between devices, swap_depth(): return lax.ppermute(value, 'z', [(i, i ^ flip) for i in range(depth)])  10 us
  transfers between devices with their start and end apart: 11, of which 7 were waited for; matrix products, arithmetic and copies ran while one was open for 0% of the time, Pallas kernels for 2%

profile of v8, /device:TPU:1, one launch (start us, length us, event | category | flops | bytes accessed | tf_op | source)
XLA Modules:
  0.0 170.7 jit_solution(4334795159962021474)
XLA Ops:
  1.3 4.9 %shard_map.131 = bf16[16,3,32,512]{3,2,1,0:T(8,128)(2,1)} custom-call(s32[1]{0:T(128)S(6)} %copy.15.split_ref, f32[1,512]{1,0:T(1,128)} %rates_hbm.3, bf16[3,512,512]{2,1,0:T(8,128)(2,1)} %bitcast.20, bf16[512,512]{1,0:T(8,128)(2,1)} %bitcast.26, bf16[512,512]{1,0:T(8,128)(2,1)} %bitcast.28), custom_call_target="tpu_custom_call" | custom-call | flops 1610612736 | bytes 4196352 | tf_op jit(solution)/shard_map/pallas_call | solution.py:331
  6.2 7.7 %all-to-all-start = ((bf16[16,3,32,512]{3,2,1,0:T(8,128)(2,1)}), bf16[16,3,32,512]{3,2,1,0:T(8,128)(2,1)S(1)}, u32[]{:S(2)}, u32[]{:S(2)}) async-start(bf16[16,3,32,512]{3,2,1,0:T(8,128)(2,1)} %shard_map.131), calls=%async_computation | async-start | bytes 3145728 | tf_op jit(solution)/shard_map/all_to_all | solution.py:438
  14.0 5.0 %collective-permute-start = (bf16[320,512]{1,0:T(8,128)(2,1)S(1)}, bf16[320,512]{1,0:T(8,128)(2,1)S(1)}, u32[]{:S(2)}, u32[]{:S(2)}) collective-permute-start(bf16[320,512]{1,0:T(8,128)(2,1)S(1)} %slice_bitcast_fusion.1), channel_id=1, source_target_pairs={{0,4},{4,8},{8,12},{1,5},{5,9},{9,13},{2,6},{6,10},{10,14},{3,7},{... | collective-permute-start | bytes 983048 | tf_op jit(solution)/shard_map/ppermute | solution.py:434
  19.0 15.5 %all-to-all-done.received_ref = bf16[16,3,32,512]{3,2,1,0:T(8,128)(2,1)S(1)} async-done(((bf16[16,3,32,512]{3,2,1,0:T(8,128)(2,1)}), bf16[16,3,32,512]{3,2,1,0:T(8,128)(2,1)S(1)}, u32[]{:S(2)}, u32[]{:S(2)}) %all-to-all-start) | async-done | bytes 1572896 | tf_op jit(solution)/shard_map/all_to_all | solution.py:438
  34.5 0.2 shard_map.132
  34.8 3.1 %collective-permute-start.1 = (bf16[3,32,512]{2,1,0:T(8,128)(2,1)S(1)}, bf16[3,32,512]{2,1,0:T(8,128)(2,1)S(1)}, u32[]{:S(2)}, u32[]{:S(2)}) collective-permute-start(bf16[3,32,512]{2,1,0:T(8,128)(2,1)S(1)} %shard_map.132), channel_id=1, source_target_pairs={{0,4},{4,0},{8,12},{12,8},{1,5},{5,1},{9,13},{13,9},{2,6},{6,2},{1... | collective-permute-start | bytes 294920 | tf_op jit(solution)/shard_map/ppermute | solution.py:450
  37.9 2.0 %collective-permute-done.1 = bf16[3,32,512]{2,1,0:T(8,128)(2,1)S(1)} collective-permute-done((bf16[3,32,512]{2,1,0:T(8,128)(2,1)S(1)}, bf16[3,32,512]{2,1,0:T(8,128)(2,1)S(1)}, u32[]{:S(2)}, u32[]{:S(2)}) %collective-permute-start.1) | collective-permute-done | bytes 98336 | tf_op jit(solution)/shard_map/ppermute | solution.py:450
  39.9 5.6 %collective-permute-start.2 = (bf16[3,32,512]{2,1,0:T(8,128)(2,1)S(1)}, bf16[3,32,512]{2,1,0:T(8,128)(2,1)S(1)}, u32[]{:S(2)}, u32[]{:S(2)}) collective-permute-start(bf16[3,32,512]{2,1,0:T(8,128)(2,1)S(1)} %add_convert_fusion.1.refs_0_), channel_id=1, source_target_pairs={{0,12},{4,8},{8,4},{12,0},{1,13},{5,9},{9,5},{13,1},{2,14},{6,10},... | collective-permute-start | bytes 294920 | tf_op jit(solution)/shard_map/ppermute | solution.py:450
  45.5 2.1 %collective-permute-done.2.refs_1_ = bf16[3,32,512]{2,1,0:T(8,128)(2,1)S(1)} collective-permute-done((bf16[3,32,512]{2,1,0:T(8,128)(2,1)S(1)}, bf16[3,32,512]{2,1,0:T(8,128)(2,1)S(1)}, u32[]{:S(2)}, u32[]{:S(2)}) %collective-permute-start.2) | collective-permute-done | bytes 98336 | tf_op jit(solution)/shard_map/ppermute | solution.py:450
  47.5 1.3 shard_map.133
  48.8 5.8 %all-to-all-start.1 = ((bf16[16,3,32,512]{3,2,1,0:T(8,128)(2,1)}), bf16[16,3,32,512]{3,2,1,0:T(8,128)(2,1)}, u32[]{:S(2)}, u32[]{:S(2)}) async-start(bf16[16,3,32,512]{3,2,1,0:T(8,128)(2,1)} %shard_map.133), calls=%async_computation.1 | async-start | bytes 3145728 | tf_op jit(solution)/shard_map/all_to_all | solution.py:464
  55.3 4.6 %collective-permute-start.4 = (bf16[128,512]{1,0:T(8,128)(2,1)S(1)}, bf16[128,512]{1,0:T(8,128)(2,1)S(1)}, u32[]{:S(2)}, u32[]{:S(2)}) collective-permute-start(bf16[128,512]{1,0:T(8,128)(2,1)S(1)} %slice_bitcast_fusion.3), channel_id=1, source_target_pairs={{0,4},{4,8},{8,12},{1,5},{5,9},{9,13},{2,6},{6,10},{10,14},{3,7},{... | collective-permute-start | bytes 393224 | tf_op jit(solution)/shard_map/ppermute | solution.py:434
  59.9 4.6 %collective-permute-start.3 = (bf16[192,512]{1,0:T(8,128)(2,1)S(1)}, bf16[192,512]{1,0:T(8,128)(2,1)S(1)}, u32[]{:S(2)}, u32[]{:S(2)}) collective-permute-start(bf16[192,512]{1,0:T(8,128)(2,1)S(1)} %slice_bitcast_fusion.2), channel_id=1, source_target_pairs={{0,4},{4,8},{8,12},{1,5},{5,9},{9,13},{2,6},{6,10},{10,14},{3,7},{... | collective-permute-start | bytes 589832 | tf_op jit(solution)/shard_map/ppermute | solution.py:434
  64.5 0.8 slice_bitcast_fusion
  65.3 0.7 copy-done.10
  66.0 2.0 %collective-permute-done.3.keys_b_ref = bf16[192,512]{1,0:T(8,128)(2,1)S(1)} collective-permute-done((bf16[192,512]{1,0:T(8,128)(2,1)S(1)}, bf16[192,512]{1,0:T(8,128)(2,1)S(1)}, u32[]{:S(2)}, u32[]{:S(2)}) %collective-permute-start.3) | collective-permute-done | bytes 196640 | tf_op jit(solution)/shard_map/ppermute | solution.py:434
  67.9 0.7 copy-done.8
  68.6 4.8 %all-to-all-done.1.gathered_hbm = bf16[16,3,32,512]{3,2,1,0:T(8,128)(2,1)} async-done(((bf16[16,3,32,512]{3,2,1,0:T(8,128)(2,1)}), bf16[16,3,32,512]{3,2,1,0:T(8,128)(2,1)}, u32[]{:S(2)}, u32[]{:S(2)}) %all-to-all-start.1) | async-done | bytes 1572896 | tf_op jit(solution)/shard_map/all_to_all | solution.py:464
  73.4 10.8 %shard_map.134 = (bf16[16,3,32,512]{3,2,1,0:T(8,128)(2,1)}, bf16[3,512,512]{2,1,0:T(8,128)(2,1)}) custom-call(s32[1]{0:T(128)S(6)} %copy.15.split_ref, f32[1]{0:T(128)S(6)} %copy.16.step_ref, f32[1,512]{1,0:T(1,128)} %rates_hbm.3, bf16[16,3,32,512]{3,2,1,0:T(8,128)(2,1)} %all-to-all-done.1.gathered_hbm, bf16[3,512,512]{2,1,0:T(8,128)(2,1)} %bitcast.21, ...), custom_call_target="tpu_custom_call" | custom-call | flops 6442450944 | bytes 7342080 | tf_op jit(solution)/shard_map/pallas_call | solution.py:331
  84.2 6.2 %all-to-all-start.2 = ((bf16[16,3,32,512]{3,2,1,0:T(8,128)(2,1)}), bf16[16,3,32,512]{3,2,1,0:T(8,128)(2,1)S(1)}, u32[]{:S(2)}, u32[]{:S(2)}) async-start(bf16[16,3,32,512]{3,2,1,0:T(8,128)(2,1)} %get-tuple-element.28), calls=%async_computation.2 | async-start | bytes 3145728 | tf_op jit(solution)/shard_map/all_to_all | solution.py:438
  90.3 4.5 %collective-permute-start.5 = (bf16[384,512]{1,0:T(8,128)(2,1)}, bf16[384,512]{1,0:T(8,128)(2,1)S(1)}, u32[]{:S(2)}, u32[]{:S(2)}) collective-permute-start(bf16[384,512]{1,0:T(8,128)(2,1)} %slice_bitcast_fusion), channel_id=1, source_target_pairs={{0,4},{4,8},{8,12},{1,5},{5,9},{9,13},{2,6},{6,10},{10,14},{3,7},{... | collective-permute-start | bytes 1179656 | tf_op jit(solution)/shard_map/ppermute | solution.py:434
  94.9 14.6 %all-to-all-done.2.received_ref = bf16[16,3,32,512]{3,2,1,0:T(8,128)(2,1)S(1)} async-done(((bf16[16,3,32,512]{3,2,1,0:T(8,128)(2,1)}), bf16[16,3,32,512]{3,2,1,0:T(8,128)(2,1)S(1)}, u32[]{:S(2)}, u32[]{:S(2)}) %all-to-all-start.2) | async-done | bytes 1572896 | tf_op jit(solution)/shard_map/all_to_all | solution.py:438
  109.5 0.2 shard_map.135
  109.7 2.3 %collective-permute-start.6 = (bf16[3,32,512]{2,1,0:T(8,128)(2,1)S(1)}, bf16[3,32,512]{2,1,0:T(8,128)(2,1)S(1)}, u32[]{:S(2)}, u32[]{:S(2)}) collective-permute-start(bf16[3,32,512]{2,1,0:T(8,128)(2,1)S(1)} %shard_map.135), channel_id=1, source_target_pairs={{0,4},{4,0},{8,12},{12,8},{1,5},{5,1},{9,13},{13,9},{2,6},{6,2},{1... | collective-permute-start | bytes 294920 | tf_op jit(solution)/shard_map/ppermute | solution.py:450
  112.1 3.8 %shard_map.136.attended_ref = f32[512,512]{1,0:T(8,128)S(1)} custom-call(s32[16]{0:T(128)S(1)} %copy-done.3, bf16[512,512]{1,0:T(8,128)(2,1)S(1)} %bitcast.23, bf16[512,512]{1,0:T(8,128)(2,1)S(1)} %bitcast.18, bf16[512,512]{1,0:T(8,128)(2,1)S(1)} %bitcast.19, bf16[320,512]{1,0:T(8,128)(2,1)S(1)} %copy-done.7, bf16[192,512]{1,0:T(8,128)(2,1)S(1)} %copy-done.9, ...), custom_call_target="tpu_custom_call" | custom-call | flops 1073741824 | bytes 3670016 | tf_op jit(solution)/shard_map/pallas_call | solution.py:331
  116.0 0.6 collective-permute-start.7
  116.6 6.0 %collective-permute-done.7.refs_1_ = bf16[3,32,512]{2,1,0:T(8,128)(2,1)S(1)} collective-permute-done((bf16[3,32,512]{2,1,0:T(8,128)(2,1)S(1)}, bf16[3,32,512]{2,1,0:T(8,128)(2,1)S(1)}, u32[]{:S(2)}, u32[]{:S(2)}) %collective-permute-start.7) | collective-permute-done | bytes 98336 | tf_op jit(solution)/shard_map/ppermute | solution.py:450
  122.5 0.1 shard_map.137
  122.7 23.2 %all_to_all.20.gathered_ref = bf16[16,3,32,512]{3,2,1,0:T(8,128)(2,1)S(1)} all-to-all(bf16[16,3,32,512]{3,2,1,0:T(8,128)(2,1)S(1)} %shard_map.137), channel_id=1, replica_groups=mesh['x'=4,'y'=4,'z'=4,'w'=2,'c'=2] {'x','y'}, dimensions={0} | all-to-all | bytes 3145728 | tf_op jit(solution)/shard_map/all_to_all | solution.py:464
  146.0 8.9 %shard_map.138 = (f32[512,512]{1,0:T(8,128)S(1)}, f32[1,512]{1,0:T(1,128)S(1)}, bf16[3,512,512]{2,1,0:T(8,128)(2,1)}) custom-call(s32[1]{0:T(128)S(6)} %copy.15.split_ref, s32[16]{0:T(128)S(1)} %copy-done.12, f32[1]{0:T(128)S(6)} %copy.16.step_ref, bf16[16,3,32,512]{3,2,1,0:T(8,128)(2,1)S(1)} %all_to_all.20.gathered_ref, ...), custom_call_target="tpu_custom_call" | custom-call | flops 5637144576 | bytes 8914944 | tf_op jit(solution)/shard_map/pallas_call | solution.py:331
  154.9 14.3 %psum.7.energy_ref = f32[1,512]{1,0:T(1,128)S(1)} all-reduce(f32[1,512]{1,0:T(1,128)S(1)} %get-tuple-element.40), channel_id=1, replica_groups=mesh['x'=4,'y'=4,'z'=4,'w'=2,'c'=2] {'w','c'}, use_global_device_ids=true, to_apply=%region_0.0 | all-reduce | flops 512 | bytes 4096 | tf_op jit(solution)/shard_map/psum | solution.py:516
  169.2 1.5 shard_map.139
  (35 shorter events, 0.2 us)
Async XLA Ops:
  6.2 7.8 %copy-start = (bf16[1,512,512]{2,1,0:T(8,128)(2,1)S(1)}, bf16[1,512,512]{2,1,0:T(8,128)(2,1)}, u32[]{:S(2)}) copy-start(bf16[1,512,512]{2,1,0:T(8,128)(2,1)} %param.19) | copy-start | bytes 1572868
  6.2 28.4 %all-to-all-start = ((bf16[16,3,32,512]{3,2,1,0:T(8,128)(2,1)}), bf16[16,3,32,512]{3,2,1,0:T(8,128)(2,1)S(1)}, u32[]{:S(2)}, u32[]{:S(2)}) async-start(bf16[16,3,32,512]{3,2,1,0:T(8,128)(2,1)} %shard_map.131), calls=%async_computation | async-start | bytes 3145728 | tf_op jit(solution)/shard_map/all_to_all | solution.py:438
  13.9 31.5 %copy-start.1 = (bf16[1,512,512]{2,1,0:T(8,128)(2,1)S(1)}, bf16[1,512,512]{2,1,0:T(8,128)(2,1)}, u32[]{:S(2)}) copy-start(bf16[1,512,512]{2,1,0:T(8,128)(2,1)} %param.20) | copy-start | bytes 1572868
  14.0 20.8 %collective-permute-start = (bf16[320,512]{1,0:T(8,128)(2,1)S(1)}, bf16[320,512]{1,0:T(8,128)(2,1)S(1)}, u32[]{:S(2)}, u32[]{:S(2)}) collective-permute-start(bf16[320,512]{1,0:T(8,128)(2,1)S(1)} %slice_bitcast_fusion.1), channel_id=1, source_target_pairs={{0,4},{4,8},{8,12},{1,5},{5,9},{9,13},{2,6},{6,10},{10,14},{3,7},{... | collective-permute-start | bytes 983048 | tf_op jit(solution)/shard_map/ppermute | solution.py:434
  34.8 14.1 %copy-start.6 = (bf16[320,512]{1,0:T(8,128)(2,1)}, bf16[320,512]{1,0:T(8,128)(2,1)S(1)}, u32[]{:S(2)}) copy-start(bf16[320,512]{1,0:T(8,128)(2,1)S(1)} %collective-permute-done.keys_a_ref) | copy-start | bytes 983044
  34.8 5.1 %collective-permute-start.1 = (bf16[3,32,512]{2,1,0:T(8,128)(2,1)S(1)}, bf16[3,32,512]{2,1,0:T(8,128)(2,1)S(1)}, u32[]{:S(2)}, u32[]{:S(2)}) collective-permute-start(bf16[3,32,512]{2,1,0:T(8,128)(2,1)S(1)} %shard_map.132), channel_id=1, source_target_pairs={{0,4},{4,0},{8,12},{12,8},{1,5},{5,1},{9,13},{13,9},{2,6},{6,2},{1... | collective-permute-start | bytes 294920 | tf_op jit(solution)/shard_map/ppermute | solution.py:450
  39.9 7.6 %collective-permute-start.2 = (bf16[3,32,512]{2,1,0:T(8,128)(2,1)S(1)}, bf16[3,32,512]{2,1,0:T(8,128)(2,1)S(1)}, u32[]{:S(2)}, u32[]{:S(2)}) collective-permute-start(bf16[3,32,512]{2,1,0:T(8,128)(2,1)S(1)} %add_convert_fusion.1.refs_0_), channel_id=1, source_target_pairs={{0,12},{4,8},{8,4},{12,0},{1,13},{5,9},{9,5},{13,1},{2,14},{6,10},... | collective-permute-start | bytes 294920 | tf_op jit(solution)/shard_map/ppermute | solution.py:450
  48.8 24.5 %all-to-all-start.1 = ((bf16[16,3,32,512]{3,2,1,0:T(8,128)(2,1)}), bf16[16,3,32,512]{3,2,1,0:T(8,128)(2,1)}, u32[]{:S(2)}, u32[]{:S(2)}) async-start(bf16[16,3,32,512]{3,2,1,0:T(8,128)(2,1)} %shard_map.133), calls=%async_computation.1 | async-start | bytes 3145728 | tf_op jit(solution)/shard_map/all_to_all | solution.py:464
  55.3 10.0 %collective-permute-start.4 = (bf16[128,512]{1,0:T(8,128)(2,1)S(1)}, bf16[128,512]{1,0:T(8,128)(2,1)S(1)}, u32[]{:S(2)}, u32[]{:S(2)}) collective-permute-start(bf16[128,512]{1,0:T(8,128)(2,1)S(1)} %slice_bitcast_fusion.3), channel_id=1, source_target_pairs={{0,4},{4,8},{8,12},{1,5},{5,9},{9,13},{2,6},{6,10},{10,14},{3,7},{... | collective-permute-start | bytes 393224 | tf_op jit(solution)/shard_map/ppermute | solution.py:434
  59.9 8.0 %collective-permute-start.3 = (bf16[192,512]{1,0:T(8,128)(2,1)S(1)}, bf16[192,512]{1,0:T(8,128)(2,1)S(1)}, u32[]{:S(2)}, u32[]{:S(2)}) collective-permute-start(bf16[192,512]{1,0:T(8,128)(2,1)S(1)} %slice_bitcast_fusion.2), channel_id=1, source_target_pairs={{0,4},{4,8},{8,12},{1,5},{5,9},{9,13},{2,6},{6,10},{10,14},{3,7},{... | collective-permute-start | bytes 589832 | tf_op jit(solution)/shard_map/ppermute | solution.py:434
  65.3 0.7 copy-start.10
  67.9 0.7 copy-start.8
  84.2 25.3 %all-to-all-start.2 = ((bf16[16,3,32,512]{3,2,1,0:T(8,128)(2,1)}), bf16[16,3,32,512]{3,2,1,0:T(8,128)(2,1)S(1)}, u32[]{:S(2)}, u32[]{:S(2)}) async-start(bf16[16,3,32,512]{3,2,1,0:T(8,128)(2,1)} %get-tuple-element.28), calls=%async_computation.2 | async-start | bytes 3145728 | tf_op jit(solution)/shard_map/all_to_all | solution.py:438
  90.3 21.7 %copy-start.3 = (s32[16]{0:T(128)S(1)}, s32[16]{0:T(128)}, u32[]{:S(2)}) copy-start(s32[16]{0:T(128)} %length_ref.3) | copy-start | bytes 196
  90.3 21.7 %copy-start.5 = (bf16[1,512,512]{2,1,0:T(8,128)(2,1)S(1)}, bf16[1,512,512]{2,1,0:T(8,128)(2,1)}, u32[]{:S(2)}) copy-start(bf16[1,512,512]{2,1,0:T(8,128)(2,1)} %param.18) | copy-start | bytes 1572868
  90.3 19.4 %collective-permute-start.5 = (bf16[384,512]{1,0:T(8,128)(2,1)}, bf16[384,512]{1,0:T(8,128)(2,1)S(1)}, u32[]{:S(2)}, u32[]{:S(2)}) collective-permute-start(bf16[384,512]{1,0:T(8,128)(2,1)} %slice_bitcast_fusion), channel_id=1, source_target_pairs={{0,4},{4,8},{8,12},{1,5},{5,9},{9,13},{2,6},{6,10},{10,14},{3,7},{... | collective-permute-start | bytes 1179656 | tf_op jit(solution)/shard_map/ppermute | solution.py:434
  109.5 2.6 %copy-start.7 = (bf16[320,512]{1,0:T(8,128)(2,1)S(1)}, bf16[320,512]{1,0:T(8,128)(2,1)}, u32[]{:S(2)}) copy-start(bf16[320,512]{1,0:T(8,128)(2,1)} %copy-done.6) | copy-start | bytes 983044
  109.5 2.6 %copy-start.9 = (bf16[192,512]{1,0:T(8,128)(2,1)S(1)}, bf16[192,512]{1,0:T(8,128)(2,1)}, u32[]{:S(2)}) copy-start(bf16[192,512]{1,0:T(8,128)(2,1)} %copy-done.8) | copy-start | bytes 589828
  109.5 2.6 %copy-start.11 = (bf16[128,512]{1,0:T(8,128)(2,1)S(1)}, bf16[128,512]{1,0:T(8,128)(2,1)}, u32[]{:S(2)}) copy-start(bf16[128,512]{1,0:T(8,128)(2,1)} %copy-done.10) | copy-start | bytes 393220
  109.7 6.2 %collective-permute-start.6 = (bf16[3,32,512]{2,1,0:T(8,128)(2,1)S(1)}, bf16[3,32,512]{2,1,0:T(8,128)(2,1)S(1)}, u32[]{:S(2)}, u32[]{:S(2)}) collective-permute-start(bf16[3,32,512]{2,1,0:T(8,128)(2,1)S(1)} %shard_map.135), channel_id=1, source_target_pairs={{0,4},{4,0},{8,12},{12,8},{1,5},{5,1},{9,13},{13,9},{2,6},{6,2},{1... | collective-permute-start | bytes 294920 | tf_op jit(solution)/shard_map/ppermute | solution.py:450
  116.0 6.6 %collective-permute-start.7 = (bf16[3,32,512]{2,1,0:T(8,128)(2,1)S(1)}, bf16[3,32,512]{2,1,0:T(8,128)(2,1)S(1)}, u32[]{:S(2)}, u32[]{:S(2)}) collective-permute-start(bf16[3,32,512]{2,1,0:T(8,128)(2,1)S(1)} %add_convert_fusion.refs_0_), channel_id=1, source_target_pairs={{0,12},{4,8},{8,4},{12,0},{1,13},{5,9},{9,5},{13,1},{2,14},{6,10},... | collective-permute-start | bytes 294920 | tf_op jit(solution)/shard_map/ppermute | solution.py:450
  122.7 23.3 %copy-start.4 = (bf16[3,1,512,512]{3,2,1,0:T(8,128)(2,1)S(1)}, bf16[3,1,512,512]{3,2,1,0:T(8,128)(2,1)}, u32[]{:S(2)}) copy-start(bf16[3,1,512,512]{3,2,1,0:T(8,128)(2,1)} %param.16) | copy-start | bytes 4718596
  122.7 23.3 %copy-start.12 = (s32[16]{0:T(128)S(1)}, s32[16]{0:T(128)}, u32[]{:S(2)}) copy-start(s32[16]{0:T(128)} %fork_ref.1) | copy-start | bytes 196
  122.7 23.3 %copy-start.13 = (bf16[3,512,512]{2,1,0:T(8,128)(2,1)S(1)}, bf16[3,512,512]{2,1,0:T(8,128)(2,1)}, u32[]{:S(2)}) copy-start(bf16[3,512,512]{2,1,0:T(8,128)(2,1)} %get-tuple-element.38.state_hbm) | copy-start | bytes 4718596
  146.0 23.2 %copy-start.2 = (f32[1,512]{1,0:T(1,128)S(1)}, f32[1,512]{1,0:T(1,128)}, u32[]{:S(2)}) copy-start(f32[1,512]{1,0:T(1,128)} %gain_ref.1) | copy-start | bytes 6148

commit v9 on v8

--- a/solution.py
+++ b/solution.py
@@ -488,7 +488,7 @@
     total_width = width * lax.axis_size(HEAD)
     parts_shape = shape((planes, 3, hidden // planes, width), jnp.bfloat16)
     barrier = lax.optimization_barrier
-    most, few = 5 * rows // 8, rows // 4
+    most, few = 11 * rows // 16, 5 * rows // 16
 
     keys_a = from_behind(own_keys[:most])
     parts = gradient_first(segment_end, trunk_rates, weights, keys, values, parts_shape)

time: 171 us -> 171 us (level)
  starting transfers between devices: 50 us -> 57.2 us
  blocking collectives: 37.6 us -> 34.1 us
  waiting for transfers between devices: 46.9 us -> 43.8 us
    ppermute x4, waiting for transfers between devices: 10 us -> 6.86 us  [swap_depth(): return lax.ppermute(value, 'z', [(i, i ^ flip) for i in range(depth)])]
    psum x1, blocking collectives: 14.3 us -> 11.3 us  [per_device(): energy = lax.psum(energy, HEAD)]
    ppermute x4, starting transfers between devices: 11.6 us -> 14.6 us  [swap_depth(): return lax.ppermute(value, 'z', [(i, i ^ flip) for i in range(depth)])]
    ppermute x4, starting transfers between devices: 18.7 us -> 21.6 us  [from_behind(): lax.ppermute(value, 'z', [(source, source + 1) for source in range(count...]
  transfers between devices with their start and end apart: 11 -> 11, of which waited for: 7 -> 7; matrix products, arithmetic and copies ran while one was open for 0% -> 0% of each run, Pallas kernels for 2% -> 3%
where the time goes in v9:
time: 171 us; the launch traced here: 170 us
  starting transfers between devices  57.2 us (33%)
  waiting for transfers between devices  43.8 us (26%)
  blocking collectives  34.1 us (20%)
  Pallas kernels  32.2 us (19%)
  between operations  2.17 us (1%)
    pallas_call x9, Pallas kernels, call(): pl.pallas_call(kernel, out_shape=(*outs, *held_outs), in_specs=[SMEM] * l...  32.2 us
    all_to_all x2, waiting for transfers between devices, sum_plane_in_kernel(): received = lax.all_to_all(parts, PLANE, 0, 0, tiled=False)  29.8 us
    all_to_all x1, blocking collectives, spread_plane(): return lax.all_to_all(copies, PLANE, 0, 0, tiled=False)  22.8 us
    ppermute x4, starting transfers between devices, from_behind(): lax.ppermute(value, 'z', [(source, source + 1) for source in range(count...  21.6 us
    all_to_all x2, starting transfers between devices, sum_plane_in_kernel(): received = lax.all_to_all(parts, PLANE, 0, 0, tiled=False)  14.6 us
    ppermute x4, starting transfers between devices, swap_depth(): return lax.ppermute(value, 'z', [(i, i ^ flip) for i in range(depth)])  14.6 us
    psum x1, blocking collectives, per_device(): energy = lax.psum(energy, HEAD)  11.3 us
    ppermute x4, waiting for transfers between devices, swap_depth(): return lax.ppermute(value, 'z', [(i, i ^ flip) for i in range(depth)])  6.86 us
  transfers between devices with their start and end apart: 11, of which 7 were waited for; matrix products, arithmetic and copies ran while one was open for 0% of the time, Pallas kernels for 3%

profile of v9, /device:TPU:1, one launch (start us, length us, event | category | flops | bytes accessed | tf_op | source)
XLA Modules:
  0.0 170.5 jit_solution(17114427993380416946)
XLA Ops:
  1.3 4.9 %shard_map.131 = bf16[16,3,32,512]{3,2,1,0:T(8,128)(2,1)} custom-call(s32[1]{0:T(128)S(6)} %copy.15.split_ref, f32[1,512]{1,0:T(1,128)} %rates_hbm.3, bf16[3,512,512]{2,1,0:T(8,128)(2,1)} %bitcast.20, bf16[512,512]{1,0:T(8,128)(2,1)} %bitcast.26, bf16[512,512]{1,0:T(8,128)(2,1)} %bitcast.28), custom_call_target="tpu_custom_call" | custom-call | flops 1610612736 | bytes 4196352 | tf_op jit(solution)/shard_map/pallas_call | solution.py:331
  6.2 0.0 copy-start
  6.2 7.7 %all-to-all-start = ((bf16[16,3,32,512]{3,2,1,0:T(8,128)(2,1)}), bf16[16,3,32,512]{3,2,1,0:T(8,128)(2,1)S(1)}, u32[]{:S(2)}, u32[]{:S(2)}) async-start(bf16[16,3,32,512]{3,2,1,0:T(8,128)(2,1)} %shard_map.131), calls=%async_computation | async-start | bytes 3145728 | tf_op jit(solution)/shard_map/all_to_all | solution.py:438
  14.0 5.0 %collective-permute-start = (bf16[352,512]{1,0:T(8,128)(2,1)S(1)}, bf16[352,512]{1,0:T(8,128)(2,1)S(1)}, u32[]{:S(2)}, u32[]{:S(2)}) collective-permute-start(bf16[352,512]{1,0:T(8,128)(2,1)S(1)} %slice_bitcast_fusion.1), channel_id=1, source_target_pairs={{0,4},{4,8},{8,12},{1,5},{5,9},{9,13},{2,6},{6,10},{10,14},{3,7},{... | collective-permute-start | bytes 1081352 | tf_op jit(solution)/shard_map/ppermute | solution.py:434
  19.0 15.5 %all-to-all-done.received_ref = bf16[16,3,32,512]{3,2,1,0:T(8,128)(2,1)S(1)} async-done(((bf16[16,3,32,512]{3,2,1,0:T(8,128)(2,1)}), bf16[16,3,32,512]{3,2,1,0:T(8,128)(2,1)S(1)}, u32[]{:S(2)}, u32[]{:S(2)}) %all-to-all-start) | async-done | bytes 1572896 | tf_op jit(solution)/shard_map/all_to_all | solution.py:438
  34.5 0.2 shard_map.132
  34.8 3.1 %collective-permute-start.1 = (bf16[3,32,512]{2,1,0:T(8,128)(2,1)S(1)}, bf16[3,32,512]{2,1,0:T(8,128)(2,1)S(1)}, u32[]{:S(2)}, u32[]{:S(2)}) collective-permute-start(bf16[3,32,512]{2,1,0:T(8,128)(2,1)S(1)} %shard_map.132), channel_id=1, source_target_pairs={{0,4},{4,0},{8,12},{12,8},{1,5},{5,1},{9,13},{13,9},{2,6},{6,2},{1... | collective-permute-start | bytes 294920 | tf_op jit(solution)/shard_map/ppermute | solution.py:450
  37.8 2.0 %collective-permute-done.1 = bf16[3,32,512]{2,1,0:T(8,128)(2,1)S(1)} collective-permute-done((bf16[3,32,512]{2,1,0:T(8,128)(2,1)S(1)}, bf16[3,32,512]{2,1,0:T(8,128)(2,1)S(1)}, u32[]{:S(2)}, u32[]{:S(2)}) %collective-permute-start.1) | collective-permute-done | bytes 98336 | tf_op jit(solution)/shard_map/ppermute | solution.py:450
  39.9 5.6 %collective-permute-start.2 = (bf16[3,32,512]{2,1,0:T(8,128)(2,1)S(1)}, bf16[3,32,512]{2,1,0:T(8,128)(2,1)S(1)}, u32[]{:S(2)}, u32[]{:S(2)}) collective-permute-start(bf16[3,32,512]{2,1,0:T(8,128)(2,1)S(1)} %add_convert_fusion.1.refs_0_), channel_id=1, source_target_pairs={{0,12},{4,8},{8,4},{12,0},{1,13},{5,9},{9,5},{13,1},{2,14},{6,10},... | collective-permute-start | bytes 294920 | tf_op jit(solution)/shard_map/ppermute | solution.py:450
  45.5 2.0 %collective-permute-done.2.refs_1_ = bf16[3,32,512]{2,1,0:T(8,128)(2,1)S(1)} collective-permute-done((bf16[3,32,512]{2,1,0:T(8,128)(2,1)S(1)}, bf16[3,32,512]{2,1,0:T(8,128)(2,1)S(1)}, u32[]{:S(2)}, u32[]{:S(2)}) %collective-permute-start.2) | collective-permute-done | bytes 98336 | tf_op jit(solution)/shard_map/ppermute | solution.py:450
  47.5 1.3 shard_map.133
  48.8 6.5 %all-to-all-start.1 = ((bf16[16,3,32,512]{3,2,1,0:T(8,128)(2,1)}), bf16[16,3,32,512]{3,2,1,0:T(8,128)(2,1)}, u32[]{:S(2)}, u32[]{:S(2)}) async-start(bf16[16,3,32,512]{3,2,1,0:T(8,128)(2,1)} %shard_map.133), calls=%async_computation.1 | async-start | bytes 3145728 | tf_op jit(solution)/shard_map/all_to_all | solution.py:464
  56.0 5.0 %collective-permute-start.3 = (bf16[160,512]{1,0:T(8,128)(2,1)S(1)}, bf16[160,512]{1,0:T(8,128)(2,1)S(1)}, u32[]{:S(2)}, u32[]{:S(2)}) collective-permute-start(bf16[160,512]{1,0:T(8,128)(2,1)S(1)} %slice_bitcast_fusion.3), channel_id=1, source_target_pairs={{0,4},{4,8},{8,12},{1,5},{5,9},{9,13},{2,6},{6,10},{10,14},{3,7},{... | collective-permute-start | bytes 491528 | tf_op jit(solution)/shard_map/ppermute | solution.py:434
  61.0 5.5 %collective-permute-start.4 = (bf16[160,512]{1,0:T(8,128)(2,1)S(1)}, bf16[160,512]{1,0:T(8,128)(2,1)S(1)}, u32[]{:S(2)}, u32[]{:S(2)}) collective-permute-start(bf16[160,512]{1,0:T(8,128)(2,1)S(1)} %slice_bitcast_fusion.2), channel_id=1, source_target_pairs={{0,4},{4,8},{8,12},{1,5},{5,9},{9,13},{2,6},{6,10},{10,14},{3,7},{... | collective-permute-start | bytes 491528 | tf_op jit(solution)/shard_map/ppermute | solution.py:434
  66.6 0.8 slice_bitcast_fusion
  67.3 2.3 %collective-permute-done.4.values_b_ref = bf16[160,512]{1,0:T(8,128)(2,1)S(1)} collective-permute-done((bf16[160,512]{1,0:T(8,128)(2,1)S(1)}, bf16[160,512]{1,0:T(8,128)(2,1)S(1)}, u32[]{:S(2)}, u32[]{:S(2)}) %collective-permute-start.4) | collective-permute-done | bytes 163872 | tf_op jit(solution)/shard_map/ppermute | solution.py:434
  69.6 4.8 %all-to-all-done.1.gathered_hbm = bf16[16,3,32,512]{3,2,1,0:T(8,128)(2,1)} async-done(((bf16[16,3,32,512]{3,2,1,0:T(8,128)(2,1)}), bf16[16,3,32,512]{3,2,1,0:T(8,128)(2,1)}, u32[]{:S(2)}, u32[]{:S(2)}) %all-to-all-start.1) | async-done | bytes 1572896 | tf_op jit(solution)/shard_map/all_to_all | solution.py:464
  74.5 10.8 %shard_map.134 = (bf16[16,3,32,512]{3,2,1,0:T(8,128)(2,1)}, bf16[3,512,512]{2,1,0:T(8,128)(2,1)}) custom-call(s32[1]{0:T(128)S(6)} %copy.15.split_ref, f32[1]{0:T(128)S(6)} %copy.16.step_ref, f32[1,512]{1,0:T(1,128)} %rates_hbm.3, bf16[16,3,32,512]{3,2,1,0:T(8,128)(2,1)} %all-to-all-done.1.gathered_hbm, bf16[3,512,512]{2,1,0:T(8,128)(2,1)} %bitcast.21, ...), custom_call_target="tpu_custom_call" | custom-call | flops 6442450944 | bytes 7342080 | tf_op jit(solution)/shard_map/pallas_call | solution.py:331
  85.3 6.9 %all-to-all-start.2 = ((bf16[16,3,32,512]{3,2,1,0:T(8,128)(2,1)}), bf16[16,3,32,512]{3,2,1,0:T(8,128)(2,1)S(1)}, u32[]{:S(2)}, u32[]{:S(2)}) async-start(bf16[16,3,32,512]{3,2,1,0:T(8,128)(2,1)} %get-tuple-element.28), calls=%async_computation.2 | async-start | bytes 3145728 | tf_op jit(solution)/shard_map/all_to_all | solution.py:438
  92.1 0.0 copy-start.5
  92.2 6.0 %collective-permute-start.5 = (bf16[352,512]{1,0:T(8,128)(2,1)}, bf16[352,512]{1,0:T(8,128)(2,1)}, u32[]{:S(2)}, u32[]{:S(2)}) collective-permute-start(bf16[352,512]{1,0:T(8,128)(2,1)} %slice_bitcast_fusion), channel_id=1, source_target_pairs={{0,4},{4,8},{8,12},{1,5},{5,9},{9,13},{2,6},{6,10},{10,14},{3,7},{... | collective-permute-start | bytes 1081352 | tf_op jit(solution)/shard_map/ppermute | solution.py:434
  98.1 14.3 %all-to-all-done.2.received_ref = bf16[16,3,32,512]{3,2,1,0:T(8,128)(2,1)S(1)} async-done(((bf16[16,3,32,512]{3,2,1,0:T(8,128)(2,1)}), bf16[16,3,32,512]{3,2,1,0:T(8,128)(2,1)S(1)}, u32[]{:S(2)}, u32[]{:S(2)}) %all-to-all-start.2) | async-done | bytes 1572896 | tf_op jit(solution)/shard_map/all_to_all | solution.py:438
  112.4 0.2 shard_map.135
  112.7 3.1 %collective-permute-start.6 = (bf16[3,32,512]{2,1,0:T(8,128)(2,1)S(1)}, bf16[3,32,512]{2,1,0:T(8,128)(2,1)S(1)}, u32[]{:S(2)}, u32[]{:S(2)}) collective-permute-start(bf16[3,32,512]{2,1,0:T(8,128)(2,1)S(1)} %shard_map.135), channel_id=1, source_target_pairs={{0,4},{4,0},{8,12},{12,8},{1,5},{5,1},{9,13},{13,9},{2,6},{6,2},{1... | collective-permute-start | bytes 294920 | tf_op jit(solution)/shard_map/ppermute | solution.py:450
  115.7 4.3 %shard_map.136.attended_ref = f32[512,512]{1,0:T(8,128)S(1)} custom-call(s32[16]{0:T(128)S(1)} %copy-done.3, bf16[512,512]{1,0:T(8,128)(2,1)S(1)} %bitcast.23, bf16[512,512]{1,0:T(8,128)(2,1)S(1)} %bitcast.18, bf16[512,512]{1,0:T(8,128)(2,1)S(1)} %bitcast.19, bf16[352,512]{1,0:T(8,128)(2,1)S(1)} %collective-permute-done.keys_a_ref, ...), custom_call_target="tpu_custom_call" | custom-call | flops 1073741824 | bytes 3670016 | tf_op jit(solution)/shard_map/pallas_call | solution.py:331
  120.1 2.9 %collective-permute-start.7 = (bf16[3,32,512]{2,1,0:T(8,128)(2,1)S(1)}, bf16[3,32,512]{2,1,0:T(8,128)(2,1)S(1)}, u32[]{:S(2)}, u32[]{:S(2)}) collective-permute-start(bf16[3,32,512]{2,1,0:T(8,128)(2,1)S(1)} %add_convert_fusion.refs_0_), channel_id=1, source_target_pairs={{0,12},{4,8},{8,4},{12,0},{1,13},{5,9},{9,5},{13,1},{2,14},{6,10},... | collective-permute-start | bytes 294920 | tf_op jit(solution)/shard_map/ppermute | solution.py:450
  122.9 2.8 %collective-permute-done.7.refs_1_ = bf16[3,32,512]{2,1,0:T(8,128)(2,1)S(1)} collective-permute-done((bf16[3,32,512]{2,1,0:T(8,128)(2,1)S(1)}, bf16[3,32,512]{2,1,0:T(8,128)(2,1)S(1)}, u32[]{:S(2)}, u32[]{:S(2)}) %collective-permute-start.7) | collective-permute-done | bytes 98336 | tf_op jit(solution)/shard_map/ppermute | solution.py:450
  125.7 0.1 shard_map.137
  125.9 22.8 %all_to_all.20.gathered_ref = bf16[16,3,32,512]{3,2,1,0:T(8,128)(2,1)S(1)} all-to-all(bf16[16,3,32,512]{3,2,1,0:T(8,128)(2,1)S(1)} %shard_map.137), channel_id=1, replica_groups=mesh['x'=4,'y'=4,'z'=4,'w'=2,'c'=2] {'x','y'}, dimensions={0} | all-to-all | bytes 3145728 | tf_op jit(solution)/shard_map/all_to_all | solution.py:464
  148.8 8.9 %shard_map.138 = (f32[512,512]{1,0:T(8,128)S(1)}, f32[1,512]{1,0:T(1,128)S(1)}, bf16[3,512,512]{2,1,0:T(8,128)(2,1)}) custom-call(s32[1]{0:T(128)S(6)} %copy.15.split_ref, s32[16]{0:T(128)S(1)} %copy-done.10, f32[1]{0:T(128)S(6)} %copy.16.step_ref, bf16[16,3,32,512]{3,2,1,0:T(8,128)(2,1)S(1)} %all_to_all.20.gathered_ref, ...), custom_call_target="tpu_custom_call" | custom-call | flops 5637144576 | bytes 8914944 | tf_op jit(solution)/shard_map/pallas_call | solution.py:331
  157.6 11.3 %psum.7.energy_ref = f32[1,512]{1,0:T(1,128)S(1)} all-reduce(f32[1,512]{1,0:T(1,128)S(1)} %get-tuple-element.40), channel_id=1, replica_groups=mesh['x'=4,'y'=4,'z'=4,'w'=2,'c'=2] {'w','c'}, use_global_device_ids=true, to_apply=%region_0.0 | all-reduce | flops 512 | bytes 4096 | tf_op jit(solution)/shard_map/psum | solution.py:516
  168.9 1.5 shard_map.139
  (31 shorter events, 0.2 us)
Async XLA Ops:
  6.2 7.8 %copy-start = (bf16[1,512,512]{2,1,0:T(8,128)(2,1)S(1)}, bf16[1,512,512]{2,1,0:T(8,128)(2,1)}, u32[]{:S(2)}) copy-start(bf16[1,512,512]{2,1,0:T(8,128)(2,1)} %param.19) | copy-start | bytes 1572868
  6.2 28.4 %all-to-all-start = ((bf16[16,3,32,512]{3,2,1,0:T(8,128)(2,1)}), bf16[16,3,32,512]{3,2,1,0:T(8,128)(2,1)S(1)}, u32[]{:S(2)}, u32[]{:S(2)}) async-start(bf16[16,3,32,512]{3,2,1,0:T(8,128)(2,1)} %shard_map.131), calls=%async_computation | async-start | bytes 3145728 | tf_op jit(solution)/shard_map/all_to_all | solution.py:438
  13.9 31.5 %copy-start.1 = (bf16[1,512,512]{2,1,0:T(8,128)(2,1)S(1)}, bf16[1,512,512]{2,1,0:T(8,128)(2,1)}, u32[]{:S(2)}) copy-start(bf16[1,512,512]{2,1,0:T(8,128)(2,1)} %param.20) | copy-start | bytes 1572868
  14.0 20.8 %collective-permute-start = (bf16[352,512]{1,0:T(8,128)(2,1)S(1)}, bf16[352,512]{1,0:T(8,128)(2,1)S(1)}, u32[]{:S(2)}, u32[]{:S(2)}) collective-permute-start(bf16[352,512]{1,0:T(8,128)(2,1)S(1)} %slice_bitcast_fusion.1), channel_id=1, source_target_pairs={{0,4},{4,8},{8,12},{1,5},{5,9},{9,13},{2,6},{6,10},{10,14},{3,7},{... | collective-permute-start | bytes 1081352 | tf_op jit(solution)/shard_map/ppermute | solution.py:434
  34.8 5.1 %collective-permute-start.1 = (bf16[3,32,512]{2,1,0:T(8,128)(2,1)S(1)}, bf16[3,32,512]{2,1,0:T(8,128)(2,1)S(1)}, u32[]{:S(2)}, u32[]{:S(2)}) collective-permute-start(bf16[3,32,512]{2,1,0:T(8,128)(2,1)S(1)} %shard_map.132), channel_id=1, source_target_pairs={{0,4},{4,0},{8,12},{12,8},{1,5},{5,1},{9,13},{13,9},{2,6},{6,2},{1... | collective-permute-start | bytes 294920 | tf_op jit(solution)/shard_map/ppermute | solution.py:450
  39.9 7.6 %collective-permute-start.2 = (bf16[3,32,512]{2,1,0:T(8,128)(2,1)S(1)}, bf16[3,32,512]{2,1,0:T(8,128)(2,1)S(1)}, u32[]{:S(2)}, u32[]{:S(2)}) collective-permute-start(bf16[3,32,512]{2,1,0:T(8,128)(2,1)S(1)} %add_convert_fusion.1.refs_0_), channel_id=1, source_target_pairs={{0,12},{4,8},{8,4},{12,0},{1,13},{5,9},{9,5},{13,1},{2,14},{6,10},... | collective-permute-start | bytes 294920 | tf_op jit(solution)/shard_map/ppermute | solution.py:450
  48.8 25.6 %all-to-all-start.1 = ((bf16[16,3,32,512]{3,2,1,0:T(8,128)(2,1)}), bf16[16,3,32,512]{3,2,1,0:T(8,128)(2,1)}, u32[]{:S(2)}, u32[]{:S(2)}) async-start(bf16[16,3,32,512]{3,2,1,0:T(8,128)(2,1)} %shard_map.133), calls=%async_computation.1 | async-start | bytes 3145728 | tf_op jit(solution)/shard_map/all_to_all | solution.py:464
  56.0 11.3 %collective-permute-start.3 = (bf16[160,512]{1,0:T(8,128)(2,1)S(1)}, bf16[160,512]{1,0:T(8,128)(2,1)S(1)}, u32[]{:S(2)}, u32[]{:S(2)}) collective-permute-start(bf16[160,512]{1,0:T(8,128)(2,1)S(1)} %slice_bitcast_fusion.3), channel_id=1, source_target_pairs={{0,4},{4,8},{8,12},{1,5},{5,9},{9,13},{2,6},{6,10},{10,14},{3,7},{... | collective-permute-start | bytes 491528 | tf_op jit(solution)/shard_map/ppermute | solution.py:434
  61.0 8.6 %collective-permute-start.4 = (bf16[160,512]{1,0:T(8,128)(2,1)S(1)}, bf16[160,512]{1,0:T(8,128)(2,1)S(1)}, u32[]{:S(2)}, u32[]{:S(2)}) collective-permute-start(bf16[160,512]{1,0:T(8,128)(2,1)S(1)} %slice_bitcast_fusion.2), channel_id=1, source_target_pairs={{0,4},{4,8},{8,12},{1,5},{5,9},{9,13},{2,6},{6,10},{10,14},{3,7},{... | collective-permute-start | bytes 491528 | tf_op jit(solution)/shard_map/ppermute | solution.py:434
  67.3 17.9 %copy-start.6 = (bf16[160,512]{1,0:T(8,128)(2,1)}, bf16[160,512]{1,0:T(8,128)(2,1)S(1)}, u32[]{:S(2)}) copy-start(bf16[160,512]{1,0:T(8,128)(2,1)S(1)} %collective-permute-done.3.keys_b_ref) | copy-start | bytes 491524
  69.6 15.6 %copy-start.8 = (bf16[160,512]{1,0:T(8,128)(2,1)}, bf16[160,512]{1,0:T(8,128)(2,1)S(1)}, u32[]{:S(2)}) copy-start(bf16[160,512]{1,0:T(8,128)(2,1)S(1)} %collective-permute-done.4.values_b_ref) | copy-start | bytes 491524
  85.3 27.2 %all-to-all-start.2 = ((bf16[16,3,32,512]{3,2,1,0:T(8,128)(2,1)}), bf16[16,3,32,512]{3,2,1,0:T(8,128)(2,1)S(1)}, u32[]{:S(2)}, u32[]{:S(2)}) async-start(bf16[16,3,32,512]{3,2,1,0:T(8,128)(2,1)} %get-tuple-element.28), calls=%async_computation.2 | async-start | bytes 3145728 | tf_op jit(solution)/shard_map/all_to_all | solution.py:438
  92.1 23.6 %copy-start.3 = (s32[16]{0:T(128)S(1)}, s32[16]{0:T(128)}, u32[]{:S(2)}) copy-start(s32[16]{0:T(128)} %length_ref.3) | copy-start | bytes 196
  92.1 23.6 %copy-start.5 = (bf16[1,512,512]{2,1,0:T(8,128)(2,1)S(1)}, bf16[1,512,512]{2,1,0:T(8,128)(2,1)}, u32[]{:S(2)}) copy-start(bf16[1,512,512]{2,1,0:T(8,128)(2,1)} %param.18) | copy-start | bytes 1572868
  92.2 20.5 %collective-permute-start.5 = (bf16[352,512]{1,0:T(8,128)(2,1)}, bf16[352,512]{1,0:T(8,128)(2,1)}, u32[]{:S(2)}, u32[]{:S(2)}) collective-permute-start(bf16[352,512]{1,0:T(8,128)(2,1)} %slice_bitcast_fusion), channel_id=1, source_target_pairs={{0,4},{4,8},{8,12},{1,5},{5,9},{9,13},{2,6},{6,10},{10,14},{3,7},{... | collective-permute-start | bytes 1081352 | tf_op jit(solution)/shard_map/ppermute | solution.py:434
  112.4 3.3 %copy-start.7 = (bf16[160,512]{1,0:T(8,128)(2,1)S(1)}, bf16[160,512]{1,0:T(8,128)(2,1)}, u32[]{:S(2)}) copy-start(bf16[160,512]{1,0:T(8,128)(2,1)} %copy-done.6) | copy-start | bytes 491524
  112.4 3.3 %copy-start.9 = (bf16[160,512]{1,0:T(8,128)(2,1)S(1)}, bf16[160,512]{1,0:T(8,128)(2,1)}, u32[]{:S(2)}) copy-start(bf16[160,512]{1,0:T(8,128)(2,1)} %copy-done.8) | copy-start | bytes 491524
  112.7 7.4 %collective-permute-start.6 = (bf16[3,32,512]{2,1,0:T(8,128)(2,1)S(1)}, bf16[3,32,512]{2,1,0:T(8,128)(2,1)S(1)}, u32[]{:S(2)}, u32[]{:S(2)}) collective-permute-start(bf16[3,32,512]{2,1,0:T(8,128)(2,1)S(1)} %shard_map.135), channel_id=1, source_target_pairs={{0,4},{4,0},{8,12},{12,8},{1,5},{5,1},{9,13},{13,9},{2,6},{6,2},{1... | collective-permute-start | bytes 294920 | tf_op jit(solution)/shard_map/ppermute | solution.py:450
  120.1 5.7 %collective-permute-start.7 = (bf16[3,32,512]{2,1,0:T(8,128)(2,1)S(1)}, bf16[3,32,512]{2,1,0:T(8,128)(2,1)S(1)}, u32[]{:S(2)}, u32[]{:S(2)}) collective-permute-start(bf16[3,32,512]{2,1,0:T(8,128)(2,1)S(1)} %add_convert_fusion.refs_0_), channel_id=1, source_target_pairs={{0,12},{4,8},{8,4},{12,0},{1,13},{5,9},{9,5},{13,1},{2,14},{6,10},... | collective-permute-start | bytes 294920 | tf_op jit(solution)/shard_map/ppermute | solution.py:450
  125.9 22.9 %copy-start.4 = (bf16[3,1,512,512]{3,2,1,0:T(8,128)(2,1)S(1)}, bf16[3,1,512,512]{3,2,1,0:T(8,128)(2,1)}, u32[]{:S(2)}) copy-start(bf16[3,1,512,512]{3,2,1,0:T(8,128)(2,1)} %param.16) | copy-start | bytes 4718596
  125.9 22.9 %copy-start.10 = (s32[16]{0:T(128)S(1)}, s32[16]{0:T(128)}, u32[]{:S(2)}) copy-start(s32[16]{0:T(128)} %fork_ref.1) | copy-start | bytes 196
  125.9 22.8 %copy-start.11 = (bf16[3,512,512]{2,1,0:T(8,128)(2,1)S(1)}, bf16[3,512,512]{2,1,0:T(8,128)(2,1)}, u32[]{:S(2)}) copy-start(bf16[3,512,512]{2,1,0:T(8,128)(2,1)} %get-tuple-element.38.state_hbm) | copy-start | bytes 4718596
  148.7 20.2 %copy-start.2 = (f32[1,512]{1,0:T(1,128)S(1)}, f32[1,512]{1,0:T(1,128)}, u32[]{:S(2)}) copy-start(f32[1,512]{1,0:T(1,128)} %gain_ref.1) | copy-start | bytes 6148

commit v10 on v9

--- a/solution.py
+++ b/solution.py
@@ -452,10 +452,10 @@
 
 def sum_depth(mine, beside=None):
     planes = lax.axis_size(PLANE)
-    other, beside = lax.optimization_barrier((swap_depth(mine, 1), beside))
+    other, beside = lax.optimization_barrier((swap_depth(mine, 3), beside))
     pair = (mine.astype(jnp.float32) + other.astype(jnp.float32)).astype(jnp.bfloat16)
     (copies,) = call(
-        replicate_kernel, (), (pair, swap_depth(pair, 3)), (shape((planes, *mine.shape), mine.dtype),)
+        replicate_kernel, (), (pair, swap_depth(pair, 1)), (shape((planes, *mine.shape), mine.dtype),)
     )
     return copies, beside
 

time: 171 us -> 170 us (level)
  starting transfers between devices: 57.2 us -> 47.5 us
  waiting for transfers between devices: 43.8 us -> 51.5 us
    ppermute x4, starting transfers between devices: 14.6 us -> 8.93 us  [swap_depth(): return lax.ppermute(value, 'z', [(i, i ^ flip) for i in range(depth)])]
    ppermute x4, starting transfers between devices: 21.6 us -> 17 us  [from_behind(): lax.ppermute(value, 'z', [(source, source + 1) for source in range(count...]
    ppermute x4, waiting for transfers between devices: 6.86 us -> 10.1 us  [swap_depth(): return lax.ppermute(value, 'z', [(i, i ^ flip) for i in range(depth)])]
    all_to_all x2, waiting for transfers between devices: 29.8 us -> 31.8 us  [sum_plane_in_kernel(): received = lax.all_to_all(parts, PLANE, 0, 0, tiled=False)]
    all_to_all x1, waiting for transfers between devices: 4.83 us -> 6.79 us  [spread_plane(): return lax.all_to_all(copies, PLANE, 0, 0, tiled=False)]
  transfers between devices with their start and end apart: 11 -> 11, of which waited for: 7 -> 8; matrix products, arithmetic and copies ran while one was open for 0% -> 0% of each run, Pallas kernels for 3% -> 3%
where the time goes in v10:
time: 170 us; the launch traced here: 169 us
  waiting for transfers between devices  51.5 us (30%)
  starting transfers between devices  47.5 us (28%)
  blocking collectives  34.2 us (20%)
  Pallas kernels  32.2 us (19%)
  between operations  2.18 us (1%)
    pallas_call x9, Pallas kernels, call(): pl.pallas_call(kernel, out_shape=(*outs, *held_outs), in_specs=[SMEM] * l...  32.2 us
    all_to_all x2, waiting for transfers between devices, sum_plane_in_kernel(): received = lax.all_to_all(parts, PLANE, 0, 0, tiled=False)  31.8 us
    all_to_all x1, blocking collectives, spread_plane(): return lax.all_to_all(copies, PLANE, 0, 0, tiled=False)  23.3 us
    ppermute x4, starting transfers between devices, from_behind(): lax.ppermute(value, 'z', [(source, source + 1) for source in range(count...  17 us
    all_to_all x2, starting transfers between devices, sum_plane_in_kernel(): received = lax.all_to_all(parts, PLANE, 0, 0, tiled=False)  14.6 us
    psum x1, blocking collectives, per_device(): energy = lax.psum(energy, HEAD)  10.9 us
    ppermute x4, waiting for transfers between devices, swap_depth(): return lax.ppermute(value, 'z', [(i, i ^ flip) for i in range(depth)])  10.1 us
    ppermute x4, starting transfers between devices, swap_depth(): return lax.ppermute(value, 'z', [(i, i ^ flip) for i in range(depth)])  8.93 us
  transfers between devices with their start and end apart: 11, of which 8 were waited for; matrix products, arithmetic and copies ran while one was open for 0% of the time, Pallas kernels for 3%

profile of v10, /device:TPU:1, one launch (start us, length us, event | category | flops | bytes accessed | tf_op | source)
XLA Modules:
  0.0 169.2 jit_solution(11170999884542566446)
XLA Ops:
  1.3 4.9 %shard_map.131 = bf16[16,3,32,512]{3,2,1,0:T(8,128)(2,1)} custom-call(s32[1]{0:T(128)S(6)} %copy.15.split_ref, f32[1,512]{1,0:T(1,128)} %rates_hbm.3, bf16[3,512,512]{2,1,0:T(8,128)(2,1)} %bitcast.20, bf16[512,512]{1,0:T(8,128)(2,1)} %bitcast.26, bf16[512,512]{1,0:T(8,128)(2,1)} %bitcast.28), custom_call_target="tpu_custom_call" | custom-call | flops 1610612736 | bytes 4196352 | tf_op jit(solution)/shard_map/pallas_call | solution.py:331
  6.2 7.7 %all-to-all-start = ((bf16[16,3,32,512]{3,2,1,0:T(8,128)(2,1)}), bf16[16,3,32,512]{3,2,1,0:T(8,128)(2,1)S(1)}, u32[]{:S(2)}, u32[]{:S(2)}) async-start(bf16[16,3,32,512]{3,2,1,0:T(8,128)(2,1)} %shard_map.131), calls=%async_computation | async-start | bytes 3145728 | tf_op jit(solution)/shard_map/all_to_all | solution.py:438
  14.0 5.0 %collective-permute-start = (bf16[352,512]{1,0:T(8,128)(2,1)S(1)}, bf16[352,512]{1,0:T(8,128)(2,1)S(1)}, u32[]{:S(2)}, u32[]{:S(2)}) collective-permute-start(bf16[352,512]{1,0:T(8,128)(2,1)S(1)} %slice_bitcast_fusion.1), channel_id=1, source_target_pairs={{0,4},{4,8},{8,12},{1,5},{5,9},{9,13},{2,6},{6,10},{10,14},{3,7},{... | collective-permute-start | bytes 1081352 | tf_op jit(solution)/shard_map/ppermute | solution.py:434
  19.0 15.5 %all-to-all-done.received_ref = bf16[16,3,32,512]{3,2,1,0:T(8,128)(2,1)S(1)} async-done(((bf16[16,3,32,512]{3,2,1,0:T(8,128)(2,1)}), bf16[16,3,32,512]{3,2,1,0:T(8,128)(2,1)S(1)}, u32[]{:S(2)}, u32[]{:S(2)}) %all-to-all-start) | async-done | bytes 1572896 | tf_op jit(solution)/shard_map/all_to_all | solution.py:438
  34.5 0.2 shard_map.132
  34.8 6.1 %collective-permute-start.1 = (bf16[3,32,512]{2,1,0:T(8,128)(2,1)S(1)}, bf16[3,32,512]{2,1,0:T(8,128)(2,1)S(1)}, u32[]{:S(2)}, u32[]{:S(2)}) collective-permute-start(bf16[3,32,512]{2,1,0:T(8,128)(2,1)S(1)} %shard_map.132), channel_id=1, source_target_pairs={{0,12},{4,8},{8,4},{12,0},{1,13},{5,9},{9,5},{13,1},{2,14},{6,10},... | collective-permute-start | bytes 294920 | tf_op jit(solution)/shard_map/ppermute | solution.py:450
  40.9 2.6 %collective-permute-done.1 = bf16[3,32,512]{2,1,0:T(8,128)(2,1)S(1)} collective-permute-done((bf16[3,32,512]{2,1,0:T(8,128)(2,1)S(1)}, bf16[3,32,512]{2,1,0:T(8,128)(2,1)S(1)}, u32[]{:S(2)}, u32[]{:S(2)}) %collective-permute-start.1) | collective-permute-done | bytes 98336 | tf_op jit(solution)/shard_map/ppermute | solution.py:450
  43.5 1.7 collective-permute-start.2
  45.2 2.8 %collective-permute-done.2.refs_1_ = bf16[3,32,512]{2,1,0:T(8,128)(2,1)S(1)} collective-permute-done((bf16[3,32,512]{2,1,0:T(8,128)(2,1)S(1)}, bf16[3,32,512]{2,1,0:T(8,128)(2,1)S(1)}, u32[]{:S(2)}, u32[]{:S(2)}) %collective-permute-start.2) | collective-permute-done | bytes 98336 | tf_op jit(solution)/shard_map/ppermute | solution.py:450
  48.0 1.3 shard_map.133
  49.4 7.0 %all-to-all-start.1 = ((bf16[16,3,32,512]{3,2,1,0:T(8,128)(2,1)}), bf16[16,3,32,512]{3,2,1,0:T(8,128)(2,1)}, u32[]{:S(2)}, u32[]{:S(2)}) async-start(bf16[16,3,32,512]{3,2,1,0:T(8,128)(2,1)} %shard_map.133), calls=%async_computation.1 | async-start | bytes 3145728 | tf_op jit(solution)/shard_map/all_to_all | solution.py:464
  57.0 4.0 %collective-permute-start.3 = (bf16[160,512]{1,0:T(8,128)(2,1)S(1)}, bf16[160,512]{1,0:T(8,128)(2,1)S(1)}, u32[]{:S(2)}, u32[]{:S(2)}) collective-permute-start(bf16[160,512]{1,0:T(8,128)(2,1)S(1)} %slice_bitcast_fusion.3), channel_id=1, source_target_pairs={{0,4},{4,8},{8,12},{1,5},{5,9},{9,13},{2,6},{6,10},{10,14},{3,7},{... | collective-permute-start | bytes 491528 | tf_op jit(solution)/shard_map/ppermute | solution.py:434
  61.1 4.1 %collective-permute-start.4 = (bf16[160,512]{1,0:T(8,128)(2,1)S(1)}, bf16[160,512]{1,0:T(8,128)(2,1)S(1)}, u32[]{:S(2)}, u32[]{:S(2)}) collective-permute-start(bf16[160,512]{1,0:T(8,128)(2,1)S(1)} %slice_bitcast_fusion.2), channel_id=1, source_target_pairs={{0,4},{4,8},{8,12},{1,5},{5,9},{9,13},{2,6},{6,10},{10,14},{3,7},{... | collective-permute-start | bytes 491528 | tf_op jit(solution)/shard_map/ppermute | solution.py:434
  65.2 0.8 slice_bitcast_fusion
  66.0 2.7 %collective-permute-done.4.values_b_ref = bf16[160,512]{1,0:T(8,128)(2,1)S(1)} collective-permute-done((bf16[160,512]{1,0:T(8,128)(2,1)S(1)}, bf16[160,512]{1,0:T(8,128)(2,1)S(1)}, u32[]{:S(2)}, u32[]{:S(2)}) %collective-permute-start.4) | collective-permute-done | bytes 163872 | tf_op jit(solution)/shard_map/ppermute | solution.py:434
  68.7 6.8 %all-to-all-done.1.gathered_hbm = bf16[16,3,32,512]{3,2,1,0:T(8,128)(2,1)} async-done(((bf16[16,3,32,512]{3,2,1,0:T(8,128)(2,1)}), bf16[16,3,32,512]{3,2,1,0:T(8,128)(2,1)}, u32[]{:S(2)}, u32[]{:S(2)}) %all-to-all-start.1) | async-done | bytes 1572896 | tf_op jit(solution)/shard_map/all_to_all | solution.py:464
  75.5 10.8 %shard_map.134 = (bf16[16,3,32,512]{3,2,1,0:T(8,128)(2,1)}, bf16[3,512,512]{2,1,0:T(8,128)(2,1)}) custom-call(s32[1]{0:T(128)S(6)} %copy.15.split_ref, f32[1]{0:T(128)S(6)} %copy.16.step_ref, f32[1,512]{1,0:T(1,128)} %rates_hbm.3, bf16[16,3,32,512]{3,2,1,0:T(8,128)(2,1)} %all-to-all-done.1.gathered_hbm, bf16[3,512,512]{2,1,0:T(8,128)(2,1)} %bitcast.21, ...), custom_call_target="tpu_custom_call" | custom-call | flops 6442450944 | bytes 7342080 | tf_op jit(solution)/shard_map/pallas_call | solution.py:331
  86.3 6.8 %all-to-all-start.2 = ((bf16[16,3,32,512]{3,2,1,0:T(8,128)(2,1)}), bf16[16,3,32,512]{3,2,1,0:T(8,128)(2,1)S(1)}, u32[]{:S(2)}, u32[]{:S(2)}) async-start(bf16[16,3,32,512]{3,2,1,0:T(8,128)(2,1)} %get-tuple-element.28), calls=%async_computation.2 | async-start | bytes 3145728 | tf_op jit(solution)/shard_map/all_to_all | solution.py:438
  93.2 3.8 %collective-permute-start.5 = (bf16[352,512]{1,0:T(8,128)(2,1)}, bf16[352,512]{1,0:T(8,128)(2,1)}, u32[]{:S(2)}, u32[]{:S(2)}) collective-permute-start(bf16[352,512]{1,0:T(8,128)(2,1)} %slice_bitcast_fusion), channel_id=1, source_target_pairs={{0,4},{4,8},{8,12},{1,5},{5,9},{9,13},{2,6},{6,10},{10,14},{3,7},{... | collective-permute-start | bytes 1081352 | tf_op jit(solution)/shard_map/ppermute | solution.py:434
  97.0 16.3 %all-to-all-done.2.received_ref = bf16[16,3,32,512]{3,2,1,0:T(8,128)(2,1)S(1)} async-done(((bf16[16,3,32,512]{3,2,1,0:T(8,128)(2,1)}), bf16[16,3,32,512]{3,2,1,0:T(8,128)(2,1)S(1)}, u32[]{:S(2)}, u32[]{:S(2)}) %all-to-all-start.2) | async-done | bytes 1572896 | tf_op jit(solution)/shard_map/all_to_all | solution.py:438
  113.4 0.2 shard_map.135
  113.6 0.1 collective-permute-start.6
  113.7 0.6 copy-done.7
  114.3 4.3 %shard_map.136.attended_ref = f32[512,512]{1,0:T(8,128)S(1)} custom-call(s32[16]{0:T(128)S(1)} %copy-done.3, bf16[512,512]{1,0:T(8,128)(2,1)S(1)} %bitcast.23, bf16[512,512]{1,0:T(8,128)(2,1)S(1)} %bitcast.18, bf16[512,512]{1,0:T(8,128)(2,1)S(1)} %bitcast.19, bf16[352,512]{1,0:T(8,128)(2,1)S(1)} %collective-permute-done.keys_a_ref, ...), custom_call_target="tpu_custom_call" | custom-call | flops 1073741824 | bytes 3670016 | tf_op jit(solution)/shard_map/pallas_call | solution.py:331
  118.6 0.6 collective-permute-done.6
  119.3 1.0 collective-permute-start.7
  120.3 4.1 %collective-permute-done.7.refs_1_ = bf16[3,32,512]{2,1,0:T(8,128)(2,1)S(1)} collective-permute-done((bf16[3,32,512]{2,1,0:T(8,128)(2,1)S(1)}, bf16[3,32,512]{2,1,0:T(8,128)(2,1)S(1)}, u32[]{:S(2)}, u32[]{:S(2)}) %collective-permute-start.7) | collective-permute-done | bytes 98336 | tf_op jit(solution)/shard_map/ppermute | solution.py:450
  124.4 0.1 shard_map.137
  124.6 23.3 %all_to_all.20.gathered_ref = bf16[16,3,32,512]{3,2,1,0:T(8,128)(2,1)S(1)} all-to-all(bf16[16,3,32,512]{3,2,1,0:T(8,128)(2,1)S(1)} %shard_map.137), channel_id=1, replica_groups=mesh['x'=4,'y'=4,'z'=4,'w'=2,'c'=2] {'x','y'}, dimensions={0} | all-to-all | bytes 3145728 | tf_op jit(solution)/shard_map/all_to_all | solution.py:464
  147.9 8.9 %shard_map.138 = (f32[512,512]{1,0:T(8,128)S(1)}, f32[1,512]{1,0:T(1,128)S(1)}, bf16[3,512,512]{2,1,0:T(8,128)(2,1)}) custom-call(s32[1]{0:T(128)S(6)} %copy.15.split_ref, s32[16]{0:T(128)S(1)} %copy-done.10, f32[1]{0:T(128)S(6)} %copy.16.step_ref, bf16[16,3,32,512]{3,2,1,0:T(8,128)(2,1)S(1)} %all_to_all.20.gathered_ref, ...), custom_call_target="tpu_custom_call" | custom-call | flops 5637144576 | bytes 8914944 | tf_op jit(solution)/shard_map/pallas_call | solution.py:331
  156.8 10.9 %psum.7.energy_ref = f32[1,512]{1,0:T(1,128)S(1)} all-reduce(f32[1,512]{1,0:T(1,128)S(1)} %get-tuple-element.40), channel_id=1, replica_groups=mesh['x'=4,'y'=4,'z'=4,'w'=2,'c'=2] {'w','c'}, use_global_device_ids=true, to_apply=%region_0.0 | all-reduce | flops 512 | bytes 4096 | tf_op jit(solution)/shard_map/psum | solution.py:516
  167.7 1.5 shard_map.139
  (31 shorter events, 0.2 us)
Async XLA Ops:
  6.2 7.8 %copy-start = (bf16[1,512,512]{2,1,0:T(8,128)(2,1)S(1)}, bf16[1,512,512]{2,1,0:T(8,128)(2,1)}, u32[]{:S(2)}) copy-start(bf16[1,512,512]{2,1,0:T(8,128)(2,1)} %param.19) | copy-start | bytes 1572868
  6.2 28.4 %all-to-all-start = ((bf16[16,3,32,512]{3,2,1,0:T(8,128)(2,1)}), bf16[16,3,32,512]{3,2,1,0:T(8,128)(2,1)S(1)}, u32[]{:S(2)}, u32[]{:S(2)}) async-start(bf16[16,3,32,512]{3,2,1,0:T(8,128)(2,1)} %shard_map.131), calls=%async_computation | async-start | bytes 3145728 | tf_op jit(solution)/shard_map/all_to_all | solution.py:438
  13.9 31.3 %copy-start.1 = (bf16[1,512,512]{2,1,0:T(8,128)(2,1)S(1)}, bf16[1,512,512]{2,1,0:T(8,128)(2,1)}, u32[]{:S(2)}) copy-start(bf16[1,512,512]{2,1,0:T(8,128)(2,1)} %param.20) | copy-start | bytes 1572868
  14.0 20.8 %collective-permute-start = (bf16[352,512]{1,0:T(8,128)(2,1)S(1)}, bf16[352,512]{1,0:T(8,128)(2,1)S(1)}, u32[]{:S(2)}, u32[]{:S(2)}) collective-permute-start(bf16[352,512]{1,0:T(8,128)(2,1)S(1)} %slice_bitcast_fusion.1), channel_id=1, source_target_pairs={{0,4},{4,8},{8,12},{1,5},{5,9},{9,13},{2,6},{6,10},{10,14},{3,7},{... | collective-permute-start | bytes 1081352 | tf_op jit(solution)/shard_map/ppermute | solution.py:434
  34.8 8.7 %collective-permute-start.1 = (bf16[3,32,512]{2,1,0:T(8,128)(2,1)S(1)}, bf16[3,32,512]{2,1,0:T(8,128)(2,1)S(1)}, u32[]{:S(2)}, u32[]{:S(2)}) collective-permute-start(bf16[3,32,512]{2,1,0:T(8,128)(2,1)S(1)} %shard_map.132), channel_id=1, source_target_pairs={{0,12},{4,8},{8,4},{12,0},{1,13},{5,9},{9,5},{13,1},{2,14},{6,10},... | collective-permute-start | bytes 294920 | tf_op jit(solution)/shard_map/ppermute | solution.py:450
  43.5 4.5 %collective-permute-start.2 = (bf16[3,32,512]{2,1,0:T(8,128)(2,1)S(1)}, bf16[3,32,512]{2,1,0:T(8,128)(2,1)S(1)}, u32[]{:S(2)}, u32[]{:S(2)}) collective-permute-start(bf16[3,32,512]{2,1,0:T(8,128)(2,1)S(1)} %add_convert_fusion.1.refs_0_), channel_id=1, source_target_pairs={{0,4},{4,0},{8,12},{12,8},{1,5},{5,1},{9,13},{13,9},{2,6},{6,2},{1... | collective-permute-start | bytes 294920 | tf_op jit(solution)/shard_map/ppermute | solution.py:450
  49.4 26.2 %all-to-all-start.1 = ((bf16[16,3,32,512]{3,2,1,0:T(8,128)(2,1)}), bf16[16,3,32,512]{3,2,1,0:T(8,128)(2,1)}, u32[]{:S(2)}, u32[]{:S(2)}) async-start(bf16[16,3,32,512]{3,2,1,0:T(8,128)(2,1)} %shard_map.133), calls=%async_computation.1 | async-start | bytes 3145728 | tf_op jit(solution)/shard_map/all_to_all | solution.py:464
  57.0 8.9 %collective-permute-start.3 = (bf16[160,512]{1,0:T(8,128)(2,1)S(1)}, bf16[160,512]{1,0:T(8,128)(2,1)S(1)}, u32[]{:S(2)}, u32[]{:S(2)}) collective-permute-start(bf16[160,512]{1,0:T(8,128)(2,1)S(1)} %slice_bitcast_fusion.3), channel_id=1, source_target_pairs={{0,4},{4,8},{8,12},{1,5},{5,9},{9,13},{2,6},{6,10},{10,14},{3,7},{... | collective-permute-start | bytes 491528 | tf_op jit(solution)/shard_map/ppermute | solution.py:434
  61.1 7.7 %collective-permute-start.4 = (bf16[160,512]{1,0:T(8,128)(2,1)S(1)}, bf16[160,512]{1,0:T(8,128)(2,1)S(1)}, u32[]{:S(2)}, u32[]{:S(2)}) collective-permute-start(bf16[160,512]{1,0:T(8,128)(2,1)S(1)} %slice_bitcast_fusion.2), channel_id=1, source_target_pairs={{0,4},{4,8},{8,12},{1,5},{5,9},{9,13},{2,6},{6,10},{10,14},{3,7},{... | collective-permute-start | bytes 491528 | tf_op jit(solution)/shard_map/ppermute | solution.py:434
  66.0 20.3 %copy-start.6 = (bf16[160,512]{1,0:T(8,128)(2,1)}, bf16[160,512]{1,0:T(8,128)(2,1)S(1)}, u32[]{:S(2)}) copy-start(bf16[160,512]{1,0:T(8,128)(2,1)S(1)} %collective-permute-done.3.keys_b_ref) | copy-start | bytes 491524
  68.7 17.6 %copy-start.8 = (bf16[160,512]{1,0:T(8,128)(2,1)}, bf16[160,512]{1,0:T(8,128)(2,1)S(1)}, u32[]{:S(2)}) copy-start(bf16[160,512]{1,0:T(8,128)(2,1)S(1)} %collective-permute-done.4.values_b_ref) | copy-start | bytes 491524
  86.3 27.0 %all-to-all-start.2 = ((bf16[16,3,32,512]{3,2,1,0:T(8,128)(2,1)}), bf16[16,3,32,512]{3,2,1,0:T(8,128)(2,1)S(1)}, u32[]{:S(2)}, u32[]{:S(2)}) async-start(bf16[16,3,32,512]{3,2,1,0:T(8,128)(2,1)} %get-tuple-element.28), calls=%async_computation.2 | async-start | bytes 3145728 | tf_op jit(solution)/shard_map/all_to_all | solution.py:438
  93.2 20.5 %copy-start.3 = (s32[16]{0:T(128)S(1)}, s32[16]{0:T(128)}, u32[]{:S(2)}) copy-start(s32[16]{0:T(128)} %length_ref.3) | copy-start | bytes 196
  93.2 20.5 %copy-start.5 = (bf16[1,512,512]{2,1,0:T(8,128)(2,1)S(1)}, bf16[1,512,512]{2,1,0:T(8,128)(2,1)}, u32[]{:S(2)}) copy-start(bf16[1,512,512]{2,1,0:T(8,128)(2,1)} %param.18) | copy-start | bytes 1572868
  93.2 20.4 %collective-permute-start.5 = (bf16[352,512]{1,0:T(8,128)(2,1)}, bf16[352,512]{1,0:T(8,128)(2,1)}, u32[]{:S(2)}, u32[]{:S(2)}) collective-permute-start(bf16[352,512]{1,0:T(8,128)(2,1)} %slice_bitcast_fusion), channel_id=1, source_target_pairs={{0,4},{4,8},{8,12},{1,5},{5,9},{9,13},{2,6},{6,10},{10,14},{3,7},{... | collective-permute-start | bytes 1081352 | tf_op jit(solution)/shard_map/ppermute | solution.py:434
  113.4 0.9 copy-start.7
  113.4 1.0 copy-start.9
  113.6 5.7 %collective-permute-start.6 = (bf16[3,32,512]{2,1,0:T(8,128)(2,1)S(1)}, bf16[3,32,512]{2,1,0:T(8,128)(2,1)S(1)}, u32[]{:S(2)}, u32[]{:S(2)}) collective-permute-start(bf16[3,32,512]{2,1,0:T(8,128)(2,1)S(1)} %shard_map.135), channel_id=1, source_target_pairs={{0,12},{4,8},{8,4},{12,0},{1,13},{5,9},{9,5},{13,1},{2,14},{6,10},... | collective-permute-start | bytes 294920 | tf_op jit(solution)/shard_map/ppermute | solution.py:450
  119.3 5.1 %collective-permute-start.7 = (bf16[3,32,512]{2,1,0:T(8,128)(2,1)S(1)}, bf16[3,32,512]{2,1,0:T(8,128)(2,1)S(1)}, u32[]{:S(2)}, u32[]{:S(2)}) collective-permute-start(bf16[3,32,512]{2,1,0:T(8,128)(2,1)S(1)} %add_convert_fusion.refs_0_), channel_id=1, source_target_pairs={{0,4},{4,0},{8,12},{12,8},{1,5},{5,1},{9,13},{13,9},{2,6},{6,2},{1... | collective-permute-start | bytes 294920 | tf_op jit(solution)/shard_map/ppermute | solution.py:450
  124.6 23.3 %copy-start.4 = (bf16[3,1,512,512]{3,2,1,0:T(8,128)(2,1)S(1)}, bf16[3,1,512,512]{3,2,1,0:T(8,128)(2,1)}, u32[]{:S(2)}) copy-start(bf16[3,1,512,512]{3,2,1,0:T(8,128)(2,1)} %param.16) | copy-start | bytes 4718596
  124.6 23.3 %copy-start.10 = (s32[16]{0:T(128)S(1)}, s32[16]{0:T(128)}, u32[]{:S(2)}) copy-start(s32[16]{0:T(128)} %fork_ref.1) | copy-start | bytes 196
  124.6 23.3 %copy-start.11 = (bf16[3,512,512]{2,1,0:T(8,128)(2,1)S(1)}, bf16[3,512,512]{2,1,0:T(8,128)(2,1)}, u32[]{:S(2)}) copy-start(bf16[3,512,512]{2,1,0:T(8,128)(2,1)} %get-tuple-element.38.state_hbm) | copy-start | bytes 4718596
  147.9 19.8 %copy-start.2 = (f32[1,512]{1,0:T(1,128)S(1)}, f32[1,512]{1,0:T(1,128)}, u32[]{:S(2)}) copy-start(f32[1,512]{1,0:T(1,128)} %gain_ref.1) | copy-start | bytes 6148
